TPU v7x, 32 devices: a whole 2x2x4 slice. The times are simulated.
32 devices in a mesh: dp: 8 (over z, x), expert: 4 (over y, core).
Axes of the slice: x: 2, y: 2, z: 4, core: 2. Of those that a mesh axis runs over, the one named last changes fastest.
Arguments:
- tokens: bfloat16 [4, 2048, 768], P('expert', 'dp'), may hold values from -6 to 6
- norm_attn: float32 [768], replicated, may hold values from 0.5 to 1.5
- query_key_value_weight: bfloat16 [768, 2304], replicated, may hold values from -0.21875 to 0.21875
- attention_output_weight: bfloat16 [768, 768], replicated, may hold values from -1.75 to 1.75
- norm_ffn: float32 [768], replicated, may hold values from 0.5 to 1.5
- router: bfloat16 [768, 8], replicated, may hold values from -0.15625 to 0.15625
- expert_in: bfloat16 [768, 8, 4096], P(None, 'expert'), may hold values from -0.21875 to 0.21875
- expert_out: bfloat16 [2048, 8, 768], P(None, 'expert'), may hold values from -0.125 to 0.125
- shared_gate_up_weight: bfloat16 [768, 4096], replicated, may hold values from -0.21875 to 0.21875
- shared_down_weight: bfloat16 [2048, 768], replicated, may hold values from -0.125 to 0.125
- block_lengths: int32 [4, 16], P('expert'), may hold values from 1 to 256, 2048 in all within a row
- routes: int32 [4, 2048, 2], P('expert', 'dp'), may hold values from 0 to 7, all different within a row
- cotangent: bfloat16 [4, 2048, 768], P('expert', 'dp'), may hold values from -6 to 6
Outputs:
- mixed: bfloat16 [4, 2048, 768], P('expert', 'dp')
- input_grad: float32 [4, 2048, 768], P('expert', 'dp')
- norm_attn_grad: float32 [768], P('dp')
- qkv_weight_grad: float32 [768, 2304], P('dp', 'expert')
- out_weight_grad: float32 [768, 768], P('dp', 'expert')
- norm_ffn_grad: float32 [768], P('dp')
- router_grad: float32 [768, 8], P('dp', 'expert')
- expert_in_grad: float32 [768, 8, 4096], P('dp', 'expert')
- expert_out_grad: float32 [2048, 8, 768], P('dp', 'expert')
- shared_in_grad: float32 [768, 4096], P('dp', 'expert')
- shared_out_grad: float32 [2048, 768], P('dp', 'expert')
Inputs may be any that keep to these rules, and one draw needn't show every extreme that they name: `block_lengths`: each sequence's 16 block lengths sum to 2048, and the longest is 256. `routes`: each token names 2 different experts.
All inputs are finite; a program needn't handle non-finite values.
Results may differ from a plain program's by a relative error of at most 0.028.
Values may be sent and summed in bfloat16 or wider, within the bound.
No kernel may reach another device: no remote copies, remote signals or barrier semaphores. Data moves between devices by JAX's collectives and lax.ppermute only.
A program may use at most 256 MiB of HBM per device.

v0:
```python
import jax
import jax.numpy as jnp
from jax import lax
from jax.sharding import PartitionSpec as P

HEADS = 12
HEAD_DIM = 64
TOP = 2


EPS = 1e-06
NEG = -1e30


def rope_table(positions):
    half_dim = HEAD_DIM // 2
    frequency = 10000.0 ** (-jnp.arange(half_dim, dtype=jnp.float32) * 2.0 / HEAD_DIM)
    angles = positions.astype(jnp.float32)[:, None] * frequency[None, :]
    return (jnp.cos(angles)[:, None, :], jnp.sin(angles)[:, None, :])


def rotate(values, cosine, sine_table, direction):
    half_dim = HEAD_DIM // 2
    first_half = values[..., :half_dim]
    second = values[..., half_dim:]
    return jnp.concatenate(
        [
            first_half * cosine - direction * second * sine_table,
            second * cosine + direction * first_half * sine_table,
        ],
        axis=-1,
    )


def block_ids(bounds, positions):
    return jnp.sum((bounds[None, :] <= positions[:, None]).astype(jnp.int32), axis=1)


def rms_scale(hidden):
    return lax.rsqrt(jnp.mean(hidden * hidden, axis=-1, keepdims=True) + EPS)


def rms_back(hidden, scale_rows, gain_vector, upstream):
    normed_grad = upstream * gain_vector
    inner_mean = jnp.mean(normed_grad * hidden, axis=-1, keepdims=True)
    return scale_rows * normed_grad - hidden * scale_rows**3 * inner_mean


def swiglu(pre_act, split_at):
    gate_half = pre_act[..., :split_at]
    return gate_half * jax.nn.sigmoid(gate_half) * pre_act[..., split_at:]


def silu_back(pre_act, upstream, split_at):
    gate_half = pre_act[..., :split_at]
    up_half = pre_act[..., split_at:]
    sigmoid_gate = jax.nn.sigmoid(gate_half)
    gate_slope = sigmoid_gate * (1.0 + gate_half * (1.0 - sigmoid_gate))
    return jnp.concatenate(
        [upstream * up_half * gate_slope, upstream * gate_half * sigmoid_gate], axis=-1
    )


def masked_scores(queries, key_heads, query_ids, key_ids):
    scores = jnp.einsum("qhd,khd->hqk", queries, key_heads, preferred_element_type=jnp.float32)
    visible = query_ids[:, None] >= key_ids[None, :]
    return (jnp.where(visible[None], scores, NEG), visible)


def score_grads(queries, grad_out, log_total, row_delta, key_heads, values, query_ids, key_ids):
    scores, visible = masked_scores(queries, key_heads, query_ids, key_ids)
    weights_full = jnp.where(visible[None], jnp.exp(scores - log_total.T[:, :, None]), 0.0)
    grad_weights = jnp.einsum("qhd,khd->hqk", grad_out, values, preferred_element_type=jnp.float32)
    grad_scores = (weights_full * (grad_weights - row_delta.T[:, :, None])).astype(jnp.bfloat16)
    return (weights_full.astype(jnp.bfloat16), grad_scores)


def local(
    tokens,
    norm_attn,
    query_key_value_weight,
    attention_output_weight,
    norm_ffn,
    router,
    expert_in,
    expert_out,
    shared_gate_up_weight,
    shared_down_weight,
    block_lengths,
    routes,
    cotangent,
):
    hidden = tokens[0].astype(jnp.float32)
    row_count = hidden.shape[0]
    model_width = hidden.shape[1]
    shard_index = lax.axis_index("dp")
    length = row_count * lax.axis_size("dp")
    positions = shard_index * row_count + jnp.arange(row_count, dtype=jnp.int32)
    bounds = jnp.cumsum(block_lengths[0])
    query_ids = block_ids(bounds, positions)
    key_ids = block_ids(bounds, jnp.arange(length, dtype=jnp.int32))
    cosine, sine_table = rope_table(positions)
    head_shape = (row_count, HEADS, HEAD_DIM)
    scale_one = rms_scale(hidden)
    normalized_rows = (hidden * scale_one * norm_attn).astype(jnp.bfloat16)
    projected_rows = jnp.dot(
        normalized_rows, query_key_value_weight, preferred_element_type=jnp.float32
    )
    queries = (
        rotate(projected_rows[:, :model_width].reshape(head_shape), cosine, sine_table, 1.0)
        * HEAD_DIM ** (-0.5)
    ).astype(jnp.bfloat16)
    key_heads = rotate(
        projected_rows[:, model_width : 2 * model_width].reshape(head_shape),
        cosine,
        sine_table,
        1.0,
    ).astype(jnp.bfloat16)
    values = projected_rows[:, 2 * model_width :].reshape(head_shape).astype(jnp.bfloat16)
    all_keys, all_values = (
        lax.all_gather(key_heads.reshape(row_count, model_width), "dp", axis=0, tiled=True),
        lax.all_gather(values.reshape(row_count, model_width), "dp", axis=0, tiled=True),
    )
    key_span = min(512, length)
    blocks = length // key_span
    key_blocks = all_keys.reshape(blocks, key_span, HEADS, HEAD_DIM)
    value_blocks = all_values.reshape(blocks, key_span, HEADS, HEAD_DIM)
    id_blocks = key_ids.reshape(blocks, key_span)

    def stat_step(running, inputs):
        largest, row_total = running
        key_block, id_block = inputs
        scores, visible = masked_scores(queries, key_block, query_ids, id_block)
        newest = jnp.maximum(largest, jnp.max(scores, axis=-1))
        row_total = row_total * jnp.exp(largest - newest) + jnp.sum(
            jnp.where(visible[None], jnp.exp(scores - newest[:, :, None]), 0.0), axis=-1
        )
        return ((newest, row_total), None)

    start_max = jnp.full((HEADS, row_count), NEG, jnp.float32)
    (largest, row_total), _ = lax.scan(
        stat_step, (start_max, jnp.zeros((HEADS, row_count), jnp.float32)), (key_blocks, id_blocks)
    )
    log_total = (largest + jnp.log(row_total)).T

    def out_step(running, inputs):
        key_block, value_block, id_block = inputs
        scores, visible = masked_scores(queries, key_block, query_ids, id_block)
        weights_low = jnp.where(
            visible[None], jnp.exp(scores - log_total.T[:, :, None]), 0.0
        ).astype(jnp.bfloat16)
        return (
            running
            + jnp.einsum(
                "hqk,khd->qhd", weights_low, value_block, preferred_element_type=jnp.float32
            ),
            None,
        )

    attention_result, _ = lax.scan(
        out_step, jnp.zeros(head_shape, jnp.float32), (key_blocks, value_blocks, id_blocks)
    )
    attended_low = attention_result.reshape(row_count, model_width).astype(jnp.bfloat16)
    residual_between = hidden + jnp.dot(
        attended_low, attention_output_weight, preferred_element_type=jnp.float32
    )
    scale_two = rms_scale(residual_between)
    combined_input = (residual_between * scale_two * norm_ffn).astype(jnp.bfloat16)
    experts_total = router.shape[1]
    local_experts = expert_in.shape[1]
    expert_ff = expert_out.shape[0]
    shared_ff = shared_down_weight.shape[0]
    groups = lax.axis_size("expert")
    capacity = row_count * TOP * 5 // (4 * experts_total)
    router_scores = jnp.dot(combined_input, router, preferred_element_type=jnp.float32)
    chosen = routes[0]
    pick_hot = (
        chosen[:, :, None] == jnp.arange(experts_total, dtype=jnp.int32)[None, None, :]
    ).astype(jnp.float32)
    picked = jnp.sum(pick_hot * router_scores[:, None, :], axis=-1)
    gate_weights = jax.nn.softmax(picked, axis=-1)
    column = jnp.arange(experts_total, dtype=jnp.int32)
    column_expert = column % groups * local_experts + column // groups
    flat_routes = chosen.reshape(row_count * TOP)
    route_hot = (flat_routes[:, None] == column_expert[None, :]).astype(jnp.int32)
    earlier = jnp.cumsum(route_hot, axis=0) - route_hot
    slot_index = jnp.sum(earlier * route_hot, axis=1)
    kept_rows = slot_index < capacity
    target = jnp.sum(route_hot * column[None, :], axis=1) * capacity + slot_index
    dispatch = (
        (target[:, None] == jnp.arange(experts_total * capacity, dtype=jnp.int32)[None, :])
        & kept_rows[:, None]
    ).astype(jnp.bfloat16)
    repeated = jnp.repeat(combined_input, TOP, axis=0)
    send_rows = jnp.einsum(
        "rc,rd->cd", dispatch, repeated, preferred_element_type=jnp.float32
    ).astype(jnp.bfloat16)
    arrived = lax.all_to_all(
        send_rows.reshape(local_experts, groups, capacity, model_width),
        "expert",
        split_axis=1,
        concat_axis=1,
        tiled=True,
    )
    expert_rows = arrived.reshape(local_experts, groups * capacity, model_width)
    gate_up = jnp.einsum("erd,def->erf", expert_rows, expert_in, preferred_element_type=jnp.float32)
    activated = swiglu(gate_up, expert_ff).astype(jnp.bfloat16)
    expert_result = jnp.einsum(
        "erf,fed->erd", activated, expert_out, preferred_element_type=jnp.float32
    ).astype(jnp.bfloat16)
    returned = lax.all_to_all(
        expert_result.reshape(local_experts, groups, capacity, model_width),
        "expert",
        split_axis=1,
        concat_axis=1,
        tiled=True,
    )
    back_rows = jnp.einsum(
        "rc,cd->rd",
        dispatch,
        returned.reshape(experts_total * capacity, model_width),
        preferred_element_type=jnp.float32,
    ).reshape(row_count, TOP, model_width)
    routed = jnp.sum(gate_weights[:, :, None] * back_rows, axis=1)
    shared_preactivation = jnp.dot(
        combined_input, shared_gate_up_weight, preferred_element_type=jnp.float32
    )
    shared_activation = swiglu(shared_preactivation, shared_ff).astype(jnp.bfloat16)
    shared_feedforward_output = jnp.dot(
        shared_activation, shared_down_weight, preferred_element_type=jnp.float32
    )
    output = (residual_between + routed + shared_feedforward_output).astype(jnp.bfloat16)[None]
    upstream = cotangent[0]
    grad_upper = upstream.astype(jnp.float32)
    grad_shared_out = jnp.einsum(
        "tf,td->fd", shared_activation, upstream, preferred_element_type=jnp.float32
    )
    grad_shared_act = jnp.einsum(
        "td,fd->tf", upstream, shared_down_weight, preferred_element_type=jnp.float32
    )
    grad_shared_pre = silu_back(shared_preactivation, grad_shared_act, shared_ff).astype(
        jnp.bfloat16
    )
    grad_shared_in = jnp.einsum(
        "td,tf->df", combined_input, grad_shared_pre, preferred_element_type=jnp.float32
    )
    grad_mixed = jnp.einsum(
        "tf,df->td", grad_shared_pre, shared_gate_up_weight, preferred_element_type=jnp.float32
    )
    grad_gates = jnp.sum(back_rows * grad_upper[:, None, :], axis=-1)
    grad_picked = gate_weights * (
        grad_gates - jnp.sum(gate_weights * grad_gates, axis=-1, keepdims=True)
    )
    grad_logits = jnp.sum(pick_hot * grad_picked[:, :, None], axis=1).astype(jnp.bfloat16)
    grad_router = jnp.einsum(
        "td,te->de", combined_input, grad_logits, preferred_element_type=jnp.float32
    )
    grad_mixed = grad_mixed + jnp.einsum(
        "te,de->td", grad_logits, router, preferred_element_type=jnp.float32
    )
    grad_rows = (
        (gate_weights[:, :, None] * grad_upper[:, None, :])
        .reshape(row_count * TOP, model_width)
        .astype(jnp.bfloat16)
    )
    grad_send = jnp.einsum(
        "rc,rd->cd", dispatch, grad_rows, preferred_element_type=jnp.float32
    ).astype(jnp.bfloat16)
    grad_arrived = lax.all_to_all(
        grad_send.reshape(local_experts, groups, capacity, model_width),
        "expert",
        split_axis=1,
        concat_axis=1,
        tiled=True,
    )
    grad_arrived = grad_arrived.reshape(local_experts, groups * capacity, model_width)
    grad_expert_out = jnp.einsum(
        "erf,erd->fed", activated, grad_arrived, preferred_element_type=jnp.float32
    )
    grad_activated = jnp.einsum(
        "erd,fed->erf", grad_arrived, expert_out, preferred_element_type=jnp.float32
    )
    grad_gate_up = silu_back(gate_up, grad_activated, expert_ff).astype(jnp.bfloat16)
    grad_expert_in = jnp.einsum(
        "erd,erf->def", expert_rows, grad_gate_up, preferred_element_type=jnp.float32
    )
    grad_expert_rows = jnp.einsum(
        "erf,def->erd", grad_gate_up, expert_in, preferred_element_type=jnp.float32
    ).astype(jnp.bfloat16)
    grad_returned = lax.all_to_all(
        grad_expert_rows.reshape(local_experts, groups, capacity, model_width),
        "expert",
        split_axis=1,
        concat_axis=1,
        tiled=True,
    )
    grad_token_rows = jnp.einsum(
        "rc,cd->rd",
        dispatch,
        grad_returned.reshape(experts_total * capacity, model_width),
        preferred_element_type=jnp.float32,
    )
    grad_mixed = grad_mixed + jnp.sum(grad_token_rows.reshape(row_count, TOP, model_width), axis=1)
    grad_norm_ffn = jnp.sum(grad_mixed * residual_between * scale_two, axis=0)
    grad_middle = grad_upper + rms_back(residual_between, scale_two, norm_ffn, grad_mixed)
    grad_attn_low = grad_middle.astype(jnp.bfloat16)
    grad_out_weight = jnp.einsum(
        "td,te->de", attended_low, grad_attn_low, preferred_element_type=jnp.float32
    )
    grad_attended = (
        jnp.einsum(
            "te,de->td", grad_attn_low, attention_output_weight, preferred_element_type=jnp.float32
        )
        .astype(jnp.bfloat16)
        .reshape(head_shape)
    )
    row_delta = jnp.sum(grad_attended.astype(jnp.float32) * attention_result, axis=-1)

    def back_step(grad_queries, inputs):
        key_block, value_block, id_block = inputs
        weights_low, grad_scores = score_grads(
            queries,
            grad_attended,
            log_total,
            row_delta,
            key_block,
            value_block,
            query_ids,
            id_block,
        )
        grad_queries = grad_queries + jnp.einsum(
            "hqk,khd->qhd", grad_scores, key_block, preferred_element_type=jnp.float32
        )
        grad_key_part = jnp.einsum(
            "hqk,qhd->khd", grad_scores, queries, preferred_element_type=jnp.float32
        ).reshape(key_span, model_width)
        grad_value_part = jnp.einsum(
            "hqk,qhd->khd", weights_low, grad_attended, preferred_element_type=jnp.float32
        ).reshape(key_span, model_width)
        return (grad_queries, jnp.concatenate([grad_key_part, grad_value_part], axis=1))

    grad_queries, key_terms = lax.scan(
        back_step, jnp.zeros(head_shape, jnp.float32), (key_blocks, value_blocks, id_blocks)
    )
    own_terms = lax.psum_scatter(
        key_terms.reshape(length, 2 * model_width).astype(jnp.bfloat16),
        "dp",
        scatter_dimension=0,
        tiled=True,
    ).astype(jnp.float32)
    grad_keys = own_terms[:, :model_width].reshape(head_shape)
    grad_values = own_terms[:, model_width:].reshape(head_shape)
    grad_queries = rotate(grad_queries * HEAD_DIM ** (-0.5), cosine, sine_table, -1.0)
    grad_keys = rotate(grad_keys, cosine, sine_table, -1.0)
    grad_projected = jnp.concatenate(
        [
            grad_queries.reshape(row_count, model_width),
            grad_keys.reshape(row_count, model_width),
            grad_values.reshape(row_count, model_width),
        ],
        axis=1,
    ).astype(jnp.bfloat16)
    grad_qkv = jnp.einsum(
        "td,te->de", normalized_rows, grad_projected, preferred_element_type=jnp.float32
    )
    grad_normed = jnp.einsum(
        "te,de->td", grad_projected, query_key_value_weight, preferred_element_type=jnp.float32
    )
    grad_norm_attn = jnp.sum(grad_normed * hidden * scale_one, axis=0)
    grad_input = grad_middle + rms_back(hidden, scale_one, norm_attn, grad_normed)
    (
        part_norm_attn,
        part_qkv,
        part_out,
        part_norm_ffn,
        part_router,
        part_shared_in,
        part_shared_out,
        part_expert_in,
        part_expert_out,
    ) = (
        lax.psum_scatter(
            grad_norm_attn.astype(jnp.bfloat16), "dp", scatter_dimension=0, tiled=True
        ).astype(jnp.float32),
        lax.psum_scatter(
            grad_qkv.astype(jnp.bfloat16), "dp", scatter_dimension=0, tiled=True
        ).astype(jnp.float32),
        lax.psum_scatter(
            grad_out_weight.astype(jnp.bfloat16), "dp", scatter_dimension=0, tiled=True
        ).astype(jnp.float32),
        lax.psum_scatter(
            grad_norm_ffn.astype(jnp.bfloat16), "dp", scatter_dimension=0, tiled=True
        ).astype(jnp.float32),
        lax.psum_scatter(
            grad_router.astype(jnp.bfloat16), "dp", scatter_dimension=0, tiled=True
        ).astype(jnp.float32),
        lax.psum_scatter(
            grad_shared_in.astype(jnp.bfloat16), "dp", scatter_dimension=0, tiled=True
        ).astype(jnp.float32),
        lax.psum_scatter(
            grad_shared_out.astype(jnp.bfloat16), "dp", scatter_dimension=0, tiled=True
        ).astype(jnp.float32),
        lax.psum_scatter(
            grad_expert_in.astype(jnp.bfloat16), "dp", scatter_dimension=0, tiled=True
        ).astype(jnp.float32),
        lax.psum_scatter(
            grad_expert_out.astype(jnp.bfloat16), "dp", scatter_dimension=0, tiled=True
        ).astype(jnp.float32),
    )
    sum_qkv, sum_out, sum_router, sum_shared_in, sum_shared_out = (
        lax.psum_scatter(
            part_qkv.astype(jnp.bfloat16), "expert", scatter_dimension=1, tiled=True
        ).astype(jnp.float32),
        lax.psum_scatter(
            part_out.astype(jnp.bfloat16), "expert", scatter_dimension=1, tiled=True
        ).astype(jnp.float32),
        lax.psum_scatter(
            part_router.astype(jnp.bfloat16), "expert", scatter_dimension=1, tiled=True
        ).astype(jnp.float32),
        lax.psum_scatter(
            part_shared_in.astype(jnp.bfloat16), "expert", scatter_dimension=1, tiled=True
        ).astype(jnp.float32),
        lax.psum_scatter(
            part_shared_out.astype(jnp.bfloat16), "expert", scatter_dimension=1, tiled=True
        ).astype(jnp.float32),
    )
    sum_norm_attn, sum_norm_ffn = lax.psum((part_norm_attn, part_norm_ffn), "expert")
    return (
        output,
        grad_input[None],
        sum_norm_attn,
        sum_qkv,
        sum_out,
        sum_norm_ffn,
        sum_router,
        part_expert_in,
        part_expert_out,
        sum_shared_in,
        sum_shared_out,
    )


def solution(mesh):
    placed = (
        P("expert", "dp", None),
        P(),
        P(),
        P(),
        P(),
        P(),
        P(None, "expert", None),
        P(None, "expert", None),
        P(),
        P(),
        P("expert", None),
        P("expert", "dp", None),
        P("expert", "dp", None),
    )
    return jax.shard_map(
        local,
        mesh=mesh,
        in_specs=placed,
        out_specs=(
            P("expert", "dp", None),
            P("expert", "dp", None),
            P("dp"),
            P("dp", "expert"),
            P("dp", "expert"),
            P("dp"),
            P("dp", "expert"),
            P("dp", "expert", None),
            P("dp", "expert", None),
            P("dp", "expert"),
            P("dp", "expert"),
        ),
        check_vma=False,
    )
```

profile of v0, /device:TPU:0, one launch (start us, length us, event | category | flops | bytes accessed | tf_op | source)
XLA Modules:
  0.0 1531.4 jit_solution(14965068707000031921)
XLA Ops:
  64.6 12.3 all-gather.3.cloned.1.call-done
  76.9 4.6 copy.127
  81.6 6.2 reshape.519
  92.0 48.7 %all-gather.5.cloned.1.call-done = bf16[2048,768]{0,1:T(8,128)(2,1)} async-done(((bf16[256,768]{0,1:T(8,128)(2,1)}), bf16[2048,768]{0,1:T(8,128)(2,1)}) %all-gather.5.cloned.1.call-update) | async-done | bytes 3145744 | tf_op jit(solution)/shard_map/all_gather | solution.py:121
  140.7 6.1 reshape.524
  151.2 50.4 %while.37 = (s32[]{:T(128)}, f32[12,256]{1,0:T(8,128)S(1)}, f32[12,256]{1,0:T(8,128)}, s32[256]{0:T(256)}, s32[4,512]{1,0:T(4,128)}, /*index=5*/bf16[4,512,12,64...) while((s32[]{:T(128)}, f32[12,256]{1,0:T(8,128)S(1)}, f32[12,256]{1,0:T(8,128)}, ...), condition=%wide.region_7.8_spmd.clone, body=%wide.region_4.7_spmd.clone.sunk | while | flops 210910208 | bytes 14945484 | solution.py:141
  152.7 5.6 fusion.192
  165.3 5.6 fusion.192
  177.9 5.6 fusion.192
  190.5 5.6 fusion.192
  202.9 27.6 %while.38 = (s32[]{:T(128)}, f32[256,12,64]{0,2,1:T(8,128)}, bf16[4,512,12,64]{1,3,2,0:T(8,128)(2,1)}, s32[256]{0:T(256)}, s32[4,512]{1,0:T(4,128)}, /*index=5*/...) while((s32[]{:T(128)}, f32[256,12,64]{0,2,1:T(8,128)}, ...), condition=%wide.region_9.10_spmd.clone, body=%wide.region_8.9_spmd.clone.sunk | while | flops 409468928 | bytes 3826298 | solution.py:160
  211.7 4.7 fusion.198
  218.5 4.7 fusion.198
  225.4 4.7 fusion.198
  235.2 6.8 fusion.130
  264.5 5.3 multiply_convert_fusion.4
  278.3 24.0 %fusion.57 = f32[2,320,4096]{2,1,0:T(8,128)} fusion(bf16[2,320,768]{2,1,0:T(8,128)(2,1)S(1)} %bitcast.249, bf16[768,2,4096]{2,1,0:T(2,128)(2,1)} %param.25), kind=kOutput, calls=%fused_computation.64 | convolution fusion | flops 4026531840 | bytes 24051712 | tf_op jit(solution)/shard_map/erd,def->erf/dot_general | solution.py:206
  303.6 12.1 multiply_convert_fusion.1
  315.7 6.0 fusion.63
  322.8 4.6 all-to-all-start.1
  327.4 23.0 %fusion.66 = bf16[2,320,768]{2,1,0:T(8,128)(2,1)} fusion(bf16[768,2,4096]{2,1,0:T(2,128)(2,1)} %param.25, bf16[2,320,2048]{2,1,0:T(8,128)(2,1)} %get-tuple-element.449, bf16[2,320,2048]{2,1,0:T(8,128)(2,1)} %get-tuple-element.448), kind=kOutput, calls=%fused_computation.98 | convolution fusion | flops 4037509120 | bytes 18808832 | tf_op jit(solution)/shard_map/erf,def->erd/dot_general | solution.py:287
  357.0 6.2 fusion.69
  388.5 100.1 %while.39 = (s32[]{:T(128)}, f32[256,12,64]{0,2,1:T(8,128)}, bf16[4,512,1536]{2,1,0:T(8,128)(2,1)}, bf16[4,512,12,64]{1,3,2,0:T(8,128)(2,1)}, s32[256]{0:T(256)S...) while((s32[]{:T(128)}, f32[256,12,64]{0,2,1:T(8,128)}, ...), condition=%wide.region_26.27_spmd.clone, body=%wide.region_25.26_spmd.clone.sunk | while | flops 1026031616 | bytes 88927680 | solution.py:342
  392.0 5.5 fusion.210
  401.2 4.6 fusion.212
  416.7 5.5 fusion.210
  426.1 4.5 fusion.212
  441.6 5.5 fusion.210
  451.2 4.5 fusion.212
  466.7 5.5 fusion.210
  476.2 4.7 fusion.212
  488.7 6.2 convolution_convert_fusion
  499.4 16.5 %reduce-scatter.32.cloned.1.call-done = bf16[256,768]{1,0:T(8,128)(2,1)} async-done(((bf16[2048,768]{1,0:T(8,128)(2,1)}), bf16[256,768]{1,0:T(8,128)(2,1)}) %reduce-scatter.32.cloned.1.call-update) | async-done | bytes 393232 | tf_op jit(solution)/shard_map/reduce_scatter | solution.py:400
  517.9 8.2 convert_bitcast_fusion.1
  526.2 11.9 convert_bitcast_fusion
  538.1 31.7 %copy.159 = bf16[768,2,4096]{2,1,0:T(2,128)(2,1)} copy(bf16[768,2,4096]{0,2,1:T(8,128)(2,1)} %convert_bitcast_fusion) | data formatting | bytes 25165824 | tf_op jit(solution)/shard_map/convert_element_type | solution.py:404
  571.9 64.4 %reduce-scatter.20.cloned.1.call-done = bf16[256,1536]{1,0:T(8,128)(2,1)} async-done(((bf16[2048,1536]{1,0:T(8,128)(2,1)}), bf16[256,1536]{1,0:T(8,128)(2,1)}) %reduce-scatter.20.cloned.1.call-update) | async-done | bytes 786448 | tf_op jit(solution)/shard_map/reduce_scatter | solution.py:345
  651.7 105.2 %reduce-scatter.28.cloned.1.call-done = bf16[96,4096]{1,0:T(8,128)(2,1)} async-done(((bf16[768,4096]{1,0:T(8,128)(2,1)}), bf16[96,4096]{1,0:T(8,128)(2,1)}) %reduce-scatter.28.cloned.1.call-update) | async-done | bytes 786448 | tf_op jit(solution)/shard_map/reduce_scatter | solution.py:397
  763.8 57.2 %reduce-scatter.38.cloned.1.call-done = bf16[96,8]{1,0:T(8,128)(2,1)} async-done(((bf16[768,8]{1,0:T(8,128)(2,1)}), bf16[96,8]{1,0:T(8,128)(2,1)}) %reduce-scatter.38.cloned.1.call-update) | async-done | bytes 1552
  821.8 5.7 all-reduce.2
  828.1 14.8 reduce-scatter.36.cloned.1.call-done
  845.8 20.4 %reduce-scatter.40.cloned.1.call-done = bf16[192,256]{1,0:T(8,128)(2,1)} async-done(((bf16[768,256]{1,0:T(8,128)(2,1)}), bf16[192,256]{1,0:T(8,128)(2,1)}) %reduce-scatter.40.cloned.1.call-update) | async-done | bytes 98320
  869.5 118.5 %reduce-scatter.26.cloned.1.call-done = bf16[256,2,768]{0,2,1:T(8,128)(2,1)} async-done(((bf16[2048,2,768]{0,2,1:T(8,128)(2,1)}), bf16[256,2,768]{0,2,1:T(8,128)(2,1)}) %reduce-scatter.26.cloned.1.call-update) | async-done | bytes 786448 | tf_op jit(solution)/shard_map/reduce_scatter | solution.py:406
  991.2 397.8 %all-reduce.8.cloned.1.call-done = bf16[768,2,4096]{2,1,0:T(2,128)(2,1)} async-done(((bf16[768,2,4096]{2,1,0:T(2,128)(2,1)}), bf16[768,2,4096]{2,1,0:T(2,128)(2,1)}) %all-reduce.8.cloned.1.call-update) | async-done | bytes 12582928
  1393.4 77.7 %reduce-scatter.22.cloned.1.call-done = bf16[96,2304]{1,0:T(8,128)(2,1)} async-done(((bf16[768,2304]{1,0:T(8,128)(2,1)}), bf16[96,2304]{1,0:T(8,128)(2,1)}) %reduce-scatter.22.cloned.1.call-update) | async-done | bytes 442384 | tf_op jit(solution)/shard_map/reduce_scatter | solution.py:385
  1477.2 20.7 %all-reduce.5 = (bf16[768]{0:T(1024)(128)(2,1)}, bf16[768]{0:T(1024)(128)(2,1)}) all-reduce(bf16[768]{0:T(1024)(128)(2,1)} %get-tuple-element.386, bf16[768]{0:T(1024)(128)(2,1)S(1)} %copy-done.48), channel_id=3, replica_groups=mesh['dp'=8,'expert'=4] {'dp'}, use_global_device_ids=true, to_apply=%region_30.31.clone | all-reduce | flops 1536 | bytes 6144
  1499.9 6.3 all-reduce.4
  1511.2 10.0 reduce-scatter.34.cloned.1.call-done
  (411 shorter events, 298.2 us)
Async XLA Ops:
  7.2 69.7 %all-gather.3.cloned.1.call-start = ((), (), s32[]{:S(2)}) async-start(), calls=%async_computation.15 | async-start | bytes 3538944 | tf_op jit(solution)/shard_map/all_gather | solution.py:122
  13.7 127.0 %all-gather.5.cloned.1.call-start = ((), (), s32[]{:S(2)}) async-start(), calls=%async_computation.16 | async-start | bytes 3538944 | tf_op jit(solution)/shard_map/all_gather | solution.py:121
  152.7 5.6 copy-start.4
  165.3 5.6 copy-start.4
  177.9 5.6 copy-start.4
  190.5 5.6 copy-start.4
  235.2 6.8 copy-start.5
  235.2 6.8 copy-start.28
  235.2 7.0 copy-start.34
  253.6 18.1 %all-to-all-start = ((bf16[2,4,80,768]{3,2,0,1:T(8,128)(2,1)}), bf16[2,4,80,768]{3,2,0,1:T(8,128)(2,1)}, u32[]{:S(2)}, u32[]{:S(2)}) async-start(bf16[2,4,80,768]{3,2,0,1:T(8,128)(2,1)} %copy.138), calls=%async_computation | async-start | bytes 1966080 | tf_op jit(solution)/shard_map/all_to_all | solution.py:198
  271.7 30.6 %all-to-all-start.2 = ((bf16[2,4,80,768]{3,2,0,1:T(8,128)(2,1)}), bf16[2,4,80,768]{3,2,0,1:T(8,128)(2,1)}, u32[]{:S(2)}, u32[]{:S(2)}) async-start(bf16[2,4,80,768]{3,2,0,1:T(8,128)(2,1)} %copy.146), calls=%async_computation.2 | async-start | bytes 1966080 | tf_op jit(solution)/shard_map/all_to_all | solution.py:269
  303.6 12.2 copy-start.22
  315.7 6.0 copy-start.57
  322.8 29.9 %all-to-all-start.1 = ((bf16[2,4,80,768]{3,2,0,1:T(8,128)(2,1)}), bf16[2,4,80,768]{3,2,0,1:T(8,128)(2,1)}, u32[]{:S(2)}, u32[]{:S(2)}) async-start(bf16[2,4,80,768]{3,2,0,1:T(8,128)(2,1)} %copy.142), calls=%async_computation.1 | async-start | bytes 1966080 | tf_op jit(solution)/shard_map/all_to_all | solution.py:211
  352.6 18.1 %all-to-all-start.3 = ((bf16[2,4,80,768]{3,2,0,1:T(8,128)(2,1)}), bf16[2,4,80,768]{3,2,0,1:T(8,128)(2,1)}, u32[]{:S(2)}, u32[]{:S(2)}) async-start(bf16[2,4,80,768]{3,2,0,1:T(8,128)(2,1)} %copy.150), calls=%async_computation.3 | async-start | bytes 1966080 | tf_op jit(solution)/shard_map/all_to_all | solution.py:290
  356.9 140.8 %reduce-scatter.24.cloned.1.call-start = ((), (), s32[]{:S(2)}) async-start(), calls=%async_computation.19 | async-start | bytes 1327104 | tf_op jit(solution)/shard_map/reduce_scatter | solution.py:388
  356.9 7.5 copy-start.19
  356.9 7.5 copy-start.47
  356.9 7.5 copy-start.52
  357.0 7.5 copy-start.54
  377.7 138.2 %reduce-scatter.32.cloned.1.call-start = ((), (), s32[]{:S(2)}) async-start(), calls=%async_computation.23 | async-start | bytes 3538944 | tf_op jit(solution)/shard_map/reduce_scatter | solution.py:400
  381.8 6.7 copy-start.27
  381.8 254.6 %reduce-scatter.20.cloned.1.call-start = ((), (), s32[]{:S(2)}) async-start(), calls=%async_computation.17 | async-start | bytes 7077888 | tf_op jit(solution)/shard_map/reduce_scatter | solution.py:345
  391.0 6.5 copy-start.2
  391.9 5.5 copy-start.16
  401.2 4.6 copy-start.1
  415.7 6.5 copy-start.2
  416.6 5.6 copy-start.16
  440.6 6.5 copy-start.2
  441.5 5.5 copy-start.16
  465.8 6.5 copy-start.2
  466.7 5.6 copy-start.16
  476.2 4.7 copy-start.1
  476.2 4.7 copy-start.3
  488.6 268.3 %reduce-scatter.28.cloned.1.call-start = ((), (), s32[]{:S(2)}) async-start(), calls=%async_computation.21 | async-start | bytes 7077888 | tf_op jit(solution)/shard_map/reduce_scatter | solution.py:397
  494.9 326.1 %reduce-scatter.38.cloned.1.call-start = ((), (), s32[]{:S(2)}) async-start(), calls=%async_computation.26 | async-start | bytes 221184
  497.6 345.2 %reduce-scatter.36.cloned.1.call-start = ((), (), s32[]{:S(2)}) async-start(), calls=%async_computation.25 | async-start | bytes 245760
  499.4 366.8 %reduce-scatter.40.cloned.1.call-start = ((), (), s32[]{:S(2)}) async-start(), calls=%async_computation.27 | async-start | bytes 491520
  517.9 470.1 %reduce-scatter.26.cloned.1.call-start = ((), (), s32[]{:S(2)}) async-start(), calls=%async_computation.20 | async-start | bytes 7077888 | tf_op jit(solution)/shard_map/reduce_scatter | solution.py:406
  526.2 862.8 %all-reduce.8.cloned.1.call-start = ((), (), s32[]{:S(2)}) async-start(), calls=%async_computation.28 | async-start | bytes 25165824
  569.8 901.3 %reduce-scatter.22.cloned.1.call-start = ((), (), s32[]{:S(2)}) async-start(), calls=%async_computation.18 | async-start | bytes 3981312 | tf_op jit(solution)/shard_map/reduce_scatter | solution.py:385
  640.8 6.5 copy-start.38
  640.8 6.5 copy-start.46
  651.7 105.3 %copy-start.56 = (u32[32]{0:T(128)S(1)}, u32[32]{0:T(128)}, u32[]{:S(2)}) copy-start(u32[32]{0:T(128)} %constant.134) | copy-start | bytes 388
  651.7 105.9 %copy-start.55 = (u32[32]{0:T(128)S(1)}, u32[32]{0:T(128)}, u32[]{:S(2)}) copy-start(u32[32]{0:T(128)} %constant.142) | copy-start | bytes 388
  651.7 857.8 %reduce-scatter.30.cloned.1.call-start = ((), (), s32[]{:S(2)}) async-start(), calls=%async_computation.22 | async-start | bytes 983040 | tf_op jit(solution)/shard_map/reduce_scatter | solution.py:420
  756.9 764.2 %reduce-scatter.34.cloned.1.call-start = ((), (), s32[]{:S(2)}) async-start(), calls=%async_computation.24 | async-start | bytes 737280
  1473.2 33.6 %copy-start.50 = (f32[256]{0:T(256)S(1)}, f32[256]{0:T(256)}, u32[]{:S(2)}) copy-start(f32[256]{0:T(256)} %get-tuple-element.473) | copy-start | bytes 3076
  (67 other events, 196.2 us)
Sparse Core Ops, SparseCore 0:
  13.8 63.0 all-gather.2
  79.0 61.6 all-gather.4
  377.8 61.2 reduce-scatter.23
  442.5 73.3 reduce-scatter.31
  519.3 116.9 reduce-scatter.19
  639.8 117.0 reduce-scatter.27
  760.7 60.2 reduce-scatter.37
  824.0 18.7 reduce-scatter.35
  845.3 20.7 reduce-scatter.39
  869.6 118.3 reduce-scatter.25
  992.1 396.7 all-reduce.7
  1392.9 78.2 reduce-scatter.21
  1473.8 22.8 reduce-scatter.29
  1499.1 22.0 reduce-scatter.33
where the time goes:
time: 1550 us; the launch traced here: 1530 us
  waiting for transfers between devices  950 us (61%)
  matrix products  256 us (17%)
  local copies, waits for them, and re-layouts  171 us (11%)
  other arithmetic  86.8 us (6%)
  blocking collectives  32.6 us (2%)
  starting transfers between devices  18.1 us (1%)
  between operations  16.3 us (1%)
    unnamed x19, waiting for transfers between devices  500 us
    reduce_scatter x1, waiting for transfers between devices, local(): lax.psum_scatter(grad_expert_out.astype(jnp.bfloat16), 'dp', scatter_dime...  118 us
    reduce_scatter x1, waiting for transfers between devices, local(): lax.psum_scatter(grad_shared_in.astype(jnp.bfloat16), 'dp', scatter_dimen...  105 us
    reduce_scatter x1, waiting for transfers between devices, local(): lax.psum_scatter(grad_qkv.astype(jnp.bfloat16), 'dp', scatter_dimension=0...  77.7 us
    reduce_scatter x1, waiting for transfers between devices, local(): lax.psum_scatter(key_terms.reshape(length, 2 * model_width).astype(jnp.bf...  64.4 us
    all_gather x1, waiting for transfers between devices, local(): lax.all_gather(key_heads.reshape(row_count, model_width), 'dp', axis=0, t...  48.7 us
    unnamed x105, local copies, waits for them, and re-layouts  35.6 us
    dot_general x8, matrix products, masked_scores(): jnp.einsum('qhd,khd->hqk', queries, key_heads, preferred_element_type=jnp...  31.7 us
  transfers between devices with their start and end apart: 18, of which 14 were waited for; matrix products, arithmetic and copies ran while one was open for 24% of the time, Pallas kernels for 0%

commit v1 on v0

v1 whole, which is shorter than its diff:
```python
import functools

import jax
import jax.numpy as jnp
from jax import lax
from jax.experimental import pallas as pl
from jax.experimental.pallas import tpu as pltpu
from jax.sharding import Mesh
from jax.sharding import PartitionSpec as P

HEADS = 12
HEAD_DIM = 64
TOP = 2
EPS = 1e-06
NEG = -1e30
F32 = jnp.float32
BF16 = jnp.bfloat16
STEPS = 8
DP = ("g", "r")
EX = ("y", "c")


def rope_table(positions):
    half_dim = HEAD_DIM // 2
    frequency = 10000.0 ** (-jnp.arange(half_dim, dtype=F32) * 2.0 / HEAD_DIM)
    angles = positions.astype(F32)[:, None] * frequency[None, :]
    return (jnp.cos(angles)[:, None, :], jnp.sin(angles)[:, None, :])


def rotate(values, cosine, sine_table, direction):
    half_dim = HEAD_DIM // 2
    first_half = values[..., :half_dim]
    second = values[..., half_dim:]
    return jnp.concatenate(
        [
            first_half * cosine - direction * second * sine_table,
            second * cosine + direction * first_half * sine_table,
        ],
        axis=-1,
    )


def block_ids(bounds, positions):
    return jnp.sum((bounds[None, :] <= positions[:, None]).astype(jnp.int32), axis=1)


def rms_scale(hidden):
    return lax.rsqrt(jnp.mean(hidden * hidden, axis=-1, keepdims=True) + EPS)


def rms_back(hidden, scale_rows, gain_vector, upstream):
    normed_grad = upstream * gain_vector
    inner_mean = jnp.mean(normed_grad * hidden, axis=-1, keepdims=True)
    return scale_rows * normed_grad - hidden * scale_rows**3 * inner_mean


def masked_scores(queries, key_heads, query_ids, key_ids):
    scores = jnp.einsum("qhd,khd->hqk", queries, key_heads, preferred_element_type=F32)
    visible = query_ids[:, None] >= key_ids[None, :]
    return (jnp.where(visible[None], scores, NEG), visible)


def score_grads(queries, grad_out, log_total, row_delta, key_heads, values, query_ids, key_ids):
    scores, visible = masked_scores(queries, key_heads, query_ids, key_ids)
    weights_full = jnp.where(visible[None], jnp.exp(scores - log_total.T[:, :, None]), 0.0)
    grad_weights = jnp.einsum("qhd,khd->hqk", grad_out, values, preferred_element_type=F32)
    grad_scores = (weights_full * (grad_weights - row_delta.T[:, :, None])).astype(BF16)
    return (weights_full.astype(BF16), grad_scores)


class Place:
    def __init__(self):
        self.groups, self.lanes = lax.axis_size("g"), lax.axis_size("r")
        self.rows_y = lax.axis_size("y")
        self.dp = self.groups * self.lanes
        self.experts = self.rows_y * 2
        self.g, self.r = lax.axis_index("g"), lax.axis_index("r")
        self.y, self.c = lax.axis_index("y"), lax.axis_index("c")
        self.low, self.high = self.g % 2, self.g // 2

    def own(self, b):
        g, r = b // self.lanes, b % self.lanes
        low, high = g % 2, g // 2
        if self.lanes == 2:
            return r ^ self.r, low * 2 + high
        return low ^ self.low, high * self.lanes + r

    def flat(self, b):
        g, r = b // self.lanes, b % self.lanes
        if self.lanes == 2:
            return r * 4 + (g % 2) * 2 + g // 2
        return (g % 2 * 2 + g // 2) * self.lanes + r

    def expert_table(self, width):
        sub = STEPS // 4
        order = []
        for pos in range(STEPS):
            half, rest = pos // 4, pos % 4
            if self.lanes == 2:
                low, high, part = rest // 2, rest % 2, half ^ self.r
            else:
                low, high, part = half ^ self.low, rest // 2, rest % 2
            order.append((high * 2 + low) * sub + part)
        block = width // self.dp
        rows = []
        for b in range(self.dp):
            half, rest = self.own(b)
            rows.append(half * (width // 2) + rest * block)
        return jnp.stack([jnp.asarray(v, jnp.int32) for v in order + [0] * STEPS + rows])

    def shared_table(self, width):
        per = 16 // self.experts
        order, columns = [], []
        sub = STEPS // 4
        for pos in range(STEPS):
            half, rest = pos // 4, pos % 4
            j = (rest // per * 2 + (half ^ self.c)) * per + rest % per
            order.append(j)
            g, part = j // sub, j % sub
            if self.lanes == 2:
                columns.append(part * 4 + g % 2 * 2 + g // 2)
            else:
                columns.append((g % 2 * 2 + g // 2) * sub + part)
        block = width // self.dp
        rows = [self.flat(b) * block for b in range(self.dp)]
        own = width // self.experts
        turned = [
            (e % 2 ^ self.c) * (width // 2) + e // 2 * own for e in range(self.experts)
        ]
        return jnp.stack(
            [jnp.asarray(v, jnp.int32) for v in order + columns + rows + turned]
        )


def nt(a, b):
    return lax.dot_general(a, b, (((1,), (1,)), ((), ())), preferred_element_type=F32)


def nn(a, b):
    return lax.dot_general(a, b, (((1,), (0,)), ((), ())), preferred_element_type=F32)


def ffn_kernel(shared, dp, experts, table, x_ref, dy_ref, gate_ref, up_ref, down_ref, *refs):
    if shared:
        result, back, in_keep, in_send, out_keep, out_send, stage, turned, turned_dy = refs
    else:
        both, in_keep, in_send, out_keep, out_send, stage, turned, result, back = refs
    step = pl.program_id(0)
    width = x_ref.shape[1]
    rows = x_ref.shape[0]

    @pl.when(step == 0)
    def _():
        whole = x_ref[...].astype(F32).T
        block = width // dp
        for b in range(dp):
            start = pl.multiple_of(table[2 * STEPS + b], 8)
            stage[pl.ds(start, block), :] = whole[b * block : (b + 1) * block]
        turned[...] = stage[...].astype(BF16)
        if shared:
            whole = dy_ref[...].astype(F32).T
            block = width // experts
            for e in range(experts):
                start = pl.multiple_of(table[2 * STEPS + dp + e], 8)
                stage[pl.ds(start, block), :] = whole[e * block : (e + 1) * block]
            turned_dy[...] = stage[...].astype(BF16)
        result[...] = jnp.zeros_like(result)
        back[...] = jnp.zeros_like(back)

    x, dy = x_ref[...], dy_ref[...]
    w_gate, w_up, w_down = gate_ref[0], up_ref[0], down_ref[0]
    gate, up = nn(x, w_gate), nn(x, w_up)
    grad = nt(dy, w_down)
    sig = jax.nn.sigmoid(gate)
    silu = gate * sig
    act = (silu * up).astype(BF16)
    grad_gate = (grad * up * (sig * (1.0 + gate * (1.0 - sig)))).astype(BF16)
    grad_up = (grad * silu).astype(BF16)
    result[...] += nn(act, w_down)
    back[...] += nt(grad_gate, w_gate) + nt(grad_up, w_up)
    xt = turned[...]
    half = width // 2
    for k, upper in enumerate((grad_gate, grad_up)):
        grad_in = nn(xt, upper).astype(BF16)
        if shared:

            @pl.when(step < STEPS // 2)
            def _():
                in_keep[k] = grad_in

            @pl.when(step >= STEPS // 2)
            def _():
                in_send[k] = grad_in

        else:
            in_keep[k] = grad_in[:half]
            in_send[k] = grad_in[half:]
    if shared:
        grad_out = nn(turned_dy[...], act).astype(BF16)
        out_keep[...] = grad_out[:half]
        out_send[...] = grad_out[half:]
    else:
        grad_out = lax.dot_general(
            act, dy, (((0,), (0,)), ((), ())), preferred_element_type=F32
        ).astype(BF16)

        @pl.when(step < STEPS // 2)
        def _():
            out_keep[...] = grad_out

        @pl.when(step >= STEPS // 2)
        def _():
            out_send[...] = grad_out

        @pl.when(step == STEPS - 1)
        def _():
            both[:, :width] = result[...].astype(BF16)
            both[:, width:] = back[...].astype(BF16)


def ffn(shared, place, table, x, dy, w_in, w_out, e):
    rows, width = x.shape
    hidden = w_out.shape[1]
    chunk = hidden // STEPS
    near, far = STEPS // 2 - 1, STEPS // 2
    sds = jax.ShapeDtypeStruct
    first = lambda i, t: (0, 0, jnp.minimum(i, near))
    second = lambda i, t: (0, 0, jnp.maximum(i - far, 0))
    if shared:
        out_shape = (
            sds((rows, width), F32),
            sds((rows, width), F32),
            sds((2, width, hidden // 2), BF16),
            sds((2, width, hidden // 2), BF16),
            sds((width // 2, hidden), BF16),
            sds((width // 2, hidden), BF16),
        )
        out_specs = (
            pl.BlockSpec((rows, width), lambda i, t: (0, 0)),
            pl.BlockSpec((rows, width), lambda i, t: (0, 0)),
            pl.BlockSpec((2, width, chunk), first),
            pl.BlockSpec((2, width, chunk), second),
            pl.BlockSpec((width // 2, chunk), lambda i, t: (0, t[STEPS + i])),
            pl.BlockSpec((width // 2, chunk), lambda i, t: (0, t[STEPS + i])),
        )
        extra = [pltpu.VMEM((width, rows), BF16)]
    else:
        out_shape = (
            sds((rows, 2 * width), BF16),
            sds((2, width // 2, hidden), BF16),
            sds((2, width // 2, hidden), BF16),
            sds((hidden // 2, width), BF16),
            sds((hidden // 2, width), BF16),
        )
        out_specs = (
            pl.BlockSpec((rows, 2 * width), lambda i, t: (0, 0)),
            pl.BlockSpec((2, width // 2, chunk), lambda i, t: (0, 0, t[i])),
            pl.BlockSpec((2, width // 2, chunk), lambda i, t: (0, 0, t[i])),
            pl.BlockSpec((chunk, width), lambda i, t: (jnp.minimum(i, near), 0)),
            pl.BlockSpec((chunk, width), lambda i, t: (jnp.maximum(i - far, 0), 0)),
        )
        extra = [pltpu.VMEM((rows, width), F32), pltpu.VMEM((rows, width), F32)]
    return pl.pallas_call(
        functools.partial(ffn_kernel, shared, place.dp, place.experts),
        out_shape=out_shape,
        grid_spec=pltpu.PrefetchScalarGridSpec(
            num_scalar_prefetch=1,
            grid=(STEPS,),
            in_specs=[
                pl.BlockSpec((rows, width), lambda i, t: (0, 0)),
                pl.BlockSpec((rows, width), lambda i, t: (0, 0)),
                pl.BlockSpec((1, width, chunk), lambda i, t: (e, 0, t[i])),
                pl.BlockSpec((1, width, chunk), lambda i, t: (e, 0, STEPS + t[i])),
                pl.BlockSpec((1, chunk, width), lambda i, t: (e, t[i], 0)),
            ],
            out_specs=out_specs,
            scratch_shapes=[pltpu.VMEM((width, rows), F32), pltpu.VMEM((width, rows), BF16)]
            + extra,
        ),
        compiler_params=pltpu.CompilerParams(vmem_limit_bytes=48 * 1024 * 1024),
        cost_estimate=pl.CostEstimate(
            flops=2 * 9 * rows * width * hidden,
            bytes_accessed=12 * width * hidden,
            transcendentals=rows * hidden,
        ),
    )(table, x, dy, w_in, w_in, w_out)


def swap(a, axis, bit=1):
    size = lax.axis_size(axis)
    return lax.ppermute(a, axis, [(i, i ^ bit) for i in range(size)])


def add(a, b, kind=BF16):
    return (a.astype(F32) + b.astype(F32)).astype(kind)


def half_of(a, dim, index):
    size = a.shape[dim] // 2
    return lax.dynamic_slice_in_dim(a, index * size, size, dim)


def exchange(keep, came, dim, mine):
    return [add(half_of(keep, dim, i), half_of(came, dim, i)) for i in (mine, 1 - mine)]


def scatter(a, axis, dim):
    return lax.psum_scatter(a, axis, scatter_dimension=dim, tiled=True)


def reduce_experts(place, keep, send, dim):
    if place.lanes == 2:
        came = swap(send, "r")
        keep, send = exchange(keep, came, dim, place.low)
        came = swap(send, "g", 1)
        keep, send = exchange(keep, came, dim, place.high)
        return add(keep, swap(send, "g", 2), F32)
    came = swap(send, "g", 1)
    keep, send = exchange(keep, came, dim, place.high)
    return scatter(add(keep, swap(send, "g", 2)), "r", dim).astype(F32)


def reduce_tokens(place, keep, came, dim):
    if place.lanes == 2:
        keep, send = exchange(keep, came, dim, place.r)
        came = swap(send, "r")
    keep, send = exchange(keep, came, dim, place.low)
    came = swap(send, "g", 1)
    keep, send = exchange(keep, came, dim, place.high)
    came = swap(send, "g", 2)
    if place.lanes == 2:
        return add(keep, came, F32)
    return scatter(add(keep, came), "r", dim).astype(F32)


def reduce_shared_in(place, keep, send):
    came = swap(send, "c")
    if place.rows_y == 2:
        keep, send = [
            add(lax.dynamic_index_in_dim(keep, i, 0, False), lax.dynamic_index_in_dim(came, i, 0, False))
            for i in (place.y, 1 - place.y)
        ]
        return reduce_tokens(place, keep, swap(send, "y"), 0)
    total = add(keep, came)
    two, width, columns = total.shape
    parts = place.rows_y // 2
    total = total.reshape(two, width, parts, columns // parts).transpose(0, 2, 1, 3)
    mine = scatter(total.reshape(two * parts, width, columns // parts), "y", 0)[0]
    return reduce_tokens(place, mine, jnp.zeros_like(mine), 0)


def reduce_shared_out(place, keep, send):
    came = swap(send, "c")
    if place.rows_y == 2:
        keep, send = exchange(keep, came, 0, place.y)
        return reduce_tokens(place, keep, swap(send, "y"), 1)
    mine = scatter(add(keep, came), "y", 0)
    return reduce_tokens(place, mine, jnp.zeros_like(mine), 1)


def to_flat(place, x):
    rows, width = x.shape
    x = x.reshape(rows, 2, 2, place.lanes, width // place.dp)
    order = (0, 3, 2, 1, 4) if place.lanes == 2 else (0, 2, 1, 3, 4)
    return x.transpose(order).reshape(rows, width)


def weight_grad(place, left, right):
    rows, columns = right.shape
    own = columns // place.experts
    parts = right.reshape(rows, place.rows_y, 2, own)
    keep, send = [
        lax.dot_general(
            left,
            lax.dynamic_index_in_dim(parts, i, 2, False).reshape(rows, columns // 2),
            (((0,), (0,)), ((), ())),
            preferred_element_type=F32,
        ).astype(BF16)
        for i in (place.c, 1 - place.c)
    ]
    came = swap(send, "c")
    width = left.shape[1]
    if place.rows_y == 2:
        keep, send = [
            add(
                lax.dynamic_slice_in_dim(keep, i * own, own, 1),
                lax.dynamic_slice_in_dim(came, i * own, own, 1),
            )
            for i in (place.y, 1 - place.y)
        ]
        return reduce_tokens(place, keep, swap(send, "y"), 0)
    total = add(keep, came).reshape(width, place.rows_y, own).transpose(1, 0, 2)
    mine = scatter(total, "y", 0)[0]
    return reduce_tokens(place, mine, jnp.zeros_like(mine), 0)


def local(
    tokens,
    norm_attn,
    query_key_value_weight,
    attention_output_weight,
    norm_ffn,
    router,
    expert_in,
    expert_out,
    shared_gate_up_weight,
    shared_down_weight,
    block_lengths,
    routes,
    cotangent,
):
    place = Place()
    hidden = tokens[0].astype(F32)
    row_count, model_width = hidden.shape
    shard_index = lax.axis_index(DP)
    length = row_count * place.dp
    positions = shard_index * row_count + jnp.arange(row_count, dtype=jnp.int32)
    bounds = jnp.cumsum(block_lengths[0])
    query_ids = block_ids(bounds, positions)
    key_ids = block_ids(bounds, jnp.arange(length, dtype=jnp.int32))
    cosine, sine_table = rope_table(positions)
    head_shape = (row_count, HEADS, HEAD_DIM)
    scale_one = rms_scale(hidden)
    normalized_rows = (hidden * scale_one * norm_attn).astype(BF16)
    projected_rows = jnp.dot(
        normalized_rows, query_key_value_weight, preferred_element_type=F32
    )
    queries = (
        rotate(projected_rows[:, :model_width].reshape(head_shape), cosine, sine_table, 1.0)
        * HEAD_DIM ** (-0.5)
    ).astype(BF16)
    key_heads = rotate(
        projected_rows[:, model_width : 2 * model_width].reshape(head_shape),
        cosine,
        sine_table,
        1.0,
    ).astype(BF16)
    values = projected_rows[:, 2 * model_width :].reshape(head_shape).astype(BF16)
    all_keys, all_values = (
        lax.all_gather(key_heads.reshape(row_count, model_width), DP, axis=0, tiled=True),
        lax.all_gather(values.reshape(row_count, model_width), DP, axis=0, tiled=True),
    )
    expert_in = jnp.transpose(expert_in, (1, 0, 2))
    expert_out = jnp.transpose(expert_out, (1, 0, 2))
    key_span = min(512, length)
    blocks = length // key_span
    key_blocks = all_keys.reshape(blocks, key_span, HEADS, HEAD_DIM)
    value_blocks = all_values.reshape(blocks, key_span, HEADS, HEAD_DIM)
    id_blocks = key_ids.reshape(blocks, key_span)

    def stat_step(running, inputs):
        largest, row_total = running
        key_block, id_block = inputs
        scores, visible = masked_scores(queries, key_block, query_ids, id_block)
        newest = jnp.maximum(largest, jnp.max(scores, axis=-1))
        row_total = row_total * jnp.exp(largest - newest) + jnp.sum(
            jnp.where(visible[None], jnp.exp(scores - newest[:, :, None]), 0.0), axis=-1
        )
        return ((newest, row_total), None)

    start_max = jnp.full((HEADS, row_count), NEG, F32)
    (largest, row_total), _ = lax.scan(
        stat_step, (start_max, jnp.zeros((HEADS, row_count), F32)), (key_blocks, id_blocks)
    )
    log_total = (largest + jnp.log(row_total)).T

    def out_step(running, inputs):
        key_block, value_block, id_block = inputs
        scores, visible = masked_scores(queries, key_block, query_ids, id_block)
        weights_low = jnp.where(
            visible[None], jnp.exp(scores - log_total.T[:, :, None]), 0.0
        ).astype(BF16)
        return (
            running
            + jnp.einsum("hqk,khd->qhd", weights_low, value_block, preferred_element_type=F32),
            None,
        )

    attention_result, _ = lax.scan(
        out_step, jnp.zeros(head_shape, F32), (key_blocks, value_blocks, id_blocks)
    )
    attended_low = attention_result.reshape(row_count, model_width).astype(BF16)
    residual_between = hidden + jnp.dot(
        attended_low, attention_output_weight, preferred_element_type=F32
    )
    scale_two = rms_scale(residual_between)
    combined_input = (residual_between * scale_two * norm_ffn).astype(BF16)
    experts_total = router.shape[1]
    local_experts = expert_in.shape[0]
    groups = place.experts
    capacity = row_count * TOP * 5 // (4 * experts_total)
    router_scores = jnp.dot(combined_input, router, preferred_element_type=F32)
    chosen = routes[0]
    column = jnp.arange(experts_total, dtype=jnp.int32)
    pick_hot = (chosen[:, :, None] == column[None, None, :]).astype(F32)
    picked = jnp.sum(pick_hot * router_scores[:, None, :], axis=-1)
    gate_weights = jax.nn.softmax(picked, axis=-1)
    column_expert = column % groups * local_experts + column // groups
    flat_routes = chosen.reshape(row_count * TOP)
    route_hot = (flat_routes[:, None] == column_expert[None, :]).astype(jnp.int32)
    earlier = jnp.cumsum(route_hot, axis=0) - route_hot
    slot_index = jnp.sum(earlier * route_hot, axis=1)
    target = jnp.where(
        slot_index < capacity, jnp.sum(route_hot * column[None, :], axis=1) * capacity + slot_index, -1
    ).reshape(row_count, TOP)
    seats = jnp.arange(experts_total * capacity, dtype=jnp.int32)
    hot = [(target[:, k : k + 1] == seats[None, :]).astype(BF16) for k in range(TOP)]
    upstream = cotangent[0]
    grad_upper = upstream.astype(F32)

    def dispatch(matrix, rows):
        return lax.dot_general(
            matrix, rows, (((0,), (0,)), ((), ())), preferred_element_type=F32
        )

    def trade(rows):
        return lax.all_to_all(rows, EX, split_axis=1, concat_axis=1, tiled=True)

    seat_shape = (local_experts, groups, capacity, model_width)
    every = hot[0] + hot[1]
    send_rows = dispatch(every, combined_input).astype(BF16)
    seat_gates = jnp.sum(
        sum(
            (target[:, k : k + 1] == seats[None, :]) * gate_weights[:, k : k + 1] for k in range(TOP)
        ),
        axis=0,
    )
    grad_send = (dispatch(every, upstream) * seat_gates[:, None]).astype(BF16)
    arrived = trade(send_rows.reshape(seat_shape)).reshape(
        local_experts, groups * capacity, model_width
    )
    grad_arrived = trade(grad_send.reshape(seat_shape)).reshape(
        local_experts, groups * capacity, model_width
    )
    shared_result, grad_mixed, *shared_grads = ffn(
        True,
        place,
        place.shared_table(model_width),
        combined_input,
        upstream,
        shared_gate_up_weight[None],
        shared_down_weight[None],
        0,
    )
    table = place.expert_table(model_width)
    came_back, in_grads, out_grads = [], [], []
    for e in range(local_experts):
        both, in_keep, in_send, out_keep, out_send = ffn(
            False, place, table, arrived[e], grad_arrived[e], expert_in, expert_out, e
        )
        came_back.append(
            lax.all_to_all(
                both.reshape(groups, capacity, 2 * model_width),
                EX,
                split_axis=0,
                concat_axis=0,
                tiled=True,
            ).reshape(groups * capacity, 2 * model_width)
        )
        in_grads.append(reduce_experts(place, in_keep, in_send, 1))
        out_grads.append(reduce_experts(place, out_keep, out_send, 0))
    sum_shared_in = reduce_shared_in(place, *shared_grads[:2])
    sum_shared_out = reduce_shared_out(place, *shared_grads[2:])
    returned = jnp.concatenate(came_back, axis=0)
    back_rows = [
        jnp.dot(h, returned[:, :model_width], preferred_element_type=F32) for h in hot
    ]
    routed = sum(gate_weights[:, k : k + 1] * back_rows[k] for k in range(TOP))
    output = (residual_between + routed + shared_result).astype(BF16)[None]
    grad_gates = jnp.stack([jnp.sum(b * grad_upper, axis=-1) for b in back_rows], axis=1)
    grad_picked = gate_weights * (
        grad_gates - jnp.sum(gate_weights * grad_gates, axis=-1, keepdims=True)
    )
    grad_logits = jnp.sum(pick_hot * grad_picked[:, :, None], axis=1).astype(BF16)
    grad_router = jnp.einsum("td,te->de", combined_input, grad_logits, preferred_element_type=F32)
    grad_mixed = (
        grad_mixed
        + jnp.einsum("te,de->td", grad_logits, router, preferred_element_type=F32)
        + jnp.dot(every, returned[:, model_width:], preferred_element_type=F32)
    )
    grad_norm_ffn = jnp.sum(grad_mixed * residual_between * scale_two, axis=0)
    grad_middle = grad_upper + rms_back(residual_between, scale_two, norm_ffn, grad_mixed)
    grad_attn_low = grad_middle.astype(BF16)
    grad_attended = (
        jnp.einsum(
            "te,de->td", grad_attn_low, attention_output_weight, preferred_element_type=F32
        )
        .astype(BF16)
        .reshape(head_shape)
    )
    row_delta = jnp.sum(grad_attended.astype(F32) * attention_result, axis=-1)

    def back_step(grad_queries, inputs):
        key_block, value_block, id_block = inputs
        weights_low, grad_scores = score_grads(
            queries,
            grad_attended,
            log_total,
            row_delta,
            key_block,
            value_block,
            query_ids,
            id_block,
        )
        grad_queries = grad_queries + jnp.einsum(
            "hqk,khd->qhd", grad_scores, key_block, preferred_element_type=F32
        )
        grad_key_part = jnp.einsum(
            "hqk,qhd->khd", grad_scores, queries, preferred_element_type=F32
        ).reshape(key_span, model_width)
        grad_value_part = jnp.einsum(
            "hqk,qhd->khd", weights_low, grad_attended, preferred_element_type=F32
        ).reshape(key_span, model_width)
        return (grad_queries, jnp.concatenate([grad_key_part, grad_value_part], axis=1))

    grad_queries, key_terms = lax.scan(
        back_step, jnp.zeros(head_shape, F32), (key_blocks, value_blocks, id_blocks)
    )
    own_terms = lax.psum_scatter(
        key_terms.reshape(length, 2 * model_width).astype(BF16),
        DP,
        scatter_dimension=0,
        tiled=True,
    ).astype(F32)
    grad_keys = own_terms[:, :model_width].reshape(head_shape)
    grad_values = own_terms[:, model_width:].reshape(head_shape)
    grad_queries = rotate(grad_queries * HEAD_DIM ** (-0.5), cosine, sine_table, -1.0)
    grad_keys = rotate(grad_keys, cosine, sine_table, -1.0)
    grad_projected = jnp.concatenate(
        [
            grad_queries.reshape(row_count, model_width),
            grad_keys.reshape(row_count, model_width),
            grad_values.reshape(row_count, model_width),
        ],
        axis=1,
    ).astype(BF16)
    grad_normed = jnp.einsum(
        "te,de->td", grad_projected, query_key_value_weight, preferred_element_type=F32
    )
    grad_norm_attn = jnp.sum(grad_normed * hidden * scale_one, axis=0)
    grad_input = grad_middle + rms_back(hidden, scale_one, norm_attn, grad_normed)
    sum_qkv = weight_grad(place, to_flat(place, normalized_rows), grad_projected)
    sum_out = weight_grad(place, to_flat(place, attended_low), grad_attn_low)
    small = jnp.concatenate([grad_norm_ffn[:, None], grad_router], axis=1)
    small = lax.psum(small, DP + EX)
    own = model_width // place.dp
    small = lax.dynamic_slice_in_dim(small, shard_index * own, own, 0)
    sum_router = lax.dynamic_slice_in_dim(
        small[:, 1:], lax.axis_index(EX) * local_experts, local_experts, 1
    )
    sum_norm_attn = lax.dynamic_slice_in_dim(
        lax.psum(grad_norm_attn, DP + EX), shard_index * own, own, 0
    )
    part_in = jnp.stack([g.transpose(1, 0, 2).reshape(own, -1) for g in in_grads], axis=1)
    part_out = jnp.stack(out_grads, axis=1)
    return (
        output,
        grad_input[None],
        sum_norm_attn,
        sum_qkv,
        sum_out,
        small[:, 0],
        sum_router,
        part_in,
        part_out,
        sum_shared_in,
        sum_shared_out.T,
    )


def solution(mesh):
    dp, experts = mesh.shape["dp"], mesh.shape["expert"]
    finer = Mesh(mesh.devices.reshape(4, dp // 4, experts // 2, 2), ("g", "r", "y", "c"))
    whole = P()
    return jax.shard_map(
        local,
        mesh=finer,
        in_specs=(
            P(EX, DP, None),
            whole,
            whole,
            whole,
            whole,
            whole,
            P(None, EX, None),
            P(None, EX, None),
            whole,
            whole,
            P(EX, None),
            P(EX, DP, None),
            P(EX, DP, None),
        ),
        out_specs=(
            P(EX, DP, None),
            P(EX, DP, None),
            P(DP),
            P(DP, EX),
            P(DP, EX),
            P(DP),
            P(DP, EX),
            P(DP, EX, None),
            P(DP, EX, None),
            P(DP, EX),
            P(DP, EX),
        ),
        check_vma=False,
    )
```

time: 1550 us -> 1000 us (0.65)
  waiting for transfers between devices: 950 us -> 391 us
  matrix products: 256 us -> 112 us
  other arithmetic: 86.8 us -> 141 us
  Pallas kernels: 0 us -> 52.5 us
  starting transfers between devices: 18.1 us -> 53.3 us
    unnamed x19 -> x3, waiting for transfers between devices: 500 us -> 0.05 us
    reduce_scatter x7 -> x1, waiting for transfers between devices: 382 us -> 0.01 us  [local(): lax.psum_scatter(key_terms.reshape(length, 2 * model_width).astype(BF16),...]
    ppermute x0 -> x32, waiting for transfers between devices: none -> 343 us  [swap(): return lax.ppermute(a, axis, [(i, i ^ bit) for i in range(size)])]
    dot_general x38 -> x29, matrix products: 195 us -> 67.5 us  [the longest x8 31.6 us: masked_scores(): jnp.einsum('qhd,khd->hqk', queries, key_heads, preferred_element_type=F32)]
    pallas_call x0 -> x3, Pallas kernels: none -> 52.5 us  [ffn(): pl.pallas_call(functools.partial(ffn_kernel, shared, place.dp, place.expe...]
    convert_element_type x11 -> x29, other arithmetic: 14.3 us -> 59.3 us  [the longest x24 54.6 us: add(): return (a.astype(F32) + b.astype(F32)).astype(kind)]
    psum x1, blocking collectives: 6.27 us -> 45 us  [local(): lax.psum(grad_norm_attn, DP + EX)]
    ppermute x0 -> x32, starting transfers between devices: none -> 35.5 us  [swap(): return lax.ppermute(a, axis, [(i, i ^ bit) for i in range(size)])]
  transfers between devices with their start and end apart: 18 -> 39, of which waited for: 14 -> 16; matrix products, arithmetic and copies ran while one was open for 24% -> 25% of each run, Pallas kernels for 0% -> 4%
where the time goes in v1:
time: 1000 us; the launch traced here: 996 us
  waiting for transfers between devices  391 us (39%)
  local copies, waits for them, and re-layouts  185 us (18%)
  other arithmetic  141 us (14%)
  matrix products  112 us (11%)
  starting transfers between devices  53.3 us (5%)
  Pallas kernels  52.5 us (5%)
  blocking collectives  45 us (4%)
  between operations  15.6 us (2%)
    ppermute x32, waiting for transfers between devices, swap(): return lax.ppermute(a, axis, [(i, i ^ bit) for i in range(size)])  343 us
    unnamed x158, local copies, waits for them, and re-layouts  61.3 us
    convert_element_type x24, other arithmetic, add(): return (a.astype(F32) + b.astype(F32)).astype(kind)  54.6 us
    pallas_call x3, Pallas kernels, ffn(): pl.pallas_call(functools.partial(ffn_kernel, shared, place.dp, place.expe...  52.5 us
    psum x1, blocking collectives, local(): lax.psum(grad_norm_attn, DP + EX)  45 us
    ppermute x32, starting transfers between devices, swap(): return lax.ppermute(a, axis, [(i, i ^ bit) for i in range(size)])  35.5 us
    all_gather x1, waiting for transfers between devices, local(): lax.all_gather(key_heads.reshape(row_count, model_width), DP, axis=0, til...  35.5 us
    dot_general x8, matrix products, masked_scores(): jnp.einsum('qhd,khd->hqk', queries, key_heads, preferred_element_type=F32)  31.6 us
  transfers between devices with their start and end apart: 39, of which 16 were waited for; matrix products, arithmetic and copies ran while one was open for 25% of the time, Pallas kernels for 4%

profile of v1, /device:TPU:0, one launch (start us, length us, event | category | flops | bytes accessed | tf_op | source)
XLA Modules:
  0.0 996.2 jit_solution(333817910345183984)
XLA Ops:
  53.3 35.5 %all-gather.5.cloned.1.call-done = bf16[2048,768]{0,1:T(8,128)(2,1)} async-done(((bf16[256,768]{0,1:T(8,128)(2,1)}), bf16[2048,768]{0,1:T(8,128)(2,1)}) %all-gather.5.cloned.1.call-update) | async-done | bytes 3145744 | tf_op jit(solution)/shard_map/all_gather | solution.py:440
  88.7 6.1 reshape.487
  94.9 4.3 copy.166
  99.2 50.3 %while.37 = (s32[]{:T(128)}, f32[12,256]{1,0:T(8,128)S(1)}, f32[12,256]{1,0:T(8,128)}, s32[256]{0:T(256)}, s32[4,512]{1,0:T(4,128)}, /*index=5*/bf16[4,512,12,64...) while((s32[]{:T(128)}, f32[12,256]{1,0:T(8,128)S(1)}, f32[12,256]{1,0:T(8,128)}, ...), condition=%wide.region_7.8_spmd.clone, body=%wide.region_4.7_spmd.clone.sunk | while | flops 210910208 | bytes 14945984 | solution.py:462
  100.7 5.6 fusion.176
  107.0 4.1 select_reduce_fusion.4
  113.3 5.6 fusion.176
  119.6 4.1 select_reduce_fusion.4
  125.9 5.6 fusion.176
  132.2 4.1 select_reduce_fusion.4
  138.4 5.6 fusion.176
  144.8 4.1 select_reduce_fusion.4
  150.2 4.6 copy.160
  154.8 6.2 reshape.482
  160.9 4.3 copy.165
  165.9 27.1 %while.38 = (s32[]{:T(128)}, f32[256,12,64]{0,2,1:T(8,128)}, bf16[4,512,12,64]{1,3,2,0:T(8,128)(2,1)}, s32[256]{0:T(256)}, s32[4,512]{1,0:T(4,128)}, /*index=5*/...) while((s32[]{:T(128)}, f32[256,12,64]{0,2,1:T(8,128)}, ...), condition=%wide.region_9.10_spmd.clone, body=%wide.region_8.9_spmd.clone.sunk | while | flops 409468928 | bytes 3825779 | solution.py:479
  168.0 4.4 fusion.182
  174.6 4.7 fusion.182
  181.5 4.7 fusion.182
  188.3 4.7 fusion.182
  202.3 4.2 all-to-all-start.1
  209.1 11.2 %all-to-all-done.1 = bf16[2,4,80,768]{3,2,0,1:T(8,128)(2,1)} async-done(((bf16[2,4,80,768]{3,2,0,1:T(8,128)(2,1)}), bf16[2,4,80,768]{3,2,0,1:T(8,128)(2,1)}, u32[]{:S(2)}, u32[]{:S(2)}) %all-to-all-start.1) | async-done | bytes 983072 | tf_op jit(solution)/shard_map/all_to_all | solution.py:517
  220.3 4.5 all-to-all-start
  224.8 14.5 %copy.219 = bf16[768,2,4096]{2,0,1:T(8,128)(2,1)} copy(bf16[768,2,4096]{2,1,0:T(2,128)(2,1)} %param.25) | data formatting | bytes 25165824 | tf_op args[6]
  239.3 6.2 copy.220
  251.2 17.4 %shard_map.213 = (bf16[320,1536]{1,0:T(8,128)(2,1)S(1)}, bf16[2,384,2048]{2,1,0:T(8,128)(2,1)}, bf16[2,384,2048]{2,1,0:T(8,128)(2,1)}, bf16[1024,768]{1,0:T(8,128)(2,1)S(1)}, bf16[1024,768]{1,0:T(8,128)(2,1)}) custom-call(s32[24]{0:T(128)S(1)} %stack.151.table, bf16[320,768]{1,0:T(8,128)(2,1)S(1)} %bitcast.320, bf16[320,768]{1,0:T(8,128)(2,1)S(1)} %bitcast.319, ...), custom_call_target="tpu_custom_call" | custom-call | flops 9059696640 | bytes 18874368 | tf_op jit(solution)/shard_map/pallas_call | solution.py:263
  270.7 4.2 all-to-all-start.3
  277.0 17.3 %shard_map.212 = (bf16[320,1536]{1,0:T(8,128)(2,1)S(1)}, bf16[2,384,2048]{2,1,0:T(8,128)(2,1)}, bf16[2,384,2048]{2,1,0:T(8,128)(2,1)}, bf16[1024,768]{1,0:T(8,128)(2,1)S(1)}, bf16[1024,768]{1,0:T(8,128)(2,1)S(1)}) custom-call(s32[24]{0:T(128)S(1)} %stack.151.table, bf16[320,768]{1,0:T(8,128)(2,1)S(1)} %bitcast.318, bf16[320,768]{1,0:T(8,128)(2,1)S(1)} %bitcast.317, ...), custom_call_target="tpu_custom_call" | custom-call | flops 9059696640 | bytes 18874368 | tf_op jit(solution)/shard_map/pallas_call | solution.py:263
  297.6 4.2 all-to-all-start.2
  305.0 17.8 %shard_map.214 = (f32[256,768]{1,0:T(8,128)S(1)}, f32[256,768]{1,0:T(8,128)S(1)}, bf16[2,768,1024]{2,1,0:T(8,128)(2,1)}, bf16[2,768,1024]{2,1,0:T(8,128)(2,1)}, ...) custom-call(s32[28]{0:T(128)S(1)} %stack.172.table, bf16[256,768]{1,0:T(8,128)(2,1)S(1)} %copy-done.2, ...), custom_call_target="tpu_custom_call" | custom-call | flops 7247757312 | bytes 18874368 | tf_op jit(solution)/shard_map/pallas_call | solution.py:263
  341.1 81.1 %while.39 = (s32[]{:T(128)}, f32[256,12,64]{0,2,1:T(8,128)}, bf16[4,512,1536]{2,1,0:T(8,128)(2,1)}, bf16[4,512,12,64]{1,3,2,0:T(8,128)(2,1)}, s32[256]{0:T(256)S...) while((s32[]{:T(128)}, f32[256,12,64]{0,2,1:T(8,128)}, ...), condition=%wide.region_26.27_spmd.clone, body=%wide.region_25.26_spmd.clone.sunk | while | flops 1026031616 | bytes 61093140 | solution.py:616
  440.9 36.2 %collective-permute-done.16 = bf16[1024,768]{1,0:T(8,128)(2,1)} collective-permute-done((bf16[1024,768]{1,0:T(8,128)(2,1)}, bf16[1024,768]{1,0:T(8,128)(2,1)}, u32[]{:S(2)}, u32[]{:S(2)}) %collective-permute-start.16) | collective-permute-done | bytes 1572896 | tf_op jit(solution)/shard_map/ppermute | solution.py:291
  489.8 183.4 %collective-permute-done.7 = bf16[384,192]{0,1:T(8,128)(2,1)} collective-permute-done((bf16[384,192]{0,1:T(8,128)(2,1)}, bf16[384,192]{0,1:T(8,128)(2,1)}, u32[]{:S(2)}, u32[]{:S(2)}) %collective-permute-start.7) | collective-permute-done | bytes 147488 | tf_op jit(solution)/shard_map/ppermute | solution.py:291
  679.2 4.3 collective-permute-done.29
  696.3 5.3 add_convert_fusion.1
  701.6 7.1 collective-permute-done.9
  723.3 12.3 %collective-permute-done.20 = bf16[512,768]{1,0:T(8,128)(2,1)} collective-permute-done((bf16[512,768]{1,0:T(8,128)(2,1)}, bf16[512,768]{1,0:T(8,128)(2,1)}, u32[]{:S(2)}, u32[]{:S(2)}) %collective-permute-start.20) | collective-permute-done | bytes 786464 | tf_op jit(solution)/shard_map/ppermute | solution.py:291
  737.5 6.3 add_convert_fusion.5
  746.3 5.0 add_convert_fusion.3
  781.1 8.2 collective-permute-done.11
  791.6 54.4 %collective-permute-done.25 = bf16[192,1024]{1,0:T(8,128)(2,1)S(1)} collective-permute-done((bf16[192,1024]{1,0:T(8,128)(2,1)S(1)}, bf16[192,1024]{1,0:T(8,128)(2,1)S(1)}, u32[]{:S(2)}, u32[]{:S(2)}) %collective-permute-start.25) | collective-permute-done | bytes 393248 | tf_op jit(solution)/shard_map/ppermute | solution.py:291
  853.9 19.1 %collective-permute-done.26 = bf16[96,1024]{1,0:T(8,128)(2,1)S(1)} collective-permute-done((bf16[96,1024]{1,0:T(8,128)(2,1)S(1)}, bf16[96,1024]{1,0:T(8,128)(2,1)S(1)}, u32[]{:S(2)}, u32[]{:S(2)}) %collective-permute-start.26) | collective-permute-done | bytes 196640 | tf_op jit(solution)/shard_map/ppermute | solution.py:291
  883.4 5.7 collective-permute-done.15
  889.2 4.2 add_bitcast_fusion
  908.7 4.1 copy.192
  924.9 45.0 %all-reduce = (f32[768]{0:T(1024)}, f32[768,9]{0,1:T(8,128)}) all-reduce(f32[768]{0:T(1024)S(1)} %get-tuple-element.453, f32[768,9]{0,1:T(8,128)} %pad_maximum_fusion.7), channel_id=1, replica_groups=mesh['g'=4,'r'=2,'y'=2,'c'=2] {'g','r','y','c'}, use_global_device_ids=true, to_apply=%region_30.31 | all-reduce | flops 7680 | bytes 61440 | tf_op jit(solution)/shard_map/psum | solution.py:652
  977.2 4.5 collective-permute-done.3
  983.5 5.2 collective-permute-done.4
  (486 shorter events, 349.8 us)
Async XLA Ops:
  7.2 81.5 %all-gather.5.cloned.1.call-start = ((), (), s32[]{:S(2)}) async-start(), calls=%async_computation.6 | async-start | bytes 3538944 | tf_op jit(solution)/shard_map/all_gather | solution.py:440
  22.8 127.3 %all-gather.3.cloned.1.call-start = ((), (), s32[]{:S(2)}) async-start(), calls=%async_computation.5 | async-start | bytes 3538944 | tf_op jit(solution)/shard_map/all_gather | solution.py:441
  202.3 18.1 %all-to-all-start.1 = ((bf16[2,4,80,768]{3,2,0,1:T(8,128)(2,1)}), bf16[2,4,80,768]{3,2,0,1:T(8,128)(2,1)}, u32[]{:S(2)}, u32[]{:S(2)}) async-start(bf16[2,4,80,768]{3,2,0,1:T(8,128)(2,1)} %copy.170), calls=%async_computation.1 | async-start | bytes 1966080 | tf_op jit(solution)/shard_map/all_to_all | solution.py:517
  220.3 28.7 %all-to-all-start = ((bf16[2,4,80,768]{3,2,0,1:T(8,128)(2,1)}), bf16[2,4,80,768]{3,2,0,1:T(8,128)(2,1)}, u32[]{:S(2)}, u32[]{:S(2)}) async-start(bf16[2,4,80,768]{3,2,0,1:T(8,128)(2,1)} %copy.169), calls=%async_computation | async-start | bytes 1966080 | tf_op jit(solution)/shard_map/all_to_all | solution.py:517
  270.7 26.9 %all-to-all-start.3 = ((bf16[4,80,1536]{2,1,0:T(8,128)(2,1)}), bf16[4,80,1536]{2,1,0:T(8,128)(2,1)}, u32[]{:S(2)}, u32[]{:S(2)}) async-start(bf16[4,80,1536]{2,1,0:T(8,128)(2,1)} %bitcast.316), calls=%async_computation.3 | async-start | bytes 1966080 | tf_op jit(solution)/shard_map/all_to_all | solution.py:552
  297.6 29.4 %all-to-all-start.2 = ((bf16[4,80,1536]{2,1,0:T(8,128)(2,1)}), bf16[4,80,1536]{2,1,0:T(8,128)(2,1)}, u32[]{:S(2)}, u32[]{:S(2)}) async-start(bf16[4,80,1536]{2,1,0:T(8,128)(2,1)} %bitcast.315), calls=%async_computation.2 | async-start | bytes 1966080 | tf_op jit(solution)/shard_map/all_to_all | solution.py:552
  301.8 453.3 %reduce-scatter.2.cloned.1.call-start = ((), (), s32[]{:S(2)}) async-start(), calls=%async_computation.7 | async-start | bytes 7077888 | tf_op jit(solution)/shard_map/reduce_scatter | solution.py:619
  422.2 10.6 %collective-permute-start.27 = (bf16[384,2048]{1,0:T(8,128)(2,1)}, bf16[384,2048]{1,0:T(8,128)(2,1)}, u32[]{:S(2)}, u32[]{:S(2)}) collective-permute-start(bf16[384,2048]{1,0:T(8,128)(2,1)} %copy-done.19), channel_id=1, source_target_pairs={{0,1},{1,0},{2,3},{3,2},{4,5},{5,4},{6,7},{7,6},{8,9},{9,8},{10,11... | collective-permute-start | bytes 4718600 | tf_op jit(solution)/shard_map/ppermute | solution.py:291
  422.7 54.4 %collective-permute-start.16 = (bf16[1024,768]{1,0:T(8,128)(2,1)}, bf16[1024,768]{1,0:T(8,128)(2,1)}, u32[]{:S(2)}, u32[]{:S(2)}) collective-permute-start(bf16[1024,768]{1,0:T(8,128)(2,1)} %copy-done.18), channel_id=1, source_target_pairs={{0,4},{4,0},{1,5},{5,1},{2,6},{6,2},{3,7},{7,3},{8,12},{12,8},{9,1... | collective-permute-start | bytes 4718600 | tf_op jit(solution)/shard_map/ppermute | solution.py:291
  423.6 270.4 %collective-permute-start.22 = (bf16[2,768,1024]{2,1,0:T(8,128)(2,1)}, bf16[2,768,1024]{2,1,0:T(8,128)(2,1)}, u32[]{:S(2)}, u32[]{:S(2)}) collective-permute-start(bf16[2,768,1024]{2,1,0:T(8,128)(2,1)} %get-tuple-element.183), channel_id=1, source_target_pairs={{0,1},{1,0},{2,3},{3,2},{4,5},{5,4},{6,7},{7,6},{8,9},{9,8},{10,11... | collective-permute-start | bytes 9437192 | tf_op jit(solution)/shard_map/ppermute | solution.py:291
  431.2 7.5 collective-permute-start.5
  431.7 305.8 %collective-permute-start.10 = (bf16[2,384,2048]{2,1,0:T(8,128)(2,1)}, bf16[2,384,2048]{2,1,0:T(8,128)(2,1)}, u32[]{:S(2)}, u32[]{:S(2)}) collective-permute-start(bf16[2,384,2048]{2,1,0:T(8,128)(2,1)} %get-tuple-element.175), channel_id=1, source_target_pairs={{0,4},{4,0},{1,5},{5,1},{2,6},{6,2},{3,7},{7,3},{8,12},{12,8},{9,1... | collective-permute-start | bytes 9437192 | tf_op jit(solution)/shard_map/ppermute | solution.py:291
  436.6 46.6 %collective-permute-start.28 = (bf16[192,2048]{1,0:T(8,128)(2,1)}, bf16[192,2048]{1,0:T(8,128)(2,1)}, u32[]{:S(2)}, u32[]{:S(2)}) collective-permute-start(bf16[192,2048]{1,0:T(8,128)(2,1)} %get-tuple-element.528), channel_id=1, source_target_pairs={{0,2},{2,0},{1,3},{3,1},{4,6},{6,4},{5,7},{7,5},{8,10},{10,8},{9,1... | collective-permute-start | bytes 2359304 | tf_op jit(solution)/shard_map/ppermute | solution.py:291
  438.3 43.0 %copy-start.62 = (f32[768]{0:T(1024)S(1)}, f32[768]{0:T(1024)}, u32[]{:S(2)}) copy-start(f32[768]{0:T(1024)} %param.20) | copy-start | bytes 9220
  440.6 37.4 %collective-permute-start.6 = (bf16[768,192]{0,1:T(8,128)(2,1)S(1)}, bf16[768,192]{0,1:T(8,128)(2,1)}, u32[]{:S(2)}, u32[]{:S(2)}) collective-permute-start(bf16[768,192]{0,1:T(8,128)(2,1)S(1)} %get-tuple-element.543), channel_id=1, source_target_pairs={{0,2},{2,0},{1,3},{3,1},{4,6},{6,4},{5,7},{7,5},{8,10},{10,8},{9,1... | collective-permute-start | bytes 884744 | tf_op jit(solution)/shard_map/ppermute | solution.py:291
  477.2 208.0 %collective-permute-start.19 = (bf16[1024,768]{1,0:T(8,128)(2,1)}, bf16[1024,768]{1,0:T(8,128)(2,1)}, u32[]{:S(2)}, u32[]{:S(2)}) collective-permute-start(bf16[1024,768]{1,0:T(8,128)(2,1)} %get-tuple-element.181), channel_id=1, source_target_pairs={{0,4},{4,0},{1,5},{5,1},{2,6},{6,2},{3,7},{7,3},{8,12},{12,8},{9,1... | collective-permute-start | bytes 4718600 | tf_op jit(solution)/shard_map/ppermute | solution.py:291
  478.0 268.3 %collective-permute-start.13 = (bf16[2,384,2048]{2,1,0:T(8,128)(2,1)}, bf16[2,384,2048]{2,1,0:T(8,128)(2,1)}, u32[]{:S(2)}, u32[]{:S(2)}) collective-permute-start(bf16[2,384,2048]{2,1,0:T(8,128)(2,1)} %get-tuple-element.177), channel_id=1, source_target_pairs={{0,4},{4,0},{1,5},{5,1},{2,6},{6,2},{3,7},{7,3},{8,12},{12,8},{9,1... | collective-permute-start | bytes 9437192 | tf_op jit(solution)/shard_map/ppermute | solution.py:291
  483.3 190.0 %collective-permute-start.7 = (bf16[384,192]{0,1:T(8,128)(2,1)}, bf16[384,192]{0,1:T(8,128)(2,1)}, u32[]{:S(2)}, u32[]{:S(2)}) collective-permute-start(bf16[384,192]{0,1:T(8,128)(2,1)} %get-tuple-element.567), channel_id=1, source_target_pairs={{0,4},{4,0},{1,5},{5,1},{2,6},{6,2},{3,7},{7,3},{8,12},{12,8},{9,1... | collective-permute-start | bytes 442376 | tf_op jit(solution)/shard_map/ppermute | solution.py:291
  488.0 186.2 %copy-start.3 = (bf16[256,768]{1,0:T(8,128)(2,1)S(1)}, bf16[256,768]{1,0:T(8,128)(2,1)}, u32[]{:S(2)}) copy-start(bf16[256,768]{1,0:T(8,128)(2,1)} %copy-done.1) | copy-start | bytes 1179652
  488.0 187.0 %copy-start.7 = (bf16[1024,768]{1,0:T(8,128)(2,1)S(1)}, bf16[1024,768]{1,0:T(8,128)(2,1)}, u32[]{:S(2)}) copy-start(bf16[1024,768]{1,0:T(8,128)(2,1)} %copy-done.6) | copy-start | bytes 4718596
  673.3 10.3 %collective-permute-start.29 = (bf16[192,1024]{1,0:T(8,128)(2,1)S(1)}, bf16[192,1024]{1,0:T(8,128)(2,1)S(1)}, u32[]{:S(2)}, u32[]{:S(2)}) collective-permute-start(bf16[192,1024]{1,0:T(8,128)(2,1)S(1)} %get-tuple-element.538), channel_id=1, source_target_pairs={{0,4},{4,0},{1,5},{5,1},{2,6},{6,2},{3,7},{7,3},{8,12},{12,8},{9,1... | collective-permute-start | bytes 1179656 | tf_op jit(solution)/shard_map/ppermute | solution.py:291
  683.5 5.5 collective-permute-start.8
  685.1 8.8 copy-start.51
  685.1 8.1 collective-permute-start.30
  685.8 10.5 %copy-start.39 = (bf16[2,768,1024]{2,1,0:T(8,128)(2,1)S(1)}, bf16[2,768,1024]{2,1,0:T(8,128)(2,1)}, u32[]{:S(2)}) copy-start(bf16[2,768,1024]{2,1,0:T(8,128)(2,1)} %get-tuple-element.182) | copy-start | bytes 9437188
  689.0 30.2 %collective-permute-start.17 = (bf16[512,768]{1,0:T(8,128)(2,1)}, bf16[512,768]{1,0:T(8,128)(2,1)}, u32[]{:S(2)}, u32[]{:S(2)}) collective-permute-start(bf16[512,768]{1,0:T(8,128)(2,1)} %get-tuple-element.532), channel_id=1, source_target_pairs={{0,8},{8,0},{16,24},{24,16},{1,9},{9,1},{17,25},{25,17},{2,10},{10... | collective-permute-start | bytes 2359304 | tf_op jit(solution)/shard_map/ppermute | solution.py:291
  693.2 15.5 %collective-permute-start.9 = (bf16[96,192]{0,1:T(8,128)(2,1)S(1)}, bf16[96,192]{0,1:T(8,128)(2,1)S(1)}, u32[]{:S(2)}, u32[]{:S(2)}) collective-permute-start(bf16[96,192]{0,1:T(8,128)(2,1)S(1)} %add_convert_fusion.46), channel_id=1, source_target_pairs={{0,16},{8,24},{16,0},{24,8},{1,17},{9,25},{17,1},{25,9},{2,18},{10... | collective-permute-start | bytes 110600 | tf_op jit(solution)/shard_map/ppermute | solution.py:291
  694.0 17.7 %collective-permute-start.31 = (bf16[192,256]{1,0:T(8,128)(2,1)S(1)}, bf16[192,256]{1,0:T(8,128)(2,1)S(1)}, u32[]{:S(2)}, u32[]{:S(2)}) collective-permute-start(bf16[192,256]{1,0:T(8,128)(2,1)S(1)} %add_convert_fusion.42), channel_id=1, source_target_pairs={{0,16},{8,24},{16,0},{24,8},{1,17},{9,25},{17,1},{25,9},{2,18},{10... | collective-permute-start | bytes 294920 | tf_op jit(solution)/shard_map/ppermute | solution.py:291
  696.3 18.0 %copy-start.25 = (f32[256,12,64]{0,2,1:T(8,128)S(1)}, f32[256,12,64]{0,2,1:T(8,128)}, u32[]{:S(2)}) copy-start(f32[256,12,64]{0,2,1:T(8,128)} %get-tuple-element.172) | copy-start | bytes 2359300
  708.7 26.9 %collective-permute-start.20 = (bf16[512,768]{1,0:T(8,128)(2,1)}, bf16[512,768]{1,0:T(8,128)(2,1)}, u32[]{:S(2)}, u32[]{:S(2)}) collective-permute-start(bf16[512,768]{1,0:T(8,128)(2,1)} %get-tuple-element.534), channel_id=1, source_target_pairs={{0,8},{8,0},{16,24},{24,16},{1,9},{9,1},{17,25},{25,17},{2,10},{10... | collective-permute-start | bytes 2359304 | tf_op jit(solution)/shard_map/ppermute | solution.py:291
  711.7 39.7 %collective-permute-start.23 = (bf16[768,1024]{1,0:T(8,128)(2,1)}, bf16[768,1024]{1,0:T(8,128)(2,1)}, u32[]{:S(2)}, u32[]{:S(2)}) collective-permute-start(bf16[768,1024]{1,0:T(8,128)(2,1)} %get-tuple-element.520), channel_id=1, source_target_pairs={{0,2},{2,0},{1,3},{3,1},{4,6},{6,4},{5,7},{7,5},{8,10},{10,8},{9,1... | collective-permute-start | bytes 4718600 | tf_op jit(solution)/shard_map/ppermute | solution.py:291
  721.2 53.3 %collective-permute-start.18 = (bf16[256,768]{1,0:T(8,128)(2,1)}, bf16[256,768]{1,0:T(8,128)(2,1)}, u32[]{:S(2)}, u32[]{:S(2)}) collective-permute-start(bf16[256,768]{1,0:T(8,128)(2,1)} %add_convert_fusion.26), channel_id=1, source_target_pairs={{0,16},{8,24},{16,0},{24,8},{1,17},{9,25},{17,1},{25,9},{2,18},{10... | collective-permute-start | bytes 1179656 | tf_op jit(solution)/shard_map/ppermute | solution.py:291
  737.5 42.3 %collective-permute-start.21 = (bf16[256,768]{1,0:T(8,128)(2,1)}, bf16[256,768]{1,0:T(8,128)(2,1)}, u32[]{:S(2)}, u32[]{:S(2)}) collective-permute-start(bf16[256,768]{1,0:T(8,128)(2,1)} %add_convert_fusion.24), channel_id=1, source_target_pairs={{0,16},{8,24},{16,0},{24,8},{1,17},{9,25},{17,1},{25,9},{2,18},{10... | collective-permute-start | bytes 1179656 | tf_op jit(solution)/shard_map/ppermute | solution.py:291
  743.8 45.5 %collective-permute-start.11 = (bf16[2,192,2048]{2,1,0:T(8,128)(2,1)}, bf16[2,192,2048]{2,1,0:T(8,128)(2,1)}, u32[]{:S(2)}, u32[]{:S(2)}) collective-permute-start(bf16[2,192,2048]{2,1,0:T(8,128)(2,1)} %get-tuple-element.522), channel_id=1, source_target_pairs={{0,8},{8,0},{16,24},{24,16},{1,9},{9,1},{17,25},{25,17},{2,10},{10... | collective-permute-start | bytes 4718600 | tf_op jit(solution)/shard_map/ppermute | solution.py:291
  751.3 94.9 %collective-permute-start.14 = (bf16[2,192,2048]{2,1,0:T(8,128)(2,1)}, bf16[2,192,2048]{2,1,0:T(8,128)(2,1)}, u32[]{:S(2)}, u32[]{:S(2)}) collective-permute-start(bf16[2,192,2048]{2,1,0:T(8,128)(2,1)} %get-tuple-element.524), channel_id=1, source_target_pairs={{0,8},{8,0},{16,24},{24,16},{1,9},{9,1},{17,25},{25,17},{2,10},{10... | collective-permute-start | bytes 4718600 | tf_op jit(solution)/shard_map/ppermute | solution.py:291
  754.6 21.5 %collective-permute-start.24 = (bf16[384,1024]{1,0:T(8,128)(2,1)}, bf16[384,1024]{1,0:T(8,128)(2,1)}, u32[]{:S(2)}, u32[]{:S(2)}) collective-permute-start(bf16[384,1024]{1,0:T(8,128)(2,1)} %get-tuple-element.530), channel_id=1, source_target_pairs={{0,4},{4,0},{1,5},{5,1},{2,6},{6,2},{3,7},{7,3},{8,12},{12,8},{9,1... | collective-permute-start | bytes 2359304 | tf_op jit(solution)/shard_map/ppermute | solution.py:291
  774.5 100.0 %collective-permute-start = (bf16[768,1152]{1,0:T(8,128)(2,1)S(1)}, bf16[768,1152]{1,0:T(8,128)(2,1)S(1)}, u32[]{:S(2)}, u32[]{:S(2)}) collective-permute-start(bf16[768,1152]{1,0:T(8,128)(2,1)S(1)} %convolution_convert_fusion), channel_id=1, source_target_pairs={{0,1},{1,0},{2,3},{3,2},{4,5},{5,4},{6,7},{7,6},{8,9},{9,8},{10,11... | collective-permute-start | bytes 5308424 | tf_op jit(solution)/shard_map/ppermute | solution.py:291
  776.2 13.1 %copy-start.31 = (bf16[2,192,2048]{2,1,0:T(8,128)(2,1)S(1)}, bf16[2,192,2048]{2,1,0:T(8,128)(2,1)}, u32[]{:S(2)}) copy-start(bf16[2,192,2048]{2,1,0:T(8,128)(2,1)} %get-tuple-element.521) | copy-start | bytes 4718596
  777.7 68.3 %collective-permute-start.25 = (bf16[192,1024]{1,0:T(8,128)(2,1)S(1)}, bf16[192,1024]{1,0:T(8,128)(2,1)S(1)}, u32[]{:S(2)}, u32[]{:S(2)}) collective-permute-start(bf16[192,1024]{1,0:T(8,128)(2,1)S(1)} %get-tuple-element.540), channel_id=1, source_target_pairs={{0,8},{8,0},{16,24},{24,16},{1,9},{9,1},{17,25},{25,17},{2,10},{10... | collective-permute-start | bytes 1179656 | tf_op jit(solution)/shard_map/ppermute | solution.py:291
  781.1 65.1 %copy-start.32 = (bf16[2,192,2048]{2,1,0:T(8,128)(2,1)S(1)}, bf16[2,192,2048]{2,1,0:T(8,128)(2,1)}, u32[]{:S(2)}) copy-start(bf16[2,192,2048]{2,1,0:T(8,128)(2,1)} %get-tuple-element.523) | copy-start | bytes 4718596
  791.6 91.8 %collective-permute-start.12 = (bf16[2,96,2048]{2,1,0:T(8,128)(2,1)}, bf16[2,96,2048]{2,1,0:T(8,128)(2,1)}, u32[]{:S(2)}, u32[]{:S(2)}) collective-permute-start(bf16[2,96,2048]{2,1,0:T(8,128)(2,1)} %add_convert_fusion.16), channel_id=1, source_target_pairs={{0,16},{8,24},{16,0},{24,8},{1,17},{9,25},{17,1},{25,9},{2,18},{10... | collective-permute-start | bytes 2359304 | tf_op jit(solution)/shard_map/ppermute | solution.py:291
  846.1 26.8 %collective-permute-start.26 = (bf16[96,1024]{1,0:T(8,128)(2,1)S(1)}, bf16[96,1024]{1,0:T(8,128)(2,1)S(1)}, u32[]{:S(2)}, u32[]{:S(2)}) collective-permute-start(bf16[96,1024]{1,0:T(8,128)(2,1)S(1)} %add_convert_fusion.35), channel_id=1, source_target_pairs={{0,16},{8,24},{16,0},{24,8},{1,17},{9,25},{17,1},{25,9},{2,18},{10... | collective-permute-start | bytes 589832 | tf_op jit(solution)/shard_map/ppermute | solution.py:291
  848.5 40.6 %collective-permute-start.15 = (bf16[2,96,2048]{2,1,0:T(8,128)(2,1)}, bf16[2,96,2048]{2,1,0:T(8,128)(2,1)}, u32[]{:S(2)}, u32[]{:S(2)}) collective-permute-start(bf16[2,96,2048]{2,1,0:T(8,128)(2,1)} %add_convert_fusion.14), channel_id=1, source_target_pairs={{0,16},{8,24},{16,0},{24,8},{1,17},{9,25},{17,1},{25,9},{2,18},{10... | collective-permute-start | bytes 2359304 | tf_op jit(solution)/shard_map/ppermute | solution.py:291
  880.0 32.7 %collective-permute-start.1 = (bf16[768,576]{0,1:T(8,128)(2,1)}, bf16[768,576]{0,1:T(8,128)(2,1)}, u32[]{:S(2)}, u32[]{:S(2)}) collective-permute-start(bf16[768,576]{0,1:T(8,128)(2,1)} %copy.183), channel_id=1, source_target_pairs={{0,2},{2,0},{1,3},{3,1},{4,6},{6,4},{5,7},{7,5},{8,10},{10,8},{9,1... | collective-permute-start | bytes 2654216 | tf_op jit(solution)/shard_map/ppermute | solution.py:291
  921.8 53.0 %copy-start.77 = (f32[256]{0:T(256)S(1)}, f32[256]{0:T(256)}, u32[]{:S(2)}) copy-start(f32[256]{0:T(256)} %get-tuple-element.581) | copy-start | bytes 3076
  921.8 51.5 %collective-permute-start.2 = (bf16[384,576]{1,0:T(8,128)(2,1)}, bf16[384,576]{1,0:T(8,128)(2,1)}, u32[]{:S(2)}, u32[]{:S(2)}) collective-permute-start(bf16[384,576]{1,0:T(8,128)(2,1)} %get-tuple-element.549), channel_id=1, source_target_pairs={{0,4},{4,0},{1,5},{5,1},{2,6},{6,2},{3,7},{7,3},{8,12},{12,8},{9,1... | collective-permute-start | bytes 1327112 | tf_op jit(solution)/shard_map/ppermute | solution.py:291
  974.7 7.0 collective-permute-start.3
  981.7 6.9 collective-permute-start.4
  (97 other events, 264.7 us)
Sparse Core Ops, SparseCore 0:
  22.9 65.7 all-gather.4
  91.5 58.6 all-gather.2
  422.4 144.9 reduce-scatter.1

commit v2 on v1

--- a/solution.py
+++ b/solution.py
@@ -21,27 +21,11 @@
 
 
 def rope_table(positions):
+    lane = jnp.arange(2 * HEAD_DIM, dtype=jnp.int32) % HEAD_DIM
     half_dim = HEAD_DIM // 2
-    frequency = 10000.0 ** (-jnp.arange(half_dim, dtype=F32) * 2.0 / HEAD_DIM)
+    frequency = 10000.0 ** (-(lane % half_dim).astype(F32) * 2.0 / HEAD_DIM)
     angles = positions.astype(F32)[:, None] * frequency[None, :]
-    return (jnp.cos(angles)[:, None, :], jnp.sin(angles)[:, None, :])
-
-
-def rotate(values, cosine, sine_table, direction):
-    half_dim = HEAD_DIM // 2
-    first_half = values[..., :half_dim]
-    second = values[..., half_dim:]
-    return jnp.concatenate(
-        [
-            first_half * cosine - direction * second * sine_table,
-            second * cosine + direction * first_half * sine_table,
-        ],
-        axis=-1,
-    )
-
-
-def block_ids(bounds, positions):
-    return jnp.sum((bounds[None, :] <= positions[:, None]).astype(jnp.int32), axis=1)
+    return jnp.cos(angles), jnp.sin(angles) * jnp.where(lane < half_dim, -1.0, 1.0)
 
 
 def rms_scale(hidden):
@@ -52,20 +36,6 @@
     normed_grad = upstream * gain_vector
     inner_mean = jnp.mean(normed_grad * hidden, axis=-1, keepdims=True)
     return scale_rows * normed_grad - hidden * scale_rows**3 * inner_mean
-
-
-def masked_scores(queries, key_heads, query_ids, key_ids):
-    scores = jnp.einsum("qhd,khd->hqk", queries, key_heads, preferred_element_type=F32)
-    visible = query_ids[:, None] >= key_ids[None, :]
-    return (jnp.where(visible[None], scores, NEG), visible)
-
-
-def score_grads(queries, grad_out, log_total, row_delta, key_heads, values, query_ids, key_ids):
-    scores, visible = masked_scores(queries, key_heads, query_ids, key_ids)
-    weights_full = jnp.where(visible[None], jnp.exp(scores - log_total.T[:, :, None]), 0.0)
-    grad_weights = jnp.einsum("qhd,khd->hqk", grad_out, values, preferred_element_type=F32)
-    grad_scores = (weights_full * (grad_weights - row_delta.T[:, :, None])).astype(BF16)
-    return (weights_full.astype(BF16), grad_scores)
 
 
 class Place:
@@ -138,6 +108,362 @@
 
 def nn(a, b):
     return lax.dot_general(a, b, (((1,), (0,)), ((), ())), preferred_element_type=F32)
+
+
+def turn(x, cosine, sine):
+    width = x.shape[1]
+    lane = lax.broadcasted_iota(jnp.int32, x.shape, 1) % HEAD_DIM
+    other = jnp.where(
+        lane < HEAD_DIM // 2,
+        pltpu.roll(x, width - HEAD_DIM // 2, 1),
+        pltpu.roll(x, HEAD_DIM // 2, 1),
+    )
+    times = width // cosine.shape[1]
+    cosine = jnp.concatenate([cosine] * times, axis=1)
+    sine = jnp.concatenate([sine] * times, axis=1)
+    return x * cosine + other * sine
+
+
+def project_kernel(x_ref, gain_ref, w_ref, cos_ref, sin_ref, normed_ref, q_ref, kv_ref):
+    step = pl.program_id(0)
+    groups = q_ref.shape[0]
+    rows, width = x_ref.shape
+    half, three = rows // 2, 3 * HEAD_DIM
+
+    @pl.when(step == 0)
+    def _():
+        x = x_ref[...].astype(F32)
+        normed_ref[...] = (x * rms_scale(x) * gain_ref[...]).astype(BF16)
+
+    part = nn(normed_ref[...], w_ref[...])
+
+    @pl.when(step == 0)
+    def _():
+        q = (turn(part, cos_ref[...], sin_ref[...]) * HEAD_DIM**-0.5).astype(F32)
+        for g in range(groups):
+            own = q[:, g * three : (g + 1) * three].astype(BF16)
+            q_ref[g, :, 0:128] = own[:half, :128]
+            q_ref[g, :, 128:256] = own[half:, :128]
+            q_ref[g, :, 256:320] = own[:half, 128:]
+            q_ref[g, :, 320:384] = own[half:, 128:]
+
+    @pl.when(step == 1)
+    def _():
+        k = turn(part, cos_ref[...], sin_ref[...])
+        for g in range(groups):
+            own = k[:, g * three : (g + 1) * three].astype(BF16)
+            kv_ref[g, :, 0:128] = own[:, :128]
+            kv_ref[g, :, 256:320] = own[:, 128:]
+
+    @pl.when(step == 2)
+    def _():
+        for g in range(groups):
+            own = part[:, g * three : (g + 1) * three].astype(BF16)
+            kv_ref[g, :, 128:256] = own[:, :128]
+            kv_ref[g, :, 320:384] = own[:, 128:]
+
+
+def project(place, x, gain, weight, cosine, sine):
+    rows, width = x.shape
+    whole = lambda *shape: pl.BlockSpec(shape, lambda i: (0,) * len(shape))
+    return pl.pallas_call(
+        project_kernel,
+        grid=(3,),
+        out_shape=(
+            jax.ShapeDtypeStruct((rows, width), BF16),
+            jax.ShapeDtypeStruct((place.groups, rows // 2, 384), BF16),
+            jax.ShapeDtypeStruct((place.groups, rows, 384), BF16),
+        ),
+        in_specs=[
+            whole(rows, width),
+            whole(1, width),
+            pl.BlockSpec((width, width), lambda i: (0, i)),
+            whole(rows, 128),
+            whole(rows, 128),
+        ],
+        out_specs=(
+            whole(rows, width),
+            whole(place.groups, rows // 2, 384),
+            whole(place.groups, rows, 384),
+        ),
+        compiler_params=pltpu.CompilerParams(vmem_limit_bytes=32 * 1024 * 1024),
+        cost_estimate=pl.CostEstimate(
+            flops=6 * rows * width * width, bytes_accessed=10 * width * width, transcendentals=0
+        ),
+    )(x, gain[None], weight, cosine, sine)
+
+
+def unpack(packed, second_low):
+    half = packed.shape[0]
+    x = packed.astype(F32)
+    lane = lax.broadcasted_iota(jnp.int32, (half, 128), 1)
+    low = lane < HEAD_DIM
+    first, second, third = x[:, 0:128], x[:, 128:256], x[:, 256:384]
+    turned = pltpu.roll(third, HEAD_DIM, 1)
+    zero = jnp.zeros_like(third)
+    pair = [
+        jnp.where(low, first, zero),
+        jnp.where(low, second, zero),
+        jnp.where(low, zero, first),
+        jnp.where(low, zero, second),
+    ]
+    if second_low:
+        single = [jnp.where(low, third, zero), jnp.where(low, turned, zero)]
+    else:
+        single = [jnp.where(low, zero, turned), jnp.where(low, zero, third)]
+    return (
+        jnp.concatenate(pair, axis=0).astype(BF16),
+        jnp.concatenate(single, axis=0).astype(BF16),
+    )
+
+
+def visible_keys(kz, source, lanes, rows, limit):
+    first = (kz * lanes + source) * rows
+    place = first + lax.broadcasted_iota(jnp.int32, (rows, limit.shape[1]), 0)
+    return place < limit
+
+
+def attend_kernel(sources, lanes, info, limit_ref, q_ref, *refs):
+    kv_refs, (out_ref, lse_ref, turned) = refs[:sources], refs[sources:]
+    shards, half, _ = q_ref.shape
+    rows = 2 * half
+    for s in range(sources):
+        for z in range(shards):
+            turned[s, z] = kv_refs[s][z].astype(F32).T.astype(BF16)
+
+    def shard(z, carry):
+        pair, single = unpack(q_ref[z], True)
+        limit = limit_ref[z]
+
+        def step(kz, state):
+            largest, total, acc_pair, acc_single = state
+            scores = []
+            for s in range(sources):
+                keep = visible_keys(kz, info[shards + s], lanes, rows, limit)
+                kv = kv_refs[s]
+                two = nt(kv[kz, :, 0:128], pair)
+                one = nt(kv[kz, :, 256:384], single)
+                both = jnp.concatenate([two, one], axis=1)
+                keep = jnp.concatenate([keep] * 3, axis=1)
+                scores.append(jnp.where(keep, both, NEG))
+            newest = largest
+            for sc in scores:
+                newest = jnp.maximum(newest, jnp.max(sc, axis=0, keepdims=True))
+            fade = jnp.exp(largest - newest)
+            total = total * fade
+            acc_pair = acc_pair * fade[:, : 2 * rows]
+            acc_single = acc_single * fade[:, 2 * rows :]
+            for s, sc in enumerate(scores):
+                power = jnp.exp(sc - newest)
+                total = total + jnp.sum(power, axis=0, keepdims=True)
+                power = power.astype(BF16)
+                acc_pair = acc_pair + nn(turned[s, kz, 128:256, :], power[:, : 2 * rows])
+                acc_single = acc_single + nn(turned[s, kz, 256:384, :], power[:, 2 * rows :])
+            return newest, total, acc_pair, acc_single
+
+        largest, total, acc_pair, acc_single = lax.fori_loop(
+            0,
+            info[z],
+            step,
+            (
+                jnp.full((1, 3 * rows), NEG, F32),
+                jnp.zeros((1, 3 * rows), F32),
+                jnp.zeros((128, 2 * rows), F32),
+                jnp.zeros((128, rows), F32),
+            ),
+        )
+        lse_ref[z] = largest + jnp.log(total)
+        share = 1.0 / total
+        first = acc_pair[:HEAD_DIM, :rows] * share[:, :rows]
+        second = acc_pair[HEAD_DIM:, rows:] * share[:, rows : 2 * rows]
+        third = acc_single[HEAD_DIM:] * share[:, 2 * rows :]
+        packed = jnp.concatenate(
+            [a[:, part] for part in (slice(0, half), slice(half, rows)) for a in (first, second)]
+            + [third[:, :half], third[:, half:]],
+            axis=0,
+        )
+        out_ref[z] = packed.T.astype(BF16)
+        return carry
+
+    lax.fori_loop(0, shards, shard, 0)
+
+
+def attend(place, info, limit, q, kvs):
+    shards, half, lanes = q.shape
+    vmem = pl.BlockSpec(memory_space=pltpu.VMEM)
+    sources = len(kvs)
+    work = 2 * 4 * 3 * 2 * half * sources * shards * 2 * half * 128
+    return pl.pallas_call(
+        functools.partial(attend_kernel, sources, place.lanes),
+        out_shape=(
+            jax.ShapeDtypeStruct(q.shape, BF16),
+            jax.ShapeDtypeStruct((shards, 1, 6 * half), F32),
+        ),
+        in_specs=[pl.BlockSpec(memory_space=pltpu.SMEM)] + [vmem] * (2 + sources),
+        out_specs=(vmem, vmem),
+        scratch_shapes=[pltpu.VMEM((sources, shards, lanes, 2 * half), BF16)],
+        compiler_params=pltpu.CompilerParams(vmem_limit_bytes=40 * 1024 * 1024),
+        cost_estimate=pl.CostEstimate(flops=work, bytes_accessed=4 * 2**20, transcendentals=6 * 2**20),
+    )(info, limit, q, *kvs)
+
+
+def attend_back_kernel(sources, lanes, info, limit_ref, lse_ref, q_ref, out_ref, grad_ref, *refs):
+    kv_refs = refs[:sources]
+    dq_ref, dkv_refs, (turned, total) = refs[sources], refs[sources + 1 : -2], refs[-2:]
+    shards, half, _ = q_ref.shape
+    rows = 2 * half
+    for s in range(sources):
+        for z in range(shards):
+            turned[s, z] = kv_refs[s][z].astype(F32).T.astype(BF16)
+    total[...] = jnp.zeros_like(total)
+
+    def shard(z, carry):
+        pair, single = unpack(q_ref[z], True)
+        grad_pair, grad_single = unpack(grad_ref[z], False)
+        limit, lse = limit_ref[z], lse_ref[z]
+        product = (grad_ref[z].astype(F32) * out_ref[z].astype(F32)).T
+        sums = [
+            jnp.sum(product[i * HEAD_DIM : (i + 1) * HEAD_DIM], axis=0, keepdims=True)
+            for i in range(6)
+        ]
+        delta = jnp.concatenate([sums[0], sums[2], sums[1], sums[3], sums[4], sums[5]], axis=1)
+
+        def step(kz, state):
+            dq_pair, dq_single = state
+            for s in range(sources):
+                keep = visible_keys(kz, info[shards + s], lanes, rows, limit)
+                keep = jnp.concatenate([keep] * 3, axis=1)
+                kv = kv_refs[s]
+                k01, v01, kv2 = kv[kz, :, 0:128], kv[kz, :, 128:256], kv[kz, :, 256:384]
+                scores = jnp.concatenate([nt(k01, pair), nt(kv2, single)], axis=1)
+                grads = jnp.concatenate([nt(v01, grad_pair), nt(kv2, grad_single)], axis=1)
+                power = jnp.where(keep, jnp.exp(scores - lse), 0.0)
+                slope = (power * (grads - delta)).astype(BF16)
+                power = power.astype(BF16)
+                dq_pair = dq_pair + nn(turned[s, kz, 0:128, :], slope[:, : 2 * rows])
+                dq_single = dq_single + nn(turned[s, kz, 256:384, :], slope[:, 2 * rows :])
+                total[s, kz, :, 0:128] += nn(slope[:, : 2 * rows], pair)
+                total[s, kz, :, 128:256] += nn(power[:, : 2 * rows], grad_pair)
+                total[s, kz, :, 256:384] += nn(slope[:, 2 * rows :], single) + nn(
+                    power[:, 2 * rows :], grad_single
+                )
+            return dq_pair, dq_single
+
+        dq_pair, dq_single = lax.fori_loop(
+            0,
+            info[z],
+            step,
+            (jnp.zeros((128, 2 * rows), F32), jnp.zeros((128, rows), F32)),
+        )
+        first, second = dq_pair[:HEAD_DIM, :rows], dq_pair[HEAD_DIM:, rows:]
+        third = dq_single[:HEAD_DIM]
+        packed = jnp.concatenate(
+            [a[:, part] for part in (slice(0, half), slice(half, rows)) for a in (first, second)]
+            + [third[:, :half], third[:, half:]],
+            axis=0,
+        )
+        dq_ref[z] = packed.T.astype(BF16)
+        return carry
+
+    lax.fori_loop(0, shards, shard, 0)
+    for s in range(sources):
+        dkv_refs[s][...] = total[s].astype(BF16)
+
+
+def attend_back(place, info, limit, lse, q, out, grad, kvs):
+    shards, half, lanes = q.shape
+    vmem = pl.BlockSpec(memory_space=pltpu.VMEM)
+    sources = len(kvs)
+    work = 2 * 8 * 3 * 2 * half * sources * shards * 2 * half * 128
+    return pl.pallas_call(
+        functools.partial(attend_back_kernel, sources, place.lanes),
+        out_shape=(jax.ShapeDtypeStruct(q.shape, BF16),)
+        + (jax.ShapeDtypeStruct(kvs[0].shape, BF16),) * sources,
+        in_specs=[pl.BlockSpec(memory_space=pltpu.SMEM)] + [vmem] * (5 + sources),
+        out_specs=(vmem,) * (1 + sources),
+        scratch_shapes=[
+            pltpu.VMEM((sources, shards, lanes, 2 * half), BF16),
+            pltpu.VMEM((sources, shards, 2 * half, lanes), F32),
+        ],
+        compiler_params=pltpu.CompilerParams(vmem_limit_bytes=52 * 1024 * 1024),
+        cost_estimate=pl.CostEstimate(flops=work, bytes_accessed=6 * 2**20, transcendentals=6 * 2**20),
+    )(info, limit, lse, q, out, grad, *kvs)
+
+
+def finish_kernel(
+    dq_ref, dkv_ref, w_ref, cos_ref, sin_ref, x_ref, gain_ref, middle_ref,
+    projected_ref, input_ref, norm_ref, gather,
+):
+    groups, half, _ = dq_ref.shape
+    rows, width = x_ref.shape
+    three = 3 * HEAD_DIM
+    for g in range(groups):
+        at = g * three
+        dq, dkv = dq_ref[g].astype(F32), dkv_ref[g].astype(F32)
+        gather[0, :half, at : at + 128] = dq[:, 0:128]
+        gather[0, half:, at : at + 128] = dq[:, 128:256]
+        gather[0, :half, at + 128 : at + three] = dq[:, 256:320]
+        gather[0, half:, at + 128 : at + three] = dq[:, 320:384]
+        gather[1, :, at : at + 128] = dkv[:, 0:128]
+        gather[1, :, at + 128 : at + three] = dkv[:, 256:320]
+        gather[2, :, at : at + 128] = dkv[:, 128:256]
+        gather[2, :, at + 128 : at + three] = dkv[:, 320:384]
+    cosine, sine = cos_ref[...], -sin_ref[...]
+    parts = [
+        (turn(gather[0], cosine, sine) * HEAD_DIM**-0.5).astype(BF16),
+        turn(gather[1], cosine, sine).astype(BF16),
+        gather[2].astype(BF16),
+    ]
+    grad = jnp.zeros((rows, width), F32)
+    for i, part in enumerate(parts):
+        projected_ref[:, i * width : (i + 1) * width] = part
+        grad = grad + nt(part, w_ref[:, i * width : (i + 1) * width])
+    x = x_ref[...].astype(F32)
+    scale = rms_scale(x)
+    norm_ref[...] = jnp.sum(grad * x * scale, axis=0, keepdims=True)
+    input_ref[...] = middle_ref[...] + rms_back(x, scale, gain_ref[...], grad)
+
+
+def finish(dq, dkv, weight, cosine, sine, x, gain, middle):
+    rows, width = x.shape
+    vmem = pl.BlockSpec(memory_space=pltpu.VMEM)
+    return pl.pallas_call(
+        finish_kernel,
+        out_shape=(
+            jax.ShapeDtypeStruct((rows, 3 * width), BF16),
+            jax.ShapeDtypeStruct((rows, width), F32),
+            jax.ShapeDtypeStruct((1, width), F32),
+        ),
+        in_specs=[vmem] * 8,
+        out_specs=(vmem,) * 3,
+        scratch_shapes=[pltpu.VMEM((3, rows, width), F32)],
+        compiler_params=pltpu.CompilerParams(vmem_limit_bytes=40 * 1024 * 1024),
+        cost_estimate=pl.CostEstimate(
+            flops=6 * rows * width * width, bytes_accessed=10 * width * width, transcendentals=0
+        ),
+    )(dq, dkv, weight, cosine, sine, x, gain[None], middle)
+
+
+def heads_to_rows(packed):
+    groups, half, _ = packed.shape
+    pair = jnp.concatenate([packed[:, :, 0:128], packed[:, :, 128:256]], axis=1)
+    single = jnp.concatenate([packed[:, :, 256:320], packed[:, :, 320:384]], axis=1)
+    joined = jnp.concatenate([pair, single], axis=2)
+    return joined.transpose(1, 0, 2).reshape(2 * half, groups * 3 * HEAD_DIM)
+
+
+def rows_to_heads(rows, groups):
+    count = rows.shape[0]
+    half = count // 2
+    split = rows.reshape(count, groups, 3 * HEAD_DIM).transpose(1, 0, 2)
+    return jnp.concatenate(
+        [split[:, :half, :128], split[:, half:, :128], split[:, :half, 128:], split[:, half:, 128:]],
+        axis=2,
+    )
+
+
+def trade_heads(a):
+    return lax.all_to_all(a, "g", split_axis=0, concat_axis=0, tiled=True)
 
 
 def ffn_kernel(shared, dp, experts, table, x_ref, dy_ref, gate_ref, up_ref, down_ref, *refs):
@@ -416,70 +742,32 @@
     length = row_count * place.dp
     positions = shard_index * row_count + jnp.arange(row_count, dtype=jnp.int32)
     bounds = jnp.cumsum(block_lengths[0])
-    query_ids = block_ids(bounds, positions)
-    key_ids = block_ids(bounds, jnp.arange(length, dtype=jnp.int32))
-    cosine, sine_table = rope_table(positions)
-    head_shape = (row_count, HEADS, HEAD_DIM)
-    scale_one = rms_scale(hidden)
-    normalized_rows = (hidden * scale_one * norm_attn).astype(BF16)
-    projected_rows = jnp.dot(
-        normalized_rows, query_key_value_weight, preferred_element_type=F32
-    )
-    queries = (
-        rotate(projected_rows[:, :model_width].reshape(head_shape), cosine, sine_table, 1.0)
-        * HEAD_DIM ** (-0.5)
-    ).astype(BF16)
-    key_heads = rotate(
-        projected_rows[:, model_width : 2 * model_width].reshape(head_shape),
-        cosine,
-        sine_table,
-        1.0,
-    ).astype(BF16)
-    values = projected_rows[:, 2 * model_width :].reshape(head_shape).astype(BF16)
-    all_keys, all_values = (
-        lax.all_gather(key_heads.reshape(row_count, model_width), DP, axis=0, tiled=True),
-        lax.all_gather(values.reshape(row_count, model_width), DP, axis=0, tiled=True),
-    )
+    cosine, sine = rope_table(positions)
+    normalized_rows, own_q, own_kv = project(
+        place, tokens[0], norm_attn, query_key_value_weight, cosine, sine
+    )
+    kv = trade_heads(own_kv)
+    q = trade_heads(own_q)
+    if place.lanes == 2:
+        kvs = [kv, swap(kv, "r")]
+        lanes_of = [place.r, 1 - place.r]
+    else:
+        every_kv = lax.all_gather(kv, "r", axis=0, tiled=False)
+        kvs = [every_kv[i] for i in range(place.lanes)]
+        lanes_of = [jnp.int32(i) for i in range(place.lanes)]
+    starts = (jnp.arange(place.groups, dtype=jnp.int32) * place.lanes + place.r) * row_count
+    query_places = starts[:, None] + jnp.arange(row_count, dtype=jnp.int32)[None, :]
+    limit = jnp.min(
+        jnp.where(bounds[None, None, :] > query_places[:, :, None], bounds, length), axis=-1
+    )
+    span = row_count * place.lanes
+    info = jnp.concatenate([(jnp.max(limit, axis=1) + span - 1) // span, jnp.stack(lanes_of)])
+    info = info.astype(jnp.int32)
+    limit = limit[:, None, :]
     expert_in = jnp.transpose(expert_in, (1, 0, 2))
     expert_out = jnp.transpose(expert_out, (1, 0, 2))
-    key_span = min(512, length)
-    blocks = length // key_span
-    key_blocks = all_keys.reshape(blocks, key_span, HEADS, HEAD_DIM)
-    value_blocks = all_values.reshape(blocks, key_span, HEADS, HEAD_DIM)
-    id_blocks = key_ids.reshape(blocks, key_span)
-
-    def stat_step(running, inputs):
-        largest, row_total = running
-        key_block, id_block = inputs
-        scores, visible = masked_scores(queries, key_block, query_ids, id_block)
-        newest = jnp.maximum(largest, jnp.max(scores, axis=-1))
-        row_total = row_total * jnp.exp(largest - newest) + jnp.sum(
-            jnp.where(visible[None], jnp.exp(scores - newest[:, :, None]), 0.0), axis=-1
-        )
-        return ((newest, row_total), None)
-
-    start_max = jnp.full((HEADS, row_count), NEG, F32)
-    (largest, row_total), _ = lax.scan(
-        stat_step, (start_max, jnp.zeros((HEADS, row_count), F32)), (key_blocks, id_blocks)
-    )
-    log_total = (largest + jnp.log(row_total)).T
-
-    def out_step(running, inputs):
-        key_block, value_block, id_block = inputs
-        scores, visible = masked_scores(queries, key_block, query_ids, id_block)
-        weights_low = jnp.where(
-            visible[None], jnp.exp(scores - log_total.T[:, :, None]), 0.0
-        ).astype(BF16)
-        return (
-            running
-            + jnp.einsum("hqk,khd->qhd", weights_low, value_block, preferred_element_type=F32),
-            None,
-        )
-
-    attention_result, _ = lax.scan(
-        out_step, jnp.zeros(head_shape, F32), (key_blocks, value_blocks, id_blocks)
-    )
-    attended_low = attention_result.reshape(row_count, model_width).astype(BF16)
+    own_out, lse = attend(place, info, limit, q, kvs)
+    attended_low = heads_to_rows(trade_heads(own_out))
     residual_between = hidden + jnp.dot(
         attended_low, attention_output_weight, preferred_element_type=F32
     )
@@ -581,64 +869,26 @@
     grad_norm_ffn = jnp.sum(grad_mixed * residual_between * scale_two, axis=0)
     grad_middle = grad_upper + rms_back(residual_between, scale_two, norm_ffn, grad_mixed)
     grad_attn_low = grad_middle.astype(BF16)
-    grad_attended = (
-        jnp.einsum(
-            "te,de->td", grad_attn_low, attention_output_weight, preferred_element_type=F32
-        )
-        .astype(BF16)
-        .reshape(head_shape)
-    )
-    row_delta = jnp.sum(grad_attended.astype(F32) * attention_result, axis=-1)
-
-    def back_step(grad_queries, inputs):
-        key_block, value_block, id_block = inputs
-        weights_low, grad_scores = score_grads(
-            queries,
-            grad_attended,
-            log_total,
-            row_delta,
-            key_block,
-            value_block,
-            query_ids,
-            id_block,
-        )
-        grad_queries = grad_queries + jnp.einsum(
-            "hqk,khd->qhd", grad_scores, key_block, preferred_element_type=F32
-        )
-        grad_key_part = jnp.einsum(
-            "hqk,qhd->khd", grad_scores, queries, preferred_element_type=F32
-        ).reshape(key_span, model_width)
-        grad_value_part = jnp.einsum(
-            "hqk,qhd->khd", weights_low, grad_attended, preferred_element_type=F32
-        ).reshape(key_span, model_width)
-        return (grad_queries, jnp.concatenate([grad_key_part, grad_value_part], axis=1))
-
-    grad_queries, key_terms = lax.scan(
-        back_step, jnp.zeros(head_shape, F32), (key_blocks, value_blocks, id_blocks)
-    )
-    own_terms = lax.psum_scatter(
-        key_terms.reshape(length, 2 * model_width).astype(BF16),
-        DP,
-        scatter_dimension=0,
-        tiled=True,
-    ).astype(F32)
-    grad_keys = own_terms[:, :model_width].reshape(head_shape)
-    grad_values = own_terms[:, model_width:].reshape(head_shape)
-    grad_queries = rotate(grad_queries * HEAD_DIM ** (-0.5), cosine, sine_table, -1.0)
-    grad_keys = rotate(grad_keys, cosine, sine_table, -1.0)
-    grad_projected = jnp.concatenate(
-        [
-            grad_queries.reshape(row_count, model_width),
-            grad_keys.reshape(row_count, model_width),
-            grad_values.reshape(row_count, model_width),
-        ],
-        axis=1,
+    grad_attended = jnp.einsum(
+        "te,de->td", grad_attn_low, attention_output_weight, preferred_element_type=F32
     ).astype(BF16)
-    grad_normed = jnp.einsum(
-        "te,de->td", grad_projected, query_key_value_weight, preferred_element_type=F32
-    )
-    grad_norm_attn = jnp.sum(grad_normed * hidden * scale_one, axis=0)
-    grad_input = grad_middle + rms_back(hidden, scale_one, norm_attn, grad_normed)
+    own_grad = trade_heads(rows_to_heads(grad_attended, place.groups))
+    own_dq, *own_dkv = attend_back(place, info, limit, lse, q, own_out, own_grad, kvs)
+    if place.lanes == 2:
+        dkv = add(own_dkv[0], swap(own_dkv[1], "r"))
+    else:
+        dkv = scatter(jnp.stack(own_dkv), "r", 0)[0]
+    grad_projected, grad_input, grad_norm_attn = finish(
+        trade_heads(own_dq),
+        trade_heads(dkv),
+        query_key_value_weight,
+        cosine,
+        sine,
+        tokens[0],
+        norm_attn,
+        grad_middle,
+    )
+    grad_norm_attn = grad_norm_attn[0]
     sum_qkv = weight_grad(place, to_flat(place, normalized_rows), grad_projected)
     sum_out = weight_grad(place, to_flat(place, attended_low), grad_attn_low)
     small = jnp.concatenate([grad_norm_ffn[:, None], grad_router], axis=1)

time: 1000 us -> 709 us (0.71)
  waiting for transfers between devices: 391 us -> 266 us
  local copies, waits for them, and re-layouts: 185 us -> 82.4 us
  matrix products: 112 us -> 16.6 us
  other arithmetic: 141 us -> 78.4 us
  Pallas kernels: 52.5 us -> 91.8 us
  starting transfers between devices: 53.3 us -> 86.2 us
  blocking collectives: 45 us -> 76 us
  between operations: 15.6 us -> 2.67 us
    ppermute x32 -> x34, waiting for transfers between devices: 343 us -> 217 us  [swap(): return lax.ppermute(a, axis, [(i, i ^ bit) for i in range(size)])]
    dot_general x30 -> x0, matrix products: 94.3 us -> none  [the longest x8 31.6 us: masked_scores(): jnp.einsum('qhd,khd->hqk', queries, key_heads, preferred_element_type=F32)]
    pallas_call x0 -> x4, Pallas kernels: none -> 39.2 us  [the longest x1 18.7 us: attend_back(): pl.pallas_call(functools.partial(attend_back_kernel, sources, place.lanes...]
    all_to_all x0 -> x6, waiting for transfers between devices: none -> 36.4 us  [trade_heads(): return lax.all_to_all(a, 'g', split_axis=0, concat_axis=0, tiled=True)]
    all_gather x2 -> x0, waiting for transfers between devices: 36.2 us -> none  [the longest x1 35.5 us: local(): lax.all_gather(key_heads.reshape(row_count, model_width), DP, axis=0, til...]
    psum x1, blocking collectives: 45 us -> 76 us  [local(): lax.psum(grad_norm_attn, DP + EX)]
    all_to_all x0 -> x6, starting transfers between devices: none -> 25.9 us  [trade_heads(): return lax.all_to_all(a, 'g', split_axis=0, concat_axis=0, tiled=True)]
    reduce_sum x8 -> x0, other arithmetic: 22.2 us -> none  [the longest x4 16.3 us: stat_step(): jnp.sum(jnp.where(visible[None], jnp.exp(scores - newest[:, :, None]), 0....]
  transfers between devices with their start and end apart: 39 -> 44, of which waited for: 16 -> 16; matrix products, arithmetic and copies ran while one was open for 25% -> 21% of each run, Pallas kernels for 4% -> 8%
where the time goes in v2:
time: 709 us; the launch traced here: 700 us
  waiting for transfers between devices  266 us (38%)
  Pallas kernels  91.8 us (13%)
  starting transfers between devices  86.2 us (12%)
  local copies, waits for them, and re-layouts  82.4 us (12%)
  other arithmetic  78.4 us (11%)
  blocking collectives  76 us (11%)
  matrix products  16.6 us (2%)
    ppermute x34, waiting for transfers between devices, swap(): return lax.ppermute(a, axis, [(i, i ^ bit) for i in range(size)])  217 us
    psum x1, blocking collectives, local(): lax.psum(grad_norm_attn, DP + EX)  76 us
    convert_element_type x25, other arithmetic, add(): return (a.astype(F32) + b.astype(F32)).astype(kind)  58.8 us
    pallas_call x3, Pallas kernels, ffn(): pl.pallas_call(functools.partial(ffn_kernel, shared, place.dp, place.expe...  52.6 us
    unnamed x176, local copies, waits for them, and re-layouts  52 us
    ppermute x34, starting transfers between devices, swap(): return lax.ppermute(a, axis, [(i, i ^ bit) for i in range(size)])  43.4 us
    all_to_all x6, waiting for transfers between devices, trade_heads(): return lax.all_to_all(a, 'g', split_axis=0, concat_axis=0, tiled=True)  36.4 us
    all_to_all x6, starting transfers between devices, trade_heads(): return lax.all_to_all(a, 'g', split_axis=0, concat_axis=0, tiled=True)  25.9 us
  transfers between devices with their start and end apart: 44, of which 16 were waited for; matrix products, arithmetic and copies ran while one was open for 21% of the time, Pallas kernels for 8%

profile of v2, /device:TPU:0, one launch (start us, length us, event | category | flops | bytes accessed | tf_op | source)
XLA Modules:
  0.0 699.9 jit_solution(4312360791641951137)
XLA Ops:
  5.1 4.6 shard_map.212
  10.5 6.4 all-to-all-start.1
  17.0 20.1 %all-to-all-done.1.refs_0_ = bf16[4,256,384]{2,1,0:T(8,128)(2,1)S(1)} async-done(((bf16[4,256,384]{2,1,0:T(8,128)(2,1)}), bf16[4,256,384]{2,1,0:T(8,128)(2,1)S(1)}, u32[]{:S(2)}, u32[]{:S(2)}) %all-to-all-start.1) | async-done | bytes 786464 | tf_op jit(solution)/shard_map/all_to_all | solution.py:466
  37.1 3.5 all-to-all-start
  43.1 8.7 %all-to-all-done.q_ref = bf16[4,128,384]{2,1,0:T(8,128)(2,1)S(1)} async-done(((bf16[4,128,384]{2,1,0:T(8,128)(2,1)}), bf16[4,128,384]{2,1,0:T(8,128)(2,1)S(1)}, u32[]{:S(2)}, u32[]{:S(2)}) %all-to-all-start) | async-done | bytes 393248 | tf_op jit(solution)/shard_map/all_to_all | solution.py:466
  51.7 7.4 %collective-permute-done.refs_1_ = bf16[4,256,384]{2,1,0:T(8,128)(2,1)S(1)} collective-permute-done((bf16[4,256,384]{2,1,0:T(8,128)(2,1)S(1)}, bf16[4,256,384]{2,1,0:T(8,128)(2,1)S(1)}, u32[]{:S(2)}, u32[]{:S(2)}) %collective-permute-start) | collective-permute-done | bytes 786464 | tf_op jit(solution)/shard_map/ppermute | solution.py:617
  59.1 11.7 %shard_map.213 = (bf16[4,128,384]{2,1,0:T(8,128)(2,1)}, f32[4,1,768]{2,1,0:T(1,128)S(1)}) custom-call(s32[6]{0:T(128)S(1)} %pad_add_fusion.info, s32[4,1,256]{2,1,0:T(1,128)S(1)} %broadcast_in_dim.33.limit_ref, bf16[4,128,384]{2,1,0:T(8,128)(2,1)S(1)} %all-to-all-done.q_ref, bf16[4,256,384]{2,1,0:T(8,128)(2,1)S(1)} %all-to-all-done.1.refs_0_, ...), custom_call_target="tpu_custom_call" | custom-call | flops 1610612736 | bytes 4194304 | tf_op jit(solution)/shard_map/pallas_call | solution.py:296
  70.9 4.7 all-to-all-start.2
  77.7 7.6 %all-to-all-done.2 = bf16[4,128,384]{2,1,0:T(8,128)(2,1)S(1)} async-done(((bf16[4,128,384]{2,1,0:T(8,128)(2,1)}), bf16[4,128,384]{2,1,0:T(8,128)(2,1)S(1)}, u32[]{:S(2)}, u32[]{:S(2)}) %all-to-all-start.2) | async-done | bytes 393248 | tf_op jit(solution)/shard_map/all_to_all | solution.py:466
  90.1 3.5 all-to-all-start.4
  95.2 12.1 %all-to-all-done.4 = bf16[2,4,80,768]{3,2,0,1:T(8,128)(2,1)S(1)} async-done(((bf16[2,4,80,768]{3,2,0,1:T(8,128)(2,1)}), bf16[2,4,80,768]{3,2,0,1:T(8,128)(2,1)S(1)}, u32[]{:S(2)}, u32[]{:S(2)}) %all-to-all-start.4) | async-done | bytes 983072 | tf_op jit(solution)/shard_map/all_to_all | solution.py:805
  107.3 4.5 all-to-all-start.3
  111.8 14.5 %copy.113 = bf16[768,2,4096]{2,0,1:T(8,128)(2,1)} copy(bf16[768,2,4096]{2,1,0:T(2,128)(2,1)} %param.19) | data formatting | bytes 25165824 | tf_op args[6]
  126.3 6.2 copy.114
  135.6 17.3 %shard_map.215 = (bf16[320,1536]{1,0:T(8,128)(2,1)S(1)}, bf16[2,384,2048]{2,1,0:T(8,128)(2,1)}, bf16[2,384,2048]{2,1,0:T(8,128)(2,1)}, bf16[1024,768]{1,0:T(8,128)(2,1)S(1)}, bf16[1024,768]{1,0:T(8,128)(2,1)S(1)}) custom-call(s32[24]{0:T(128)S(1)} %stack.156.table, bf16[320,768]{1,0:T(8,128)(2,1)S(1)} %bitcast.142, bf16[320,768]{1,0:T(8,128)(2,1)S(1)} %bitcast.141, ...), custom_call_target="tpu_custom_call" | custom-call | flops 9059696640 | bytes 18874368 | tf_op jit(solution)/shard_map/pallas_call | solution.py:589
  155.1 4.2 all-to-all-start.6
  161.4 17.4 %shard_map.214 = (bf16[320,1536]{1,0:T(8,128)(2,1)S(1)}, bf16[2,384,2048]{2,1,0:T(8,128)(2,1)}, bf16[2,384,2048]{2,1,0:T(8,128)(2,1)}, bf16[1024,768]{1,0:T(8,128)(2,1)S(1)}, bf16[1024,768]{1,0:T(8,128)(2,1)}) custom-call(s32[24]{0:T(128)S(1)} %stack.156.table, bf16[320,768]{1,0:T(8,128)(2,1)S(1)} %bitcast.140, bf16[320,768]{1,0:T(8,128)(2,1)S(1)} %bitcast.139, ...), custom_call_target="tpu_custom_call" | custom-call | flops 9059696640 | bytes 18874368 | tf_op jit(solution)/shard_map/pallas_call | solution.py:589
  180.9 4.6 all-to-all-start.5
  186.2 17.9 %shard_map.216 = (f32[256,768]{1,0:T(8,128)S(1)}, f32[256,768]{1,0:T(8,128)S(1)}, bf16[2,768,1024]{2,1,0:T(8,128)(2,1)}, bf16[2,768,1024]{2,1,0:T(8,128)(2,1)}, ...) custom-call(s32[28]{0:T(128)S(1)} %stack.177.table, bf16[256,768]{1,0:T(8,128)(2,1)S(1)} %multiply_convert_fusion.1.x_ref, ...), custom_call_target="tpu_custom_call" | custom-call | flops 7247757312 | bytes 18874368 | tf_op jit(solution)/shard_map/pallas_call | solution.py:589
  208.3 4.2 collective-permute-start.18
  216.2 2.7 fusion.7
  229.0 3.7 add_convert_fusion.9
  237.6 3.5 all-to-all-start.7
  241.0 18.2 %collective-permute-done.8 = bf16[768,192]{0,1:T(8,128)(2,1)S(1)} collective-permute-done((bf16[768,192]{0,1:T(8,128)(2,1)}, bf16[768,192]{0,1:T(8,128)(2,1)S(1)}, u32[]{:S(2)}, u32[]{:S(2)}) %collective-permute-start.8) | collective-permute-done | bytes 294944 | tf_op jit(solution)/shard_map/ppermute | solution.py:617
  267.8 18.7 %shard_map.217 = (bf16[4,128,384]{2,1,0:T(8,128)(2,1)}, bf16[4,256,384]{2,1,0:T(8,128)(2,1)}, bf16[4,256,384]{2,1,0:T(8,128)(2,1)}) custom-call(s32[6]{0:T(128)S(1)} %pad_add_fusion.info, s32[4,1,256]{2,1,0:T(1,128)S(1)} %broadcast_in_dim.33.limit_ref, f32[4,1,768]{2,1,0:T(1,128)S(1)} %copy-done.35, bf16[4,128,384]{2,1,0:T(8,128)(2,1)S(1)} %copy-done.29, ...), custom_call_target="tpu_custom_call" | custom-call | flops 3221225472 | bytes 6291456 | tf_op jit(solution)/shard_map/pallas_call | solution.py:378
  286.5 6.3 collective-permute-start.1
  293.8 82.8 %collective-permute-done.31 = bf16[192,1024]{1,0:T(8,128)(2,1)} collective-permute-done((bf16[192,1024]{1,0:T(8,128)(2,1)}, bf16[192,1024]{1,0:T(8,128)(2,1)}, u32[]{:S(2)}, u32[]{:S(2)}) %collective-permute-start.31) | collective-permute-done | bytes 393248 | tf_op jit(solution)/shard_map/ppermute | solution.py:617
  377.4 3.6 all-to-all-start.8
  381.1 3.5 add_convert_fusion.13
  386.4 7.0 %collective-permute-done.1 = bf16[4,256,384]{2,1,0:T(8,128)(2,1)} collective-permute-done((bf16[4,256,384]{2,1,0:T(8,128)(2,1)}, bf16[4,256,384]{2,1,0:T(8,128)(2,1)}, u32[]{:S(2)}, u32[]{:S(2)}) %collective-permute-start.1) | collective-permute-done | bytes 786464 | tf_op jit(solution)/shard_map/ppermute | solution.py:617
  395.7 3.4 collective-permute-done.32
  399.2 4.2 all-to-all-start.9
  407.9 2.9 add_convert_fusion.11
  410.8 21.8 %collective-permute-done.33 = bf16[192,256]{1,0:T(8,128)(2,1)S(1)} collective-permute-done((bf16[192,256]{1,0:T(8,128)(2,1)S(1)}, bf16[192,256]{1,0:T(8,128)(2,1)S(1)}, u32[]{:S(2)}, u32[]{:S(2)}) %collective-permute-start.33) | collective-permute-done | bytes 98336 | tf_op jit(solution)/shard_map/ppermute | solution.py:617
  432.6 6.8 collective-permute-start.22
  441.6 6.3 add_convert_fusion.1
  451.1 6.9 collective-permute-done.22
  464.8 4.2 shard_map.218
  474.6 2.9 collective-permute-done.20
  478.8 4.7 add_convert_fusion.5
  483.5 4.5 add_convert_fusion.3
  490.0 3.3 fusion.2
  498.3 76.0 %all-reduce = (f32[768]{0:T(1024)S(1)}, f32[768,9]{0,1:T(8,128)}) all-reduce(f32[768]{0:T(1024)S(1)} %reduce.4, f32[768,9]{0,1:T(8,128)} %pad_maximum_fusion.5), channel_id=1, replica_groups=mesh['g'=4,'r'=2,'y'=2,'c'=2] {'g','r','y','c'}, use_global_device_ids=true, to_apply=%region_17.18 | all-reduce | flops 7680 | bytes 61440 | tf_op jit(solution)/shard_map/psum | solution.py:902
  581.0 4.8 add_convert_fusion.7
  602.4 53.5 %collective-permute-done.28 = bf16[96,1024]{1,0:T(8,128)(2,1)S(1)} collective-permute-done((bf16[96,1024]{1,0:T(8,128)(2,1)S(1)}, bf16[96,1024]{1,0:T(8,128)(2,1)S(1)}, u32[]{:S(2)}, u32[]{:S(2)}) %collective-permute-start.28) | collective-permute-done | bytes 196640 | tf_op jit(solution)/shard_map/ppermute | solution.py:617
  667.0 10.6 %collective-permute-done.4 = bf16[384,576]{1,0:T(8,128)(2,1)S(1)} collective-permute-done((bf16[384,576]{1,0:T(8,128)(2,1)S(1)}, bf16[384,576]{1,0:T(8,128)(2,1)S(1)}, u32[]{:S(2)}, u32[]{:S(2)}) %collective-permute-start.4) | collective-permute-done | bytes 442400 | tf_op jit(solution)/shard_map/ppermute | solution.py:617
  678.4 2.9 add_bitcast_fusion
  693.5 4.1 copy.106
  (348 shorter events, 142.2 us)
Async XLA Ops:
  0.6 85.2 %copy-start = (bf16[768,768]{1,0:T(8,128)(2,1)S(1)}, bf16[768,768]{1,0:T(8,128)(2,1)}, u32[]{:S(2)}) copy-start(bf16[768,768]{1,0:T(8,128)(2,1)} %param.16) | copy-start | bytes 3538948
  10.5 32.1 %copy-start.66 = (s32[1,256,2]{1,2,0:T(2,128)S(1)}, s32[1,256,2]{1,2,0:T(2,128)}, u32[]{:S(2)}) copy-start(s32[1,256,2]{1,2,0:T(2,128)} %param.24) | copy-start | bytes 6148
  10.5 26.6 %all-to-all-start.1 = ((bf16[4,256,384]{2,1,0:T(8,128)(2,1)}), bf16[4,256,384]{2,1,0:T(8,128)(2,1)S(1)}, u32[]{:S(2)}, u32[]{:S(2)}) async-start(bf16[4,256,384]{2,1,0:T(8,128)(2,1)} %get-tuple-element.39), calls=%async_computation.1 | async-start | bytes 1572864 | tf_op jit(solution)/shard_map/all_to_all | solution.py:466
  37.1 33.8 %copy-start.19 = (bf16[4,256,384]{2,1,0:T(8,128)(2,1)}, bf16[4,256,384]{2,1,0:T(8,128)(2,1)S(1)}, u32[]{:S(2)}) copy-start(bf16[4,256,384]{2,1,0:T(8,128)(2,1)S(1)} %all-to-all-done.1.refs_0_) | copy-start | bytes 2359300
  37.1 14.6 %all-to-all-start = ((bf16[4,128,384]{2,1,0:T(8,128)(2,1)}), bf16[4,128,384]{2,1,0:T(8,128)(2,1)S(1)}, u32[]{:S(2)}, u32[]{:S(2)}) async-start(bf16[4,128,384]{2,1,0:T(8,128)(2,1)} %get-tuple-element.38), calls=%async_computation | async-start | bytes 786432 | tf_op jit(solution)/shard_map/all_to_all | solution.py:466
  40.6 18.6 %collective-permute-start = (bf16[4,256,384]{2,1,0:T(8,128)(2,1)S(1)}, bf16[4,256,384]{2,1,0:T(8,128)(2,1)S(1)}, u32[]{:S(2)}, u32[]{:S(2)}) collective-permute-start(bf16[4,256,384]{2,1,0:T(8,128)(2,1)S(1)} %all-to-all-done.1.refs_0_), channel_id=1, source_target_pairs={{0,4},{4,0},{1,5},{5,1},{2,6},{6,2},{3,7},{7,3},{8,12},{12,8},{9,1... | collective-permute-start | bytes 2359304 | tf_op jit(solution)/shard_map/ppermute | solution.py:617
  70.9 14.4 %all-to-all-start.2 = ((bf16[4,128,384]{2,1,0:T(8,128)(2,1)}), bf16[4,128,384]{2,1,0:T(8,128)(2,1)S(1)}, u32[]{:S(2)}, u32[]{:S(2)}) async-start(bf16[4,128,384]{2,1,0:T(8,128)(2,1)} %get-tuple-element.40.out_ref), calls=%async_computation.2 | async-start | bytes 786432 | tf_op jit(solution)/shard_map/all_to_all | solution.py:466
  90.1 17.3 %all-to-all-start.4 = ((bf16[2,4,80,768]{3,2,0,1:T(8,128)(2,1)}), bf16[2,4,80,768]{3,2,0,1:T(8,128)(2,1)S(1)}, u32[]{:S(2)}, u32[]{:S(2)}) async-start(bf16[2,4,80,768]{3,2,0,1:T(8,128)(2,1)} %copy.88), calls=%async_computation.4 | async-start | bytes 1966080 | tf_op jit(solution)/shard_map/all_to_all | solution.py:805
  107.3 26.2 %all-to-all-start.3 = ((bf16[2,4,80,768]{3,2,0,1:T(8,128)(2,1)}), bf16[2,4,80,768]{3,2,0,1:T(8,128)(2,1)}, u32[]{:S(2)}, u32[]{:S(2)}) async-start(bf16[2,4,80,768]{3,2,0,1:T(8,128)(2,1)} %copy.87), calls=%async_computation.3 | async-start | bytes 1966080 | tf_op jit(solution)/shard_map/all_to_all | solution.py:805
  155.1 25.9 %all-to-all-start.6 = ((bf16[4,80,1536]{2,1,0:T(8,128)(2,1)}), bf16[4,80,1536]{2,1,0:T(8,128)(2,1)}, u32[]{:S(2)}, u32[]{:S(2)}) async-start(bf16[4,80,1536]{2,1,0:T(8,128)(2,1)} %bitcast.138), calls=%async_computation.6 | async-start | bytes 1966080 | tf_op jit(solution)/shard_map/all_to_all | solution.py:840
  180.9 31.6 %all-to-all-start.5 = ((bf16[4,80,1536]{2,1,0:T(8,128)(2,1)}), bf16[4,80,1536]{2,1,0:T(8,128)(2,1)}, u32[]{:S(2)}, u32[]{:S(2)}) async-start(bf16[4,80,1536]{2,1,0:T(8,128)(2,1)} %bitcast.137), calls=%async_computation.5 | async-start | bytes 1966080 | tf_op jit(solution)/shard_map/all_to_all | solution.py:840
  207.0 22.0 %collective-permute-start.29 = (bf16[384,2048]{1,0:T(8,128)(2,1)}, bf16[384,2048]{1,0:T(8,128)(2,1)}, u32[]{:S(2)}, u32[]{:S(2)}) collective-permute-start(bf16[384,2048]{1,0:T(8,128)(2,1)} %get-tuple-element.64), channel_id=1, source_target_pairs={{0,1},{1,0},{2,3},{3,2},{4,5},{5,4},{6,7},{7,6},{8,9},{9,8},{10,11... | collective-permute-start | bytes 4718600 | tf_op jit(solution)/shard_map/ppermute | solution.py:617
  207.5 234.1 %collective-permute-start.24 = (bf16[2,768,1024]{2,1,0:T(8,128)(2,1)}, bf16[2,768,1024]{2,1,0:T(8,128)(2,1)}, u32[]{:S(2)}, u32[]{:S(2)}) collective-permute-start(bf16[2,768,1024]{2,1,0:T(8,128)(2,1)} %get-tuple-element.62), channel_id=1, source_target_pairs={{0,1},{1,0},{2,3},{3,2},{4,5},{5,4},{6,7},{7,6},{8,9},{9,8},{10,11... | collective-permute-start | bytes 9437192 | tf_op jit(solution)/shard_map/ppermute | solution.py:617
  208.3 59.5 %collective-permute-start.18 = (bf16[1024,768]{1,0:T(8,128)(2,1)}, bf16[1024,768]{1,0:T(8,128)(2,1)}, u32[]{:S(2)}, u32[]{:S(2)}) collective-permute-start(bf16[1024,768]{1,0:T(8,128)(2,1)} %get-tuple-element.58), channel_id=1, source_target_pairs={{0,4},{4,0},{1,5},{5,1},{2,6},{6,2},{3,7},{7,3},{8,12},{12,8},{9,1... | collective-permute-start | bytes 4718600 | tf_op jit(solution)/shard_map/ppermute | solution.py:617
  225.8 8.8 %collective-permute-start.7 = (bf16[768,384]{0,1:T(8,128)(2,1)}, bf16[768,384]{0,1:T(8,128)(2,1)}, u32[]{:S(2)}, u32[]{:S(2)}) collective-permute-start(bf16[768,384]{0,1:T(8,128)(2,1)} %convolution_convert_fusion.3), channel_id=1, source_target_pairs={{0,1},{1,0},{2,3},{3,2},{4,5},{5,4},{6,7},{7,6},{8,9},{9,8},{10,11... | collective-permute-start | bytes 1769480 | tf_op jit(solution)/shard_map/ppermute | solution.py:617
  232.7 29.3 %collective-permute-start.30 = (bf16[192,2048]{1,0:T(8,128)(2,1)}, bf16[192,2048]{1,0:T(8,128)(2,1)}, u32[]{:S(2)}, u32[]{:S(2)}) collective-permute-start(bf16[192,2048]{1,0:T(8,128)(2,1)} %get-tuple-element.130), channel_id=1, source_target_pairs={{0,2},{2,0},{1,3},{3,1},{4,6},{6,4},{5,7},{7,5},{8,10},{10,8},{9,1... | collective-permute-start | bytes 2359304 | tf_op jit(solution)/shard_map/ppermute | solution.py:617
  236.5 22.8 %collective-permute-start.8 = (bf16[768,192]{0,1:T(8,128)(2,1)}, bf16[768,192]{0,1:T(8,128)(2,1)S(1)}, u32[]{:S(2)}, u32[]{:S(2)}) collective-permute-start(bf16[768,192]{0,1:T(8,128)(2,1)} %get-tuple-element.143), channel_id=1, source_target_pairs={{0,2},{2,0},{1,3},{3,1},{4,6},{6,4},{5,7},{7,5},{8,10},{10,8},{9,1... | collective-permute-start | bytes 884744 | tf_op jit(solution)/shard_map/ppermute | solution.py:617
  237.6 30.2 %all-to-all-start.7 = ((bf16[4,128,384]{2,1,0:T(8,128)(2,1)}), bf16[4,128,384]{2,1,0:T(8,128)(2,1)S(1)}, u32[]{:S(2)}, u32[]{:S(2)}) async-start(bf16[4,128,384]{2,1,0:T(8,128)(2,1)} %pad_maximum_fusion.4), calls=%async_computation.7 | async-start | bytes 786432 | tf_op jit(solution)/shard_map/all_to_all | solution.py:466
  260.0 6.9 collective-permute-start.9
  260.0 143.4 %collective-permute-start.21 = (bf16[1024,768]{1,0:T(8,128)(2,1)}, bf16[1024,768]{1,0:T(8,128)(2,1)}, u32[]{:S(2)}, u32[]{:S(2)}) collective-permute-start(bf16[1024,768]{1,0:T(8,128)(2,1)} %copy-done.30), channel_id=1, source_target_pairs={{0,4},{4,0},{1,5},{5,1},{2,6},{6,2},{3,7},{7,3},{8,12},{12,8},{9,1... | collective-permute-start | bytes 4718600 | tf_op jit(solution)/shard_map/ppermute | solution.py:617
  262.1 216.7 %collective-permute-start.12 = (bf16[2,384,2048]{2,1,0:T(8,128)(2,1)}, bf16[2,384,2048]{2,1,0:T(8,128)(2,1)}, u32[]{:S(2)}, u32[]{:S(2)}) collective-permute-start(bf16[2,384,2048]{2,1,0:T(8,128)(2,1)} %get-tuple-element.54), channel_id=1, source_target_pairs={{0,4},{4,0},{1,5},{5,1},{2,6},{6,2},{3,7},{7,3},{8,12},{12,8},{9,1... | collective-permute-start | bytes 9437192 | tf_op jit(solution)/shard_map/ppermute | solution.py:617
  267.0 109.7 %collective-permute-start.31 = (bf16[192,1024]{1,0:T(8,128)(2,1)}, bf16[192,1024]{1,0:T(8,128)(2,1)}, u32[]{:S(2)}, u32[]{:S(2)}) collective-permute-start(bf16[192,1024]{1,0:T(8,128)(2,1)} %get-tuple-element.138), channel_id=1, source_target_pairs={{0,4},{4,0},{1,5},{5,1},{2,6},{6,2},{3,7},{7,3},{8,12},{12,8},{9,1... | collective-permute-start | bytes 1179656 | tf_op jit(solution)/shard_map/ppermute | solution.py:617
  267.8 18.7 %collective-permute-start.10 = (bf16[192,192]{0,1:T(8,128)(2,1)S(1)}, bf16[192,192]{0,1:T(8,128)(2,1)S(1)}, u32[]{:S(2)}, u32[]{:S(2)}) collective-permute-start(bf16[192,192]{0,1:T(8,128)(2,1)S(1)} %get-tuple-element.171), channel_id=1, source_target_pairs={{0,8},{8,0},{16,24},{24,16},{1,9},{9,1},{17,25},{25,17},{2,10},{10... | collective-permute-start | bytes 221192 | tf_op jit(solution)/shard_map/ppermute | solution.py:617
  286.5 107.0 %collective-permute-start.1 = (bf16[4,256,384]{2,1,0:T(8,128)(2,1)}, bf16[4,256,384]{2,1,0:T(8,128)(2,1)}, u32[]{:S(2)}, u32[]{:S(2)}) collective-permute-start(bf16[4,256,384]{2,1,0:T(8,128)(2,1)} %get-tuple-element.48), channel_id=1, source_target_pairs={{0,4},{4,0},{1,5},{5,1},{2,6},{6,2},{3,7},{7,3},{8,12},{12,8},{9,1... | collective-permute-start | bytes 2359304 | tf_op jit(solution)/shard_map/ppermute | solution.py:617
  376.6 106.8 %collective-permute-start.15 = (bf16[2,384,2048]{2,1,0:T(8,128)(2,1)}, bf16[2,384,2048]{2,1,0:T(8,128)(2,1)}, u32[]{:S(2)}, u32[]{:S(2)}) collective-permute-start(bf16[2,384,2048]{2,1,0:T(8,128)(2,1)} %get-tuple-element.56), channel_id=1, source_target_pairs={{0,4},{4,0},{1,5},{5,1},{2,6},{6,2},{3,7},{7,3},{8,12},{12,8},{9,1... | collective-permute-start | bytes 9437192 | tf_op jit(solution)/shard_map/ppermute | solution.py:617
  377.4 21.7 %all-to-all-start.8 = ((bf16[4,128,384]{2,1,0:T(8,128)(2,1)}), bf16[4,128,384]{2,1,0:T(8,128)(2,1)S(1)}, u32[]{:S(2)}, u32[]{:S(2)}) async-start(bf16[4,128,384]{2,1,0:T(8,128)(2,1)} %get-tuple-element.46), calls=%async_computation.8 | async-start | bytes 786432 | tf_op jit(solution)/shard_map/all_to_all | solution.py:466
  393.5 5.7 collective-permute-start.32
  399.1 6.3 collective-permute-start.11
  399.2 60.7 %all-to-all-start.9 = ((bf16[4,256,384]{2,1,0:T(8,128)(2,1)}), bf16[4,256,384]{2,1,0:T(8,128)(2,1)}, u32[]{:S(2)}, u32[]{:S(2)}) async-start(bf16[4,256,384]{2,1,0:T(8,128)(2,1)} %add_convert_fusion.18), calls=%async_computation.9 | async-start | bytes 1572864 | tf_op jit(solution)/shard_map/all_to_all | solution.py:466
  403.4 45.8 %collective-permute-start.19 = (bf16[512,768]{1,0:T(8,128)(2,1)}, bf16[512,768]{1,0:T(8,128)(2,1)}, u32[]{:S(2)}, u32[]{:S(2)}) collective-permute-start(bf16[512,768]{1,0:T(8,128)(2,1)} %get-tuple-element.134), channel_id=1, source_target_pairs={{0,8},{8,0},{16,24},{24,16},{1,9},{9,1},{17,25},{25,17},{2,10},{10... | collective-permute-start | bytes 2359304 | tf_op jit(solution)/shard_map/ppermute | solution.py:617
  405.5 27.1 %collective-permute-start.33 = (bf16[192,256]{1,0:T(8,128)(2,1)S(1)}, bf16[192,256]{1,0:T(8,128)(2,1)S(1)}, u32[]{:S(2)}, u32[]{:S(2)}) collective-permute-start(bf16[192,256]{1,0:T(8,128)(2,1)S(1)} %add_convert_fusion.42), channel_id=1, source_target_pairs={{0,16},{8,24},{16,0},{24,8},{1,17},{9,25},{17,1},{25,9},{2,18},{10... | collective-permute-start | bytes 294920 | tf_op jit(solution)/shard_map/ppermute | solution.py:617
  407.8 32.2 %copy-start.57 = (bf16[192,192]{0,1:T(8,128)(2,1)S(1)}, bf16[192,192]{0,1:T(8,128)(2,1)}, u32[]{:S(2)}) copy-start(bf16[192,192]{0,1:T(8,128)(2,1)} %copy-done.55) | copy-start | bytes 221188
  432.6 25.3 %collective-permute-start.22 = (bf16[512,768]{1,0:T(8,128)(2,1)}, bf16[512,768]{1,0:T(8,128)(2,1)}, u32[]{:S(2)}, u32[]{:S(2)}) collective-permute-start(bf16[512,768]{1,0:T(8,128)(2,1)} %get-tuple-element.136), channel_id=1, source_target_pairs={{0,8},{8,0},{16,24},{24,16},{1,9},{9,1},{17,25},{25,17},{2,10},{10... | collective-permute-start | bytes 2359304 | tf_op jit(solution)/shard_map/ppermute | solution.py:617
  447.9 42.1 %collective-permute-start.25 = (bf16[768,1024]{1,0:T(8,128)(2,1)}, bf16[768,1024]{1,0:T(8,128)(2,1)}, u32[]{:S(2)}, u32[]{:S(2)}) collective-permute-start(bf16[768,1024]{1,0:T(8,128)(2,1)} %get-tuple-element.122), channel_id=1, source_target_pairs={{0,2},{2,0},{1,3},{3,1},{4,6},{6,4},{5,7},{7,5},{8,10},{10,8},{9,1... | collective-permute-start | bytes 4718600 | tf_op jit(solution)/shard_map/ppermute | solution.py:617
  451.1 26.4 %collective-permute-start.20 = (bf16[256,768]{1,0:T(8,128)(2,1)}, bf16[256,768]{1,0:T(8,128)(2,1)}, u32[]{:S(2)}, u32[]{:S(2)}) collective-permute-start(bf16[256,768]{1,0:T(8,128)(2,1)} %add_convert_fusion.27), channel_id=1, source_target_pairs={{0,16},{8,24},{16,0},{24,8},{1,17},{9,25},{17,1},{25,9},{2,18},{10... | collective-permute-start | bytes 1179656 | tf_op jit(solution)/shard_map/ppermute | solution.py:617
  459.8 34.7 %collective-permute-start.23 = (bf16[256,768]{1,0:T(8,128)(2,1)}, bf16[256,768]{1,0:T(8,128)(2,1)}, u32[]{:S(2)}, u32[]{:S(2)}) collective-permute-start(bf16[256,768]{1,0:T(8,128)(2,1)} %add_convert_fusion.25), channel_id=1, source_target_pairs={{0,16},{8,24},{16,0},{24,8},{1,17},{9,25},{17,1},{25,9},{2,18},{10... | collective-permute-start | bytes 1179656 | tf_op jit(solution)/shard_map/ppermute | solution.py:617
  477.5 103.5 %collective-permute-start.2 = (bf16[768,1152]{1,0:T(8,128)(2,1)}, bf16[768,1152]{1,0:T(8,128)(2,1)}, u32[]{:S(2)}, u32[]{:S(2)}) collective-permute-start(bf16[768,1152]{1,0:T(8,128)(2,1)} %convolution_convert_fusion), channel_id=1, source_target_pairs={{0,1},{1,0},{2,3},{3,2},{4,5},{5,4},{6,7},{7,6},{8,9},{9,8},{10,11... | collective-permute-start | bytes 5308424 | tf_op jit(solution)/shard_map/ppermute | solution.py:617
  483.5 108.7 %collective-permute-start.13 = (bf16[2,192,2048]{2,1,0:T(8,128)(2,1)}, bf16[2,192,2048]{2,1,0:T(8,128)(2,1)}, u32[]{:S(2)}, u32[]{:S(2)}) collective-permute-start(bf16[2,192,2048]{2,1,0:T(8,128)(2,1)} %get-tuple-element.124), channel_id=1, source_target_pairs={{0,8},{8,0},{16,24},{24,16},{1,9},{9,1},{17,25},{25,17},{2,10},{10... | collective-permute-start | bytes 4718600 | tf_op jit(solution)/shard_map/ppermute | solution.py:617
  488.0 110.5 %collective-permute-start.16 = (bf16[2,192,2048]{2,1,0:T(8,128)(2,1)}, bf16[2,192,2048]{2,1,0:T(8,128)(2,1)}, u32[]{:S(2)}, u32[]{:S(2)}) collective-permute-start(bf16[2,192,2048]{2,1,0:T(8,128)(2,1)} %get-tuple-element.126), channel_id=1, source_target_pairs={{0,8},{8,0},{16,24},{24,16},{1,9},{9,1},{17,25},{25,17},{2,10},{10... | collective-permute-start | bytes 4718600 | tf_op jit(solution)/shard_map/ppermute | solution.py:617
  493.3 84.3 %collective-permute-start.26 = (bf16[384,1024]{1,0:T(8,128)(2,1)}, bf16[384,1024]{1,0:T(8,128)(2,1)}, u32[]{:S(2)}, u32[]{:S(2)}) collective-permute-start(bf16[384,1024]{1,0:T(8,128)(2,1)} %get-tuple-element.132), channel_id=1, source_target_pairs={{0,4},{4,0},{1,5},{5,1},{2,6},{6,2},{3,7},{7,3},{8,12},{12,8},{9,1... | collective-permute-start | bytes 2359304 | tf_op jit(solution)/shard_map/ppermute | solution.py:617
  579.7 16.4 %collective-permute-start.27 = (bf16[192,1024]{1,0:T(8,128)(2,1)}, bf16[192,1024]{1,0:T(8,128)(2,1)}, u32[]{:S(2)}, u32[]{:S(2)}) collective-permute-start(bf16[192,1024]{1,0:T(8,128)(2,1)} %get-tuple-element.140), channel_id=1, source_target_pairs={{0,8},{8,0},{16,24},{24,16},{1,9},{9,1},{17,25},{25,17},{2,10},{10... | collective-permute-start | bytes 1179656 | tf_op jit(solution)/shard_map/ppermute | solution.py:617
  588.0 69.6 %collective-permute-start.3 = (bf16[768,576]{0,1:T(8,128)(2,1)}, bf16[768,576]{0,1:T(8,128)(2,1)S(1)}, u32[]{:S(2)}, u32[]{:S(2)}) collective-permute-start(bf16[768,576]{0,1:T(8,128)(2,1)} %copy.96), channel_id=1, source_target_pairs={{0,2},{2,0},{1,3},{3,1},{4,6},{6,4},{5,7},{7,5},{8,10},{10,8},{9,1... | collective-permute-start | bytes 2654216 | tf_op jit(solution)/shard_map/ppermute | solution.py:617
  594.5 70.8 %collective-permute-start.14 = (bf16[2,96,2048]{2,1,0:T(8,128)(2,1)}, bf16[2,96,2048]{2,1,0:T(8,128)(2,1)}, u32[]{:S(2)}, u32[]{:S(2)}) collective-permute-start(bf16[2,96,2048]{2,1,0:T(8,128)(2,1)} %add_convert_fusion.16), channel_id=1, source_target_pairs={{0,16},{8,24},{16,0},{24,8},{1,17},{9,25},{17,1},{25,9},{2,18},{10... | collective-permute-start | bytes 2359304 | tf_op jit(solution)/shard_map/ppermute | solution.py:617
  597.1 58.8 %collective-permute-start.28 = (bf16[96,1024]{1,0:T(8,128)(2,1)S(1)}, bf16[96,1024]{1,0:T(8,128)(2,1)S(1)}, u32[]{:S(2)}, u32[]{:S(2)}) collective-permute-start(bf16[96,1024]{1,0:T(8,128)(2,1)S(1)} %add_convert_fusion.36), channel_id=1, source_target_pairs={{0,16},{8,24},{16,0},{24,8},{1,17},{9,25},{17,1},{25,9},{2,18},{10... | collective-permute-start | bytes 589832 | tf_op jit(solution)/shard_map/ppermute | solution.py:617
  600.7 77.7 %collective-permute-start.17 = (bf16[2,96,2048]{2,1,0:T(8,128)(2,1)}, bf16[2,96,2048]{2,1,0:T(8,128)(2,1)}, u32[]{:S(2)}, u32[]{:S(2)}) collective-permute-start(bf16[2,96,2048]{2,1,0:T(8,128)(2,1)} %add_convert_fusion.14), channel_id=1, source_target_pairs={{0,16},{8,24},{16,0},{24,8},{1,17},{9,25},{17,1},{25,9},{2,18},{10... | collective-permute-start | bytes 2359304 | tf_op jit(solution)/shard_map/ppermute | solution.py:617
  664.5 13.1 %collective-permute-start.4 = (bf16[384,576]{1,0:T(8,128)(2,1)S(1)}, bf16[384,576]{1,0:T(8,128)(2,1)S(1)}, u32[]{:S(2)}, u32[]{:S(2)}) collective-permute-start(bf16[384,576]{1,0:T(8,128)(2,1)S(1)} %get-tuple-element.149), channel_id=1, source_target_pairs={{0,4},{4,0},{1,5},{5,1},{2,6},{6,2},{3,7},{7,3},{8,12},{12,8},{9,1... | collective-permute-start | bytes 1327112 | tf_op jit(solution)/shard_map/ppermute | solution.py:617
  678.4 10.6 %collective-permute-start.5 = (bf16[192,576]{1,0:T(8,128)(2,1)}, bf16[192,576]{1,0:T(8,128)(2,1)}, u32[]{:S(2)}, u32[]{:S(2)}) collective-permute-start(bf16[192,576]{1,0:T(8,128)(2,1)} %get-tuple-element.147), channel_id=1, source_target_pairs={{0,8},{8,0},{16,24},{24,16},{1,9},{9,1},{17,25},{25,17},{2,10},{10... | collective-permute-start | bytes 663560 | tf_op jit(solution)/shard_map/ppermute | solution.py:617
  689.9 7.9 %collective-permute-start.6 = (bf16[96,576]{1,0:T(8,128)(2,1)S(1)}, bf16[96,576]{1,0:T(8,128)(2,1)S(1)}, u32[]{:S(2)}, u32[]{:S(2)}) collective-permute-start(bf16[96,576]{1,0:T(8,128)(2,1)S(1)} %add_convert_fusion.40), channel_id=1, source_target_pairs={{0,16},{8,24},{16,0},{24,8},{1,17},{9,25},{17,1},{25,9},{2,18},{10... | collective-permute-start | bytes 331784 | tf_op jit(solution)/shard_map/ppermute | solution.py:617
  (80 other events, 435.0 us)

commit v3 on v2

v3 whole, which is shorter than its diff:
```python
import functools

import jax
import jax.numpy as jnp
from jax import lax
from jax.experimental import pallas as pl
from jax.experimental.pallas import tpu as pltpu
from jax.sharding import Mesh
from jax.sharding import PartitionSpec as P

HEADS = 12
HEAD_DIM = 64
TOP = 2
EPS = 1e-06
NEG = -1e30
F32 = jnp.float32
BF16 = jnp.bfloat16
STEPS = 8
DP = ("g", "r")
EX = ("y", "c")
LEADS = ("g", "r")
SMALL = pl.CostEstimate(flops=1024, bytes_accessed=1024, transcendentals=0)


def rope_table(positions):
    lane = jnp.arange(2 * HEAD_DIM, dtype=jnp.int32) % HEAD_DIM
    half_dim = HEAD_DIM // 2
    frequency = 10000.0 ** (-(lane % half_dim).astype(F32) * 2.0 / HEAD_DIM)
    angles = positions.astype(F32)[:, None] * frequency[None, :]
    return jnp.cos(angles), jnp.sin(angles) * jnp.where(lane < half_dim, -1.0, 1.0)


def rms_scale(hidden):
    return lax.rsqrt(jnp.mean(hidden * hidden, axis=-1, keepdims=True) + EPS)


def rms_back(hidden, scale_rows, gain_vector, upstream):
    normed_grad = upstream * gain_vector
    inner_mean = jnp.mean(normed_grad * hidden, axis=-1, keepdims=True)
    return scale_rows * normed_grad - hidden * scale_rows**3 * inner_mean


class Place:
    def __init__(self):
        self.groups, self.lanes = lax.axis_size("g"), lax.axis_size("r")
        self.rows_y = lax.axis_size("y")
        self.dp = self.groups * self.lanes
        self.experts = self.rows_y * 2
        self.g, self.r = lax.axis_index("g"), lax.axis_index("r")
        self.y, self.c = lax.axis_index("y"), lax.axis_index("c")
        self.low, self.high = self.g % 2, self.g // 2

    def own(self, b):
        g, r = b // self.lanes, b % self.lanes
        low, high = g % 2, g // 2
        if self.lanes == 2:
            return r ^ self.r, low * 2 + high
        return low ^ self.low, high * self.lanes + r

    def flat(self, b):
        g, r = b // self.lanes, b % self.lanes
        if self.lanes == 2:
            return r * 4 + (g % 2) * 2 + g // 2
        return (g % 2 * 2 + g // 2) * self.lanes + r

    def expert_table(self, width, lead):
        sub = STEPS // 4
        order = []
        for pos in range(STEPS):
            half, rest = pos // 4, pos % 4
            if self.lanes == 2 and lead == "r":
                low, high, part = rest // 2, rest % 2, half ^ self.r
            elif self.lanes == 2:
                low, high, part = half ^ self.low, rest % 2, rest // 2
            else:
                low, high, part = half ^ self.low, rest // 2, rest % 2
            order.append((high * 2 + low) * sub + part)
        block = width // self.dp
        rows = []
        for b in range(self.dp):
            half, rest = self.own(b)
            rows.append(half * (width // 2) + rest * block)
        return jnp.stack([jnp.asarray(v, jnp.int32) for v in order + [0] * STEPS + rows])

    def shared_table(self, width):
        per = 16 // self.experts
        order, columns = [], []
        sub = STEPS // 4
        for pos in range(STEPS):
            half, rest = pos // 4, pos % 4
            j = (rest // per * 2 + (half ^ self.c)) * per + rest % per
            order.append(j)
            g, part = j // sub, j % sub
            if self.lanes == 2:
                columns.append(part * 4 + g % 2 * 2 + g // 2)
            else:
                columns.append((g % 2 * 2 + g // 2) * sub + part)
        block = width // self.dp
        rows = [self.flat(b) * block for b in range(self.dp)]
        own = width // self.experts
        turned = [
            (e % 2 ^ self.c) * (width // 2) + e // 2 * own for e in range(self.experts)
        ]
        return jnp.stack(
            [jnp.asarray(v, jnp.int32) for v in order + columns + rows + turned]
        )


def nt(a, b):
    return lax.dot_general(a, b, (((1,), (1,)), ((), ())), preferred_element_type=F32)


def nn(a, b):
    return lax.dot_general(a, b, (((1,), (0,)), ((), ())), preferred_element_type=F32)


def turn(x, cosine, sine):
    width = x.shape[1]
    lane = lax.broadcasted_iota(jnp.int32, x.shape, 1) % HEAD_DIM
    other = jnp.where(
        lane < HEAD_DIM // 2,
        pltpu.roll(x, width - HEAD_DIM // 2, 1),
        pltpu.roll(x, HEAD_DIM // 2, 1),
    )
    times = width // cosine.shape[1]
    cosine = jnp.concatenate([cosine] * times, axis=1)
    sine = jnp.concatenate([sine] * times, axis=1)
    return x * cosine + other * sine


def project_kernel(here, x_ref, gain_ref, w_ref, cos_ref, sin_ref, normed_ref, *refs):
    step = pl.program_id(0)
    groups = (len(refs) - 2) // 2
    q_refs, kv_refs, (q_all, kv_all) = refs[:groups], refs[groups:-2], refs[-2:]
    half, three = x_ref.shape[0] // 2, 3 * HEAD_DIM

    @pl.when(step == 0)
    def _():
        x = x_ref[...].astype(F32)
        normed_ref[...] = (x * rms_scale(x) * gain_ref[...]).astype(BF16)

    part = nn(normed_ref[...], w_ref[...])

    @pl.when(step == 0)
    def _():
        pack_heads(turn(part, cos_ref[...], sin_ref[...]) * HEAD_DIM**-0.5, q_all)

    @pl.when(step == 1)
    def _():
        k = turn(part, cos_ref[...], sin_ref[...])
        for g in range(groups):
            own = k[:, g * three : (g + 1) * three].astype(BF16)
            kv_all[g, :, 0:128] = own[:, :128]
            kv_all[g, :, 256:320] = own[:, 128:]

    @pl.when(step == 2)
    def _():
        for g in range(groups):
            own = part[:, g * three : (g + 1) * three].astype(BF16)
            kv_all[g, :, 128:256] = own[:, :128]
            kv_all[g, :, 320:384] = own[:, 128:]
        for d in range(groups):
            q_refs[d][...] = q_all[here[0] ^ d]
            kv_refs[d][...] = kv_all[here[0] ^ d]


def pack_heads(rows, packed_ref):
    half, three = rows.shape[0] // 2, 3 * HEAD_DIM
    for g in range(packed_ref.shape[0]):
        own = rows[:, g * three : (g + 1) * three].astype(BF16)
        packed_ref[g, :, 0:128] = own[:half, :128]
        packed_ref[g, :, 128:256] = own[half:, :128]
        packed_ref[g, :, 256:320] = own[:half, 128:]
        packed_ref[g, :, 320:384] = own[half:, 128:]


def project(place, x, gain, weight, cosine, sine):
    rows, width = x.shape
    groups = place.groups
    sds = jax.ShapeDtypeStruct
    whole = lambda *shape: pl.BlockSpec(shape, lambda i, t: (0,) * len(shape))
    normed, *parts = pl.pallas_call(
        project_kernel,
        out_shape=(sds((rows, width), BF16),)
        + (sds((rows // 2, 384), BF16),) * groups
        + (sds((rows, 384), BF16),) * groups,
        grid_spec=pltpu.PrefetchScalarGridSpec(
            num_scalar_prefetch=1,
            grid=(3,),
            in_specs=[
                whole(rows, width),
                whole(1, width),
                pl.BlockSpec((width, width), lambda i, t: (0, i)),
                whole(rows, 128),
                whole(rows, 128),
            ],
            out_specs=(whole(rows, width),)
            + (whole(rows // 2, 384),) * groups
            + (whole(rows, 384),) * groups,
            scratch_shapes=[
                pltpu.VMEM((groups, rows // 2, 384), BF16),
                pltpu.VMEM((groups, rows, 384), BF16),
            ],
        ),
        compiler_params=pltpu.CompilerParams(vmem_limit_bytes=32 * 1024 * 1024),
        cost_estimate=SMALL,
    )(place.g[None], x, gain[None], weight, cosine, sine)
    return normed, parts[:groups], parts[groups:]


def unpack(packed, second_low):
    half = packed.shape[0]
    x = packed.astype(F32)
    lane = lax.broadcasted_iota(jnp.int32, (half, 128), 1)
    low = lane < HEAD_DIM
    first, second, third = x[:, 0:128], x[:, 128:256], x[:, 256:384]
    turned = pltpu.roll(third, HEAD_DIM, 1)
    zero = jnp.zeros_like(third)
    pair = [
        jnp.where(low, first, zero),
        jnp.where(low, second, zero),
        jnp.where(low, zero, first),
        jnp.where(low, zero, second),
    ]
    if second_low:
        single = [jnp.where(low, third, zero), jnp.where(low, turned, zero)]
    else:
        single = [jnp.where(low, zero, turned), jnp.where(low, zero, third)]
    return (
        jnp.concatenate(pair, axis=0).astype(BF16),
        jnp.concatenate(single, axis=0).astype(BF16),
    )


def visible_keys(kz, source, lanes, rows, limit):
    first = (kz * lanes + source) * rows
    place = first + lax.broadcasted_iota(jnp.int32, (rows, limit.shape[1]), 0)
    return place < limit


def attend_kernel(sources, shards, lanes, info, limit_ref, *refs):
    q_refs, kv_refs = refs[:shards], refs[shards : shards * (1 + sources)]
    out_refs, (lse_ref, q_ref, kv_all, turned, out_ref) = refs[shards * (1 + sources) : -5], refs[-5:]
    half = q_ref.shape[1]
    rows = 2 * half
    gather_heads(info, q_refs, q_ref)
    gather_keys(info, shards, kv_refs, kv_all, turned)

    def shard(z, carry):
        pair, single = unpack(q_ref[z], True)
        limit = limit_ref[z]

        def step(kz, state):
            largest, total, acc_pair, acc_single = state
            scores = []
            for s in range(sources):
                keep = visible_keys(kz, info[1 + shards + s], lanes, rows, limit)
                two = nt(kv_all[s, kz, :, 0:128], pair)
                one = nt(kv_all[s, kz, :, 256:384], single)
                both = jnp.concatenate([two, one], axis=1)
                keep = jnp.concatenate([keep] * 3, axis=1)
                scores.append(jnp.where(keep, both, NEG))
            newest = largest
            for sc in scores:
                newest = jnp.maximum(newest, jnp.max(sc, axis=0, keepdims=True))
            fade = jnp.exp(largest - newest)
            total = total * fade
            acc_pair = acc_pair * fade[:, : 2 * rows]
            acc_single = acc_single * fade[:, 2 * rows :]
            for s, sc in enumerate(scores):
                power = jnp.exp(sc - newest)
                total = total + jnp.sum(power, axis=0, keepdims=True)
                power = power.astype(BF16)
                acc_pair = acc_pair + nn(turned[s, kz, 128:256, :], power[:, : 2 * rows])
                acc_single = acc_single + nn(turned[s, kz, 256:384, :], power[:, 2 * rows :])
            return newest, total, acc_pair, acc_single

        largest, total, acc_pair, acc_single = lax.fori_loop(
            0,
            info[1 + z],
            step,
            (
                jnp.full((1, 3 * rows), NEG, F32),
                jnp.zeros((1, 3 * rows), F32),
                jnp.zeros((128, 2 * rows), F32),
                jnp.zeros((128, rows), F32),
            ),
        )
        lse_ref[z] = largest + jnp.log(total)
        share = 1.0 / total
        first = acc_pair[:HEAD_DIM, :rows] * share[:, :rows]
        second = acc_pair[HEAD_DIM:, rows:] * share[:, rows : 2 * rows]
        third = acc_single[HEAD_DIM:] * share[:, 2 * rows :]
        packed = jnp.concatenate(
            [a[:, part] for part in (slice(0, half), slice(half, rows)) for a in (first, second)]
            + [third[:, :half], third[:, half:]],
            axis=0,
        )
        out_ref[z] = packed.T.astype(BF16)
        return carry

    lax.fori_loop(0, shards, shard, 0)


    for d in range(shards):
        out_refs[d][...] = out_ref[info[0] ^ d]


def gather_heads(info, refs, packed_ref):
    for d, ref in enumerate(refs):
        packed_ref[info[0] ^ d] = ref[...]


def gather_keys(info, shards, refs, kv_all, turned):
    for i, ref in enumerate(refs):
        at = info[0] ^ (i % shards)
        kv_all[i // shards, at] = ref[...]
        turned[i // shards, at] = ref[...].astype(F32).T.astype(BF16)


def attend(place, info, limit, qs, kvs):
    half, lanes = qs[0].shape
    shards, sources = len(qs), len(kvs) // len(qs)
    vmem = pl.BlockSpec(memory_space=pltpu.VMEM)
    sds = jax.ShapeDtypeStruct
    *outs, lse = pl.pallas_call(
        functools.partial(attend_kernel, sources, shards, place.lanes),
        out_shape=(sds((half, lanes), BF16),) * shards + (sds((shards, 1, 6 * half), F32),),
        in_specs=[pl.BlockSpec(memory_space=pltpu.SMEM)] + [vmem] * (1 + shards * (1 + sources)),
        out_specs=(vmem,) * (shards + 1),
        scratch_shapes=[
            pltpu.VMEM((shards, half, lanes), BF16),
            pltpu.VMEM((sources, shards, 2 * half, lanes), BF16),
            pltpu.VMEM((sources, shards, lanes, 2 * half), BF16),
            pltpu.VMEM((shards, half, lanes), BF16),
        ],
        compiler_params=pltpu.CompilerParams(vmem_limit_bytes=48 * 1024 * 1024),
        cost_estimate=SMALL,
    )(info, limit, *qs, *kvs)
    return outs, lse


def attend_back_kernel(sources, shards, lanes, info, limit_ref, lse_ref, *refs):
    q_refs, o_refs, g_refs = (refs[i * shards : (i + 1) * shards] for i in range(3))
    kv_refs = refs[3 * shards : (3 + sources) * shards]
    dq_refs = refs[(3 + sources) * shards : (4 + sources) * shards]
    dkv_refs = refs[(4 + sources) * shards : (4 + 2 * sources) * shards]
    q_ref, out_ref, grad_ref, dq_ref, kv_all, turned, total = refs[-7:]
    half = q_ref.shape[1]
    rows = 2 * half
    gather_heads(info, q_refs, q_ref)
    gather_heads(info, o_refs, out_ref)
    gather_heads(info, g_refs, grad_ref)
    gather_keys(info, shards, kv_refs, kv_all, turned)
    total[...] = jnp.zeros_like(total)

    def shard(z, carry):
        pair, single = unpack(q_ref[z], True)
        grad_pair, grad_single = unpack(grad_ref[z], False)
        limit, lse = limit_ref[z], lse_ref[z]
        product = (grad_ref[z].astype(F32) * out_ref[z].astype(F32)).T
        sums = [
            jnp.sum(product[i * HEAD_DIM : (i + 1) * HEAD_DIM], axis=0, keepdims=True)
            for i in range(6)
        ]
        delta = jnp.concatenate([sums[0], sums[2], sums[1], sums[3], sums[4], sums[5]], axis=1)

        def step(kz, state):
            dq_pair, dq_single = state
            for s in range(sources):
                keep = visible_keys(kz, info[1 + shards + s], lanes, rows, limit)
                keep = jnp.concatenate([keep] * 3, axis=1)
                k01, v01 = kv_all[s, kz, :, 0:128], kv_all[s, kz, :, 128:256]
                kv2 = kv_all[s, kz, :, 256:384]
                scores = jnp.concatenate([nt(k01, pair), nt(kv2, single)], axis=1)
                grads = jnp.concatenate([nt(v01, grad_pair), nt(kv2, grad_single)], axis=1)
                power = jnp.where(keep, jnp.exp(scores - lse), 0.0)
                slope = (power * (grads - delta)).astype(BF16)
                power = power.astype(BF16)
                dq_pair = dq_pair + nn(turned[s, kz, 0:128, :], slope[:, : 2 * rows])
                dq_single = dq_single + nn(turned[s, kz, 256:384, :], slope[:, 2 * rows :])
                total[s, kz, :, 0:128] += nn(slope[:, : 2 * rows], pair)
                total[s, kz, :, 128:256] += nn(power[:, : 2 * rows], grad_pair)
                total[s, kz, :, 256:384] += nn(slope[:, 2 * rows :], single) + nn(
                    power[:, 2 * rows :], grad_single
                )
            return dq_pair, dq_single

        dq_pair, dq_single = lax.fori_loop(
            0,
            info[1 + z],
            step,
            (jnp.zeros((128, 2 * rows), F32), jnp.zeros((128, rows), F32)),
        )
        first, second = dq_pair[:HEAD_DIM, :rows], dq_pair[HEAD_DIM:, rows:]
        third = dq_single[:HEAD_DIM]
        packed = jnp.concatenate(
            [a[:, part] for part in (slice(0, half), slice(half, rows)) for a in (first, second)]
            + [third[:, :half], third[:, half:]],
            axis=0,
        )
        dq_ref[z] = packed.T.astype(BF16)
        return carry

    lax.fori_loop(0, shards, shard, 0)
    for d in range(shards):
        dq_refs[d][...] = dq_ref[info[0] ^ d]
    for i, ref in enumerate(dkv_refs):
        ref[...] = total[i // shards, info[0] ^ (i % shards)].astype(BF16)


def attend_back(place, info, limit, lse, qs, outs, grads, kvs):
    half, lanes = qs[0].shape
    shards, sources = len(qs), len(kvs) // len(qs)
    vmem = pl.BlockSpec(memory_space=pltpu.VMEM)
    sds = jax.ShapeDtypeStruct
    parts = pl.pallas_call(
        functools.partial(attend_back_kernel, sources, shards, place.lanes),
        out_shape=(sds((half, lanes), BF16),) * shards
        + (sds((2 * half, lanes), BF16),) * (shards * sources),
        in_specs=[pl.BlockSpec(memory_space=pltpu.SMEM)] + [vmem] * (2 + shards * (3 + sources)),
        out_specs=(vmem,) * (shards * (1 + sources)),
        scratch_shapes=[pltpu.VMEM((shards, half, lanes), BF16)] * 4
        + [
            pltpu.VMEM((sources, shards, 2 * half, lanes), BF16),
            pltpu.VMEM((sources, shards, lanes, 2 * half), BF16),
            pltpu.VMEM((sources, shards, 2 * half, lanes), F32),
        ],
        compiler_params=pltpu.CompilerParams(vmem_limit_bytes=56 * 1024 * 1024),
        cost_estimate=SMALL,
    )(info, limit, lse, *qs, *outs, *grads, *kvs)
    return parts[:shards], [parts[i * shards : (i + 1) * shards] for i in range(1, 1 + sources)]


def finish_kernel(
    here, w_ref, cos_ref, sin_ref, x_ref, gain_ref, middle_ref, *refs,
):
    groups = (len(refs) - 6) // 2
    dq_refs, dkv_refs = refs[:groups], refs[groups : 2 * groups]
    projected_ref, input_ref, norm_ref, dq_all, dkv_all, gather = refs[2 * groups :]
    rows, width = x_ref.shape
    half, three = rows // 2, 3 * HEAD_DIM
    for d in range(groups):
        dq_all[here[0] ^ d] = dq_refs[d][...].astype(F32)
        dkv_all[here[0] ^ d] = dkv_refs[d][...].astype(F32)
    for g in range(groups):
        at = g * three
        dq, dkv = dq_all[g], dkv_all[g]
        gather[0, :half, at : at + 128] = dq[:, 0:128]
        gather[0, half:, at : at + 128] = dq[:, 128:256]
        gather[0, :half, at + 128 : at + three] = dq[:, 256:320]
        gather[0, half:, at + 128 : at + three] = dq[:, 320:384]
        gather[1, :, at : at + 128] = dkv[:, 0:128]
        gather[1, :, at + 128 : at + three] = dkv[:, 256:320]
        gather[2, :, at : at + 128] = dkv[:, 128:256]
        gather[2, :, at + 128 : at + three] = dkv[:, 320:384]
    cosine, sine = cos_ref[...], -sin_ref[...]
    parts = [
        (turn(gather[0], cosine, sine) * HEAD_DIM**-0.5).astype(BF16),
        turn(gather[1], cosine, sine).astype(BF16),
        gather[2].astype(BF16),
    ]
    grad = jnp.zeros((rows, width), F32)
    for i, part in enumerate(parts):
        projected_ref[:, i * width : (i + 1) * width] = part
        grad = grad + nt(part, w_ref[:, i * width : (i + 1) * width])
    x = x_ref[...].astype(F32)
    scale = rms_scale(x)
    norm_ref[...] = jnp.sum(grad * x * scale, axis=0, keepdims=True)
    input_ref[...] = middle_ref[...] + rms_back(x, scale, gain_ref[...], grad)


def finish(place, dqs, dkvs, weight, cosine, sine, x, gain, middle):
    rows, width = x.shape
    groups = place.groups
    vmem = pl.BlockSpec(memory_space=pltpu.VMEM)
    return pl.pallas_call(
        finish_kernel,
        out_shape=(
            jax.ShapeDtypeStruct((rows, 3 * width), BF16),
            jax.ShapeDtypeStruct((rows, width), F32),
            jax.ShapeDtypeStruct((1, width), F32),
        ),
        in_specs=[pl.BlockSpec(memory_space=pltpu.SMEM)] + [vmem] * (6 + 2 * groups),
        out_specs=(vmem,) * 3,
        scratch_shapes=[
            pltpu.VMEM((groups, rows // 2, 384), F32),
            pltpu.VMEM((groups, rows, 384), F32),
            pltpu.VMEM((3, rows, width), F32),
        ],
        compiler_params=pltpu.CompilerParams(vmem_limit_bytes=48 * 1024 * 1024),
        cost_estimate=SMALL,
    )(place.g[None], weight, cosine, sine, x, gain[None], middle, *dqs, *dkvs)


def middle_kernel(
    here, x_ref, grad_ref, w_ref, gain_ref, router_ref, pick0, pick1, seat0, seat1, *refs,
):
    groups = 4
    o_refs = refs[:groups]
    low_ref, middle_ref, mixed_ref, gate_ref = refs[groups : groups + 4]
    sent = refs[groups + 4 : -2]
    o_all, gather = refs[-2:]
    count = len(sent) // 2
    half, three = x_ref.shape[0] // 2, 3 * HEAD_DIM
    for d in range(groups):
        o_all[here[0] ^ d] = o_refs[d][...].astype(F32)
    for g in range(groups):
        at = g * three
        gather[:half, at : at + 128] = o_all[g, :, 0:128]
        gather[half:, at : at + 128] = o_all[g, :, 128:256]
        gather[:half, at + 128 : at + three] = o_all[g, :, 256:320]
        gather[half:, at + 128 : at + three] = o_all[g, :, 320:384]
    low = gather[...].astype(BF16)
    low_ref[...] = low
    middle = x_ref[...].astype(F32) + nn(low, w_ref[...])
    middle_ref[...] = middle
    mixed = (middle * rms_scale(middle) * gain_ref[...]).astype(BF16)
    mixed_ref[...] = mixed
    scores = nn(mixed, router_ref[...])
    picked = [jnp.sum(scores * p[...], axis=1, keepdims=True) for p in (pick0, pick1)]
    largest = jnp.maximum(*picked)
    powers = [jnp.exp(p - largest) for p in picked]
    gates = [p / (powers[0] + powers[1]) for p in powers]
    gate_ref[...] = jnp.concatenate(gates, axis=1)
    seats = (seat0[...], seat1[...])
    held = jnp.zeros((seats[0].shape[0], 1), F32)
    for seat, gate in zip(seats, gates):
        high = gate.astype(BF16)
        rest = (gate - high.astype(F32)).astype(BF16)
        held = held + jnp.sum(nn(seat, jnp.concatenate([high, rest], axis=1)), axis=1, keepdims=True)
    every = seats[0] + seats[1]
    rows = nn(every, mixed).astype(BF16)
    grads = (nn(every, grad_ref[...]) * held).astype(BF16)
    capacity = sent[0].shape[1]
    for d in range(count):
        for e in range(sent[0].shape[0]):
            at = (e * count + d) * capacity
            sent[d][e] = rows[at : at + capacity]
            sent[count + d][e] = grads[at : at + capacity]


def middle_part(place, capacity, outs, x, grad, weight, gain, router, picks, seats):
    rows, width = x.shape
    groups, count = place.groups, place.experts
    local = router.shape[1] // count
    vmem = pl.BlockSpec(memory_space=pltpu.VMEM)
    sds = jax.ShapeDtypeStruct
    low, middle, mixed, gates, *sent = pl.pallas_call(
        middle_kernel,
        out_shape=(
            sds((rows, width), BF16),
            sds((rows, width), F32),
            sds((rows, width), BF16),
            sds((rows, TOP), F32),
        )
        + (sds((local, capacity, width), BF16),) * (2 * count),
        in_specs=[pl.BlockSpec(memory_space=pltpu.SMEM)] + [vmem] * (9 + groups),
        out_specs=(vmem,) * (4 + 2 * count),
        scratch_shapes=[
            pltpu.VMEM((groups, rows // 2, 384), F32),
            pltpu.VMEM((rows, width), F32),
        ],
        compiler_params=pltpu.CompilerParams(vmem_limit_bytes=48 * 1024 * 1024),
        cost_estimate=SMALL,
    )(place.g[None], x, grad, weight, gain[None], router, *picks, *seats, *outs)
    return low, middle, mixed, gates, sent[:count], sent[count:]


def trade(parts, axis):
    size = lax.axis_size(axis)
    return [parts[0]] + [
        lax.ppermute(parts[d], axis, [(i, i ^ d) for i in range(size)]) for d in range(1, size)
    ]


def ffn_kernel(shared, count, dp, experts, table, *refs):
    x_refs, dy_refs, (gate_ref, up_ref, down_ref) = refs[:count], refs[count : 2 * count], refs[2 * count : 2 * count + 3]
    refs = refs[2 * count + 3 :]
    if shared:
        result, back, in_keep, in_send, out_keep, out_send, stage, turned, turned_dy = refs
        x_ref, dy_ref = x_refs[0], dy_refs[0]
    else:
        both, refs = refs[:count], refs[count:]
        gate_keep, gate_send, up_keep, up_send, out_keep, out_send = refs[:6]
        in_keep, in_send = (gate_keep, up_keep), (gate_send, up_send)
        stage, turned, result, back, x_ref, dy_ref = refs[6:]
    step = pl.program_id(0)
    width = x_ref.shape[1]
    rows = x_ref.shape[0]

    @pl.when(step == 0)
    def _():
        if not shared:
            part = rows // count
            for d in range(count):
                x_ref[d * part : (d + 1) * part] = x_refs[d][0]
                dy_ref[d * part : (d + 1) * part] = dy_refs[d][0]
        whole = x_ref[...].astype(F32).T
        block = width // dp
        for b in range(dp):
            start = pl.multiple_of(table[2 * STEPS + b], 8)
            stage[pl.ds(start, block), :] = whole[b * block : (b + 1) * block]
        turned[...] = stage[...].astype(BF16)
        if shared:
            whole = dy_ref[...].astype(F32).T
            block = width // experts
            for e in range(experts):
                start = pl.multiple_of(table[2 * STEPS + dp + e], 8)
                stage[pl.ds(start, block), :] = whole[e * block : (e + 1) * block]
            turned_dy[...] = stage[...].astype(BF16)
        result[...] = jnp.zeros_like(result)
        back[...] = jnp.zeros_like(back)

    x, dy = x_ref[...], dy_ref[...]
    w_gate, w_up, w_down = gate_ref[0], up_ref[0], down_ref[0]
    gate, up = nn(x, w_gate), nn(x, w_up)
    grad = nt(dy, w_down)
    sig = jax.nn.sigmoid(gate)
    silu = gate * sig
    act = (silu * up).astype(BF16)
    grad_gate = (grad * up * (sig * (1.0 + gate * (1.0 - sig)))).astype(BF16)
    grad_up = (grad * silu).astype(BF16)
    result[...] += nn(act, w_down)
    back[...] += nt(grad_gate, w_gate) + nt(grad_up, w_up)
    xt = turned[...]
    half = width // 2
    for k, upper in enumerate((grad_gate, grad_up)):
        grad_in = nn(xt, upper).astype(BF16)
        if shared:

            @pl.when(step < STEPS // 2)
            def _():
                in_keep[k] = grad_in

            @pl.when(step >= STEPS // 2)
            def _():
                in_send[k] = grad_in

        else:
            in_keep[k][...] = grad_in[:half]
            in_send[k][...] = grad_in[half:]
    if shared:
        grad_out = nn(turned_dy[...], act).astype(BF16)
        out_keep[...] = grad_out[:half]
        out_send[...] = grad_out[half:]
    else:
        grad_out = lax.dot_general(
            act, dy, (((0,), (0,)), ((), ())), preferred_element_type=F32
        ).astype(BF16)

        @pl.when(step < STEPS // 2)
        def _():
            out_keep[...] = grad_out

        @pl.when(step >= STEPS // 2)
        def _():
            out_send[...] = grad_out

        @pl.when(step == STEPS - 1)
        def _():
            part = rows // count
            for d in range(count):
                both[d][:, :width] = result[d * part : (d + 1) * part].astype(BF16)
                both[d][:, width:] = back[d * part : (d + 1) * part].astype(BF16)


def ffn(shared, place, table, xs, dys, w_in, w_out, e):
    count = len(xs)
    part, width = xs[0].shape[-2:]
    rows = part * count
    if shared:
        given = pl.BlockSpec((rows, width), lambda i, t: (0, 0))
    else:
        given = pl.BlockSpec((1, part, width), lambda i, t: (e, 0, 0))
    hidden = w_out.shape[1]
    chunk = hidden // STEPS
    near, far = STEPS // 2 - 1, STEPS // 2
    sds = jax.ShapeDtypeStruct
    first = lambda i, t: (0, 0, jnp.minimum(i, near))
    second = lambda i, t: (0, 0, jnp.maximum(i - far, 0))
    if shared:
        out_shape = (
            sds((rows, width), F32),
            sds((rows, width), F32),
            sds((2, width, hidden // 2), BF16),
            sds((2, width, hidden // 2), BF16),
            sds((width // 2, hidden), BF16),
            sds((width // 2, hidden), BF16),
        )
        out_specs = (
            pl.BlockSpec((rows, width), lambda i, t: (0, 0)),
            pl.BlockSpec((rows, width), lambda i, t: (0, 0)),
            pl.BlockSpec((2, width, chunk), first),
            pl.BlockSpec((2, width, chunk), second),
            pl.BlockSpec((width // 2, chunk), lambda i, t: (0, t[STEPS + i])),
            pl.BlockSpec((width // 2, chunk), lambda i, t: (0, t[STEPS + i])),
        )
        extra = [pltpu.VMEM((width, rows), BF16)]
    else:
        out_shape = (
            *[sds((part, 2 * width), BF16)] * count,
            *[sds((width // 2, hidden), BF16)] * 4,
            sds((hidden // 2, width), BF16),
            sds((hidden // 2, width), BF16),
        )
        out_specs = (
            *[pl.BlockSpec((part, 2 * width), lambda i, t: (0, 0))] * count,
            *[pl.BlockSpec((width // 2, chunk), lambda i, t: (0, t[i]))] * 4,
            pl.BlockSpec((chunk, width), lambda i, t: (jnp.minimum(i, near), 0)),
            pl.BlockSpec((chunk, width), lambda i, t: (jnp.maximum(i - far, 0), 0)),
        )
        extra = [pltpu.VMEM((rows, width), F32)] * 2 + [pltpu.VMEM((rows, width), BF16)] * 2
    return pl.pallas_call(
        functools.partial(ffn_kernel, shared, count, place.dp, place.experts),
        out_shape=out_shape,
        grid_spec=pltpu.PrefetchScalarGridSpec(
            num_scalar_prefetch=1,
            grid=(STEPS,),
            in_specs=[
                *[given] * (2 * count),
                pl.BlockSpec((1, width, chunk), lambda i, t: (e, 0, t[i])),
                pl.BlockSpec((1, width, chunk), lambda i, t: (e, 0, STEPS + t[i])),
                pl.BlockSpec((1, chunk, width), lambda i, t: (e, t[i], 0)),
            ],
            out_specs=out_specs,
            scratch_shapes=[pltpu.VMEM((width, rows), F32), pltpu.VMEM((width, rows), BF16)]
            + extra,
        ),
        compiler_params=pltpu.CompilerParams(vmem_limit_bytes=48 * 1024 * 1024),
        cost_estimate=SMALL,
    )(table, *xs, *dys, w_in, w_in, w_out)


def swap(a, axis, bit=1):
    size = lax.axis_size(axis)
    return lax.ppermute(a, axis, [(i, i ^ bit) for i in range(size)])


def add(a, b, kind=BF16):
    return (a.astype(F32) + b.astype(F32)).astype(kind)


def half_of(a, dim, index):
    size = a.shape[dim] // 2
    return lax.dynamic_slice_in_dim(a, index * size, size, dim)


def exchange(keep, came, dim, mine):
    return [add(half_of(keep, dim, i), half_of(came, dim, i)) for i in (mine, 1 - mine)]


def scatter(a, axis, dim):
    return lax.psum_scatter(a, axis, scatter_dimension=dim, tiled=True)


def reduce_experts(place, keep, send):
    came = swap(send, "g", 1)
    keep, send = exchange(keep, came, 0, place.high)
    return scatter(add(keep, swap(send, "g", 2)), "r", 0).astype(F32)


def after(x, *values):
    return lax.optimization_barrier((x, *values))[0]


def reduce_tokens(place, keep, came, dim):
    keep, send = exchange(keep, came, dim, place.low)
    came = swap(send, "g", 1)
    keep, send = exchange(keep, came, dim, place.high)
    came = swap(send, "g", 2)
    return scatter(add(keep, came), "r", dim).astype(F32)


def reduce_shared_in(place, keep, send):
    total = add(keep, swap(send, "c"))
    two, width, columns = total.shape
    parts = place.rows_y // 2
    total = total.reshape(two, width, parts, columns // parts).transpose(0, 2, 1, 3)
    mine = scatter(total.reshape(two * parts, width, columns // parts), "y", 0)[0]
    return reduce_tokens(place, mine, jnp.zeros_like(mine), 0)


def reduce_shared_out(place, keep, send):
    mine = scatter(add(keep, swap(send, "c")), "y", 0)
    return reduce_tokens(place, mine, jnp.zeros_like(mine), 1)


def to_flat(place, x):
    rows, width = x.shape
    x = x.reshape(rows, 2, 2, place.lanes, width // place.dp)
    order = (0, 3, 2, 1, 4) if place.lanes == 2 else (0, 2, 1, 3, 4)
    return x.transpose(order).reshape(rows, width)


def weight_grad(place, left, right, extra):
    rows, columns = right.shape
    width = left.shape[1]
    own = columns // place.experts
    parts = right.reshape(rows, place.rows_y, 2, own)
    extra = extra.reshape(width, place.rows_y, 2, extra.shape[-1]).astype(BF16)
    keep, send = [
        jnp.concatenate(
            [
                lax.dot_general(
                    left,
                    lax.dynamic_index_in_dim(parts, i, 2, False).reshape(rows, columns // 2),
                    (((0,), (0,)), ((), ())),
                    preferred_element_type=F32,
                )
                .astype(BF16)
                .reshape(width, place.rows_y, own),
                lax.dynamic_index_in_dim(extra, i, 2, False),
            ],
            axis=2,
        ).transpose(1, 0, 2)
        for i in (place.c, 1 - place.c)
    ]
    return keep, send


def reduce_weight(place, keep, send):
    mine = scatter(add(keep, swap(send, "c")), "y", 0)[0]
    return reduce_tokens(place, mine, jnp.zeros_like(mine), 0)


def in_two(vector):
    high = vector.astype(BF16).astype(F32)
    return [high, vector - high]


def beside(place, columns, experts_of):
    width = columns[0].shape[0]
    every = jnp.stack(columns, axis=1)[:, None, :]
    every = jnp.broadcast_to(every, (width, place.experts, len(columns)))
    parts = [every] if experts_of is None else [every, experts_of]
    used = sum(p.shape[2] for p in parts)
    return jnp.concatenate(parts + [jnp.zeros((width, place.experts, 64 - used), F32)], axis=2)


def combine_kernel(
    here, hot0, hot1, gate_ref, pick0, pick1, grad_ref, middle_ref,
    shared_ref, back_ref, mixed_in_ref, router_ref, gain_ref, w_ref, *refs,
):
    output_ref, middle_grad_ref, low_ref, *head_refs = refs[-11:-4]
    norm_ref, router_grad_ref, returned, heads = refs[-4:]
    ret_refs = refs[:-11]
    width = grad_ref.shape[1]
    part = ret_refs[0].shape[0]
    for i, ref in enumerate(ret_refs):
        returned[i * part : (i + 1) * part] = ref[...]
    hots = (hot0[...], hot1[...])
    grad = grad_ref[...].astype(F32)
    middle = middle_ref[...]
    backs = [nn(h, returned[:, :width]) for h in hots]
    gates = [gate_ref[:, k : k + 1] for k in range(TOP)]
    routed = sum(gates[k] * backs[k] for k in range(TOP))
    output_ref[...] = (middle + routed + shared_ref[...]).astype(BF16)
    slopes = [jnp.sum(b * grad, axis=1, keepdims=True) for b in backs]
    inner = sum(gates[k] * slopes[k] for k in range(TOP))
    logits = sum(
        pick[...] * (gates[k] * (slopes[k] - inner)) for k, pick in enumerate((pick0, pick1))
    ).astype(BF16)
    router_grad_ref[...] = lax.dot_general(
        logits, mixed_in_ref[...], (((0,), (0,)), ((), ())), preferred_element_type=F32
    )
    mixed = back_ref[...] + nn(logits, router_ref[...]) + nn(hots[0] + hots[1], returned[:, width:])
    scale = rms_scale(middle)
    norm_ref[...] = jnp.sum(mixed * middle * scale, axis=0, keepdims=True)
    middle_grad = grad + rms_back(middle, scale, gain_ref[...], mixed)
    middle_grad_ref[...] = middle_grad
    low = middle_grad.astype(BF16)
    low_ref[...] = low
    pack_heads(nt(low, w_ref[...]), heads)
    for d, ref in enumerate(head_refs):
        ref[...] = heads[here[0] ^ d]


def combine(place, hots, rets, gates, picks, grad, middle, shared, back, mixed_in, router, gain, weight):
    rows, width = grad.shape
    vmem = pl.BlockSpec(memory_space=pltpu.VMEM)
    sds = jax.ShapeDtypeStruct
    output, middle_grad, low, *heads, norm, router_grad = pl.pallas_call(
        combine_kernel,
        out_shape=(
            sds((rows, width), BF16),
            sds((rows, width), F32),
            sds((rows, width), BF16),
        )
        + (sds((rows // 2, 384), BF16),) * place.groups
        + (
            sds((1, width), F32),
            sds((router.shape[1], width), F32),
        ),
        in_specs=[pl.BlockSpec(memory_space=pltpu.SMEM)] + [vmem] * (13 + len(rets)),
        out_specs=(vmem,) * (5 + place.groups),
        scratch_shapes=[
            pltpu.VMEM((hots[0].shape[1], 2 * width), BF16),
            pltpu.VMEM((place.groups, rows // 2, 384), BF16),
        ],
        compiler_params=pltpu.CompilerParams(vmem_limit_bytes=48 * 1024 * 1024),
        cost_estimate=SMALL,
    )(
        place.g[None], *hots, gates, *picks, grad, middle, shared, back, mixed_in,
        router.T, gain[None], weight, *rets,
    )
    return output, middle_grad, low, heads, norm, router_grad


class Sum:
    def __init__(self, keep, send, stages):
        self.keep, self.send, self.stages = keep, send, list(stages)

    def step(self, *behind):
        axis, bit, dim, mine = self.stages.pop(0)
        send = after(self.send, *behind) if behind else self.send
        came = swap(send, axis, bit)
        if dim is None:
            self.keep = add(self.keep, came, F32)
        else:
            self.keep, self.send = exchange(self.keep, came, dim, mine)
        return self.keep

    def finish(self):
        while self.stages:
            self.step()
        return self.keep


def expert_sum(place, keep, send, lead):
    if lead == "r":
        near = [("r", 1, 0, place.low), ("g", 1, 0, place.high)]
    else:
        near = [("g", 1, 0, place.r), ("r", 1, 0, place.high)]
    return Sum(keep, send, near + [("g", 2, None, None)])


def every_sum(place, keep, send, dim):
    return Sum(
        keep,
        send,
        [
            ("c", 1, 0, place.y),
            ("y", 1, dim, place.r),
            ("r", 1, dim, place.low),
            ("g", 1, dim, place.high),
            ("g", 2, None, None),
        ],
    )


def local(
    tokens,
    norm_attn,
    query_key_value_weight,
    attention_output_weight,
    norm_ffn,
    router,
    expert_in,
    expert_out,
    shared_gate_up_weight,
    shared_down_weight,
    block_lengths,
    routes,
    cotangent,
):
    place = Place()
    fast = place.lanes == 2 and place.rows_y == 2
    _, row_count, model_width = tokens.shape
    shard_index = lax.axis_index(DP)
    length = row_count * place.dp
    positions = shard_index * row_count + jnp.arange(row_count, dtype=jnp.int32)
    bounds = jnp.cumsum(block_lengths[0])
    cosine, sine = rope_table(positions)
    experts_total = router.shape[1]
    local_experts = expert_in.shape[1]
    groups = place.experts
    capacity = row_count * TOP * 5 // (4 * experts_total)
    chosen = routes[0]
    column = jnp.arange(experts_total, dtype=jnp.int32)
    picks = [(chosen[:, k : k + 1] == column[None, :]).astype(F32) for k in range(TOP)]
    flat_routes = chosen.reshape(row_count * TOP)
    route_hot = (flat_routes[:, None] == column[None, :]).astype(jnp.int32)
    earlier = jnp.cumsum(route_hot, axis=0) - route_hot
    slot_index = jnp.sum(earlier * route_hot, axis=1)
    partner = (flat_routes // local_experts) ^ lax.axis_index(EX)
    target = jnp.where(
        slot_index < capacity,
        (flat_routes % local_experts * groups + partner) * capacity + slot_index,
        -1,
    ).reshape(row_count, TOP)
    seats = jnp.arange(experts_total * capacity, dtype=jnp.int32)
    hots = [(target[:, k : k + 1] == seats[None, :]).astype(BF16) for k in range(TOP)]
    seated = [(target[:, k][None, :] == seats[:, None]).astype(BF16) for k in range(TOP)]
    upstream = cotangent[0]

    normalized_rows, own_q, own_kv = project(
        place, tokens[0], norm_attn, query_key_value_weight, cosine, sine
    )
    kv = trade(own_kv, "g")
    q = trade(own_q, "g")
    if fast:
        kvs = kv + [swap(a, "r") for a in kv]
        lanes_of = [place.r, 1 - place.r]
    else:
        every_kv = [lax.all_gather(a, "r", axis=0, tiled=False) for a in kv]
        kvs = [a[i] for i in range(place.lanes) for a in every_kv]
        lanes_of = [jnp.int32(i) for i in range(place.lanes)]
    starts = (jnp.arange(place.groups, dtype=jnp.int32) * place.lanes + place.r) * row_count
    query_places = starts[:, None] + jnp.arange(row_count, dtype=jnp.int32)[None, :]
    limit = jnp.min(
        jnp.where(bounds[None, None, :] > query_places[:, :, None], bounds, length), axis=-1
    )
    span = row_count * place.lanes
    info = jnp.concatenate(
        [place.g[None], (jnp.max(limit, axis=1) + span - 1) // span, jnp.stack(lanes_of)]
    ).astype(jnp.int32)
    limit = limit[:, None, :]
    expert_in = jnp.transpose(expert_in, (1, 0, 2))
    expert_out = jnp.transpose(expert_out, (1, 0, 2))
    q[0] = after(q[0], expert_in, expert_out)
    own_out, lse = attend(place, info, limit, q, kvs)
    attended_low, middle, mixed_in, gates, send_rows, send_grads = middle_part(
        place,
        capacity,
        trade(own_out, "g"),
        tokens[0],
        upstream,
        attention_output_weight,
        norm_ffn,
        router,
        picks,
        seated,
    )
    arrived = trade(send_rows, EX)
    grad_arrived = trade(send_grads, EX)
    shared_result, shared_back, *shared_grads = ffn(
        True,
        place,
        place.shared_table(model_width),
        [mixed_in],
        [upstream],
        shared_gate_up_weight[None],
        shared_down_weight[None],
        0,
    )
    came_back, parts = [], []
    behind = shared_result
    for e in range(local_experts):
        own = [after(arrived[0], behind)] + arrived[1:]
        results = ffn(
            False,
            place,
            place.expert_table(model_width, LEADS[e]),
            own,
            grad_arrived,
            expert_in,
            expert_out,
            e,
        )
        behind = results[0]
        came_back.append(trade(results[:groups], EX))
        parts.append(results[groups:])
    rets = [a for back in came_back for a in back]
    if fast:
        sums = [
            [expert_sum(place, *parts[e][k : k + 2], "r") for k in (0, 2)]
            + [expert_sum(place, *parts[e][4:], LEADS[e])]
            for e in range(local_experts)
        ]
        shared_in = every_sum(place, *shared_grads[:2], 1)
        shared_out = every_sum(place, *shared_grads[2:], 1)
        shared_in.step()
        shared_out.step()
        (first, second, third), (fourth, fifth, sixth) = sums
        first.step()
        third.step()
        rets[-1] = after(rets[-1], first.keep, third.keep)
    output, grad_middle, grad_attn_low, own_grad, grad_norm_ffn, grad_router = combine(
        place,
        hots,
        rets,
        gates,
        picks,
        upstream,
        middle,
        shared_result,
        shared_back,
        mixed_in,
        router,
        norm_ffn,
        attention_output_weight,
    )
    flat = lambda x: to_flat(place, x)
    extra = beside(
        place,
        in_two(flat(grad_norm_ffn)[0]),
        flat(grad_router).T.reshape(model_width, groups, local_experts),
    )
    own_grad = trade(own_grad, "g")
    sides_out = weight_grad(place, flat(attended_low), grad_attn_low, extra)
    if fast:
        second.step(first.keep)
        first.step()
        third.step()
        shared_in.step(rets[-1])
        shared_out.step(rets[-1])
        sum_out = every_sum(place, *sides_out, 1)
        sum_out.step()
        own_grad[0] = after(own_grad[0], first.keep)
    own_dq, own_dkv = attend_back(place, info, limit, lse, q, own_out, own_grad, kvs)
    dq = trade(own_dq, "g")
    if fast:
        first.step()
        came = [swap(a, "r") for a in own_dkv[1]]
        came[0] = after(came[0], second.keep, third.keep)
        dkv = [add(a, b) for a, b in zip(own_dkv[0], came)]
        fourth.step(came[0])
        second.step()
    else:
        dkv = [
            scatter(jnp.stack([a[d] for a in own_dkv]), "r", 0)[0] for d in range(place.groups)
        ]
    dkv = trade(dkv, "g")
    if fast:
        dkv[0] = after(dkv[0], second.keep, fourth.keep, shared_in.keep)
    grad_projected, grad_input, grad_norm_attn = finish(
        place,
        dq,
        dkv,
        query_key_value_weight,
        cosine,
        sine,
        tokens[0],
        norm_attn,
        grad_middle,
    )
    extra = beside(place, in_two(flat(grad_norm_attn)[0]), None)
    sides_qkv = weight_grad(place, flat(normalized_rows), grad_projected, extra)
    if fast:
        fifth.step(fourth.keep)
        sum_qkv = every_sum(place, *sides_qkv, 1)
        sum_qkv.step()
        fourth.step()
        sixth.step(fifth.keep)
        in_grads = [[s.finish() for s in row[:2]] for row in sums]
        out_grads = [row[2].finish() for row in sums]
        sum_shared_in, sum_shared_out = shared_in.finish()[0], shared_out.finish()
        sum_out, sum_qkv = sum_out.finish()[0], sum_qkv.finish()[0]
    else:
        in_grads = [
            [reduce_experts(place, *part[k : k + 2]) for k in (0, 2)] for part in parts
        ]
        out_grads = [reduce_experts(place, *part[4:]) for part in parts]
        sum_shared_in = reduce_shared_in(place, *shared_grads[:2])
        sum_shared_out = reduce_shared_out(place, *shared_grads[2:])
        sum_out, sum_qkv = reduce_weight(place, *sides_out), reduce_weight(place, *sides_qkv)
    own = model_width // place.experts
    sum_out, small = sum_out[:, :own], sum_out[:, own:]
    sum_norm_ffn, sum_router = small[:, 0] + small[:, 1], small[:, 2 : 2 + local_experts]
    sum_qkv, small = sum_qkv[:, : 3 * own], sum_qkv[:, 3 * own :]
    sum_norm_attn = small[:, 0] + small[:, 1]
    part_in = jnp.stack([jnp.concatenate(g, axis=1) for g in in_grads], axis=1)
    part_out = jnp.stack(out_grads, axis=1)
    return (
        output[None],
        grad_input[None],
        sum_norm_attn,
        sum_qkv,
        sum_out,
        sum_norm_ffn,
        sum_router,
        part_in,
        part_out,
        sum_shared_in,
        sum_shared_out.T,
    )


def solution(mesh):
    dp, experts = mesh.shape["dp"], mesh.shape["expert"]
    finer = Mesh(mesh.devices.reshape(4, dp // 4, experts // 2, 2), ("g", "r", "y", "c"))
    whole = P()
    return jax.shard_map(
        local,
        mesh=finer,
        in_specs=(
            P(EX, DP, None),
            whole,
            whole,
            whole,
            whole,
            whole,
            P(None, EX, None),
            P(None, EX, None),
            whole,
            whole,
            P(EX, None),
            P(EX, DP, None),
            P(EX, DP, None),
        ),
        out_specs=(
            P(EX, DP, None),
            P(EX, DP, None),
            P(DP),
            P(DP, EX),
            P(DP, EX),
            P(DP),
            P(DP, EX),
            P(DP, EX, None),
            P(DP, EX, None),
            P(DP, EX),
            P(DP, EX),
        ),
        check_vma=False,
    )
```

time: 709 us -> 531 us (0.75)
  waiting for transfers between devices: 266 us -> 182 us
  blocking collectives: 76 us -> 0 us
  other arithmetic: 78.4 us -> 61.3 us
  Pallas kernels: 91.8 us -> 104 us
  matrix products: 16.6 us -> 5.56 us
    ppermute x34 -> x46, waiting for transfers between devices: 217 us -> 135 us  [swap(): return lax.ppermute(a, axis, [(i, i ^ bit) for i in range(size)])]
    psum x1 -> x0, blocking collectives: 76 us -> none  [local(): lax.psum(grad_norm_attn, DP + EX)]
    all_to_all x10 -> x0, waiting for transfers between devices: 48.5 us -> none  [the longest x6 36.4 us: trade_heads(): return lax.all_to_all(a, 'g', split_axis=0, concat_axis=0, tiled=True)]
    ppermute x0 -> x30, waiting for transfers between devices: none -> 46.6 us  [trade(): lax.ppermute(parts[d], axis, [(i, i ^ d) for i in range(size)])]
    all_to_all x10 -> x0, starting transfers between devices: 42.8 us -> none  [the longest x6 25.9 us: trade_heads(): return lax.all_to_all(a, 'g', split_axis=0, concat_axis=0, tiled=True)]
    ppermute x0 -> x30, starting transfers between devices: none -> 36.9 us  [trade(): lax.ppermute(parts[d], axis, [(i, i ^ d) for i in range(size)])]
    convert_element_type x25 -> x32, other arithmetic: 58.8 us -> 38 us  [add(): return (a.astype(F32) + b.astype(F32)).astype(kind)]
    dot_general x10 -> x0, matrix products: 11.4 us -> none  [the longest x2 4.38 us: local(): jnp.dot(h, returned[:, :model_width], preferred_element_type=F32)]
  transfers between devices with their start and end apart: 44 -> 76, of which waited for: 16 -> 29; matrix products, arithmetic and copies ran while one was open for 21% -> 21% of each run, Pallas kernels for 8% -> 16%
where the time goes in v3:
time: 531 us; the launch traced here: 521 us
  waiting for transfers between devices  182 us (34%)
  Pallas kernels  104 us (20%)
  starting transfers between devices  88.1 us (17%)
  local copies, waits for them, and re-layouts  77.8 us (15%)
  other arithmetic  61.3 us (12%)
  matrix products  5.56 us (1%)
    ppermute x46, waiting for transfers between devices, swap(): return lax.ppermute(a, axis, [(i, i ^ bit) for i in range(size)])  135 us
    unnamed x272, local copies, waits for them, and re-layouts  58.8 us
    pallas_call x3, Pallas kernels, ffn(): pl.pallas_call(functools.partial(ffn_kernel, shared, count, place.dp, pla...  54.5 us
    ppermute x46, starting transfers between devices, swap(): return lax.ppermute(a, axis, [(i, i ^ bit) for i in range(size)])  51.1 us
    ppermute x30, waiting for transfers between devices, trade(): lax.ppermute(parts[d], axis, [(i, i ^ d) for i in range(size)])  46.6 us
    convert_element_type x32, other arithmetic, add(): return (a.astype(F32) + b.astype(F32)).astype(kind)  38 us
    ppermute x30, starting transfers between devices, trade(): lax.ppermute(parts[d], axis, [(i, i ^ d) for i in range(size)])  36.9 us
    pallas_call x1, Pallas kernels, attend_back(): pl.pallas_call(functools.partial(attend_back_kernel, sources, shards, pla...  19.6 us
  transfers between devices with their start and end apart: 76, of which 29 were waited for; matrix products, arithmetic and copies ran while one was open for 21% of the time, Pallas kernels for 16%

profile of v3, /device:TPU:0, one launch (start us, length us, event | category | flops | bytes accessed | tf_op | source)
XLA Modules:
  0.0 521.0 jit_solution(4614490269283102641)
XLA Ops:
  5.0 3.6 shard_map.212
  9.4 3.0 collective-permute-start.3
  20.8 14.7 %copy.109 = bf16[768,2,4096]{2,0,1:T(8,128)(2,1)} copy(bf16[768,2,4096]{2,1,0:T(2,128)(2,1)} %param.19) | data formatting | bytes 25165824 | tf_op args[6]
  35.6 3.4 copy.110
  39.0 3.6 collective-permute-start.1
  47.6 5.2 %collective-permute-done.2.refs_3_ = bf16[128,384]{1,0:T(8,128)(2,1)S(1)} collective-permute-done((bf16[128,384]{1,0:T(8,128)(2,1)S(1)}, bf16[128,384]{1,0:T(8,128)(2,1)S(1)}, u32[]{:S(2)}, u32[]{:S(2)}) %collective-permute-start.2) | collective-permute-done | bytes 98336 | tf_op jit(solution)/shard_map/ppermute | solution.py:573
  56.0 11.9 %shard_map.213 = (bf16[128,384]{1,0:T(8,128)(2,1)S(1)}, bf16[128,384]{1,0:T(8,128)(2,1)S(1)}, bf16[128,384]{1,0:T(8,128)(2,1)}, bf16[128,384]{1,0:T(8,128)(2,1)}, f32[4,1,768]{2,1,0:T(1,128)S(1)}) custom-call(s32[7]{0:T(128)S(1)} %pad_add_fusion.info, s32[4,1,256]{2,1,0:T(1,128)S(1)} %broadcast_in_dim.41.limit_ref, ...), custom_call_target="tpu_custom_call" | custom-call | flops 1024 | bytes 1024 | tf_op jit(solution)/shard_map/pallas_call | solution.py:326
  69.4 3.5 collective-permute-start.12
  80.5 4.2 shard_map.214
  89.3 18.2 %shard_map.215 = (f32[256,768]{1,0:T(8,128)S(1)}, f32[256,768]{1,0:T(8,128)S(1)}, bf16[2,768,1024]{2,1,0:T(8,128)(2,1)}, bf16[2,768,1024]{2,1,0:T(8,128)(2,1)}, ...) custom-call(s32[28]{0:T(128)S(1)} %stack.203.table, ...), custom_call_target="tpu_custom_call" | custom-call | flops 1024 | bytes 1024 | tf_op jit(solution)/shard_map/pallas_call | solution.py:714
  113.2 5.6 %collective-permute-done.15.refs_3_ = bf16[2,80,768]{2,1,0:T(8,128)(2,1)S(1)} collective-permute-done((bf16[2,80,768]{2,1,0:T(8,128)(2,1)}, bf16[2,80,768]{2,1,0:T(8,128)(2,1)S(1)}, u32[]{:S(2)}, u32[]{:S(2)}) %collective-permute-start.15) | collective-permute-done | bytes 245792 | tf_op jit(solution)/shard_map/ppermute | solution.py:573
  118.8 6.1 %collective-permute-done.17.refs_6_ = bf16[2,80,768]{2,1,0:T(8,128)(2,1)S(1)} collective-permute-done((bf16[2,80,768]{2,1,0:T(8,128)(2,1)}, bf16[2,80,768]{2,1,0:T(8,128)(2,1)S(1)}, u32[]{:S(2)}, u32[]{:S(2)}) %collective-permute-start.17) | collective-permute-done | bytes 245792 | tf_op jit(solution)/shard_map/ppermute | solution.py:573
  124.8 4.5 collective-permute-done.18.refs_7_
  129.3 18.1 %shard_map.216 = (bf16[80,1536]{1,0:T(8,128)(2,1)S(1)}, bf16[80,1536]{1,0:T(8,128)(2,1)S(1)}, bf16[80,1536]{1,0:T(8,128)(2,1)S(1)}, bf16[80,1536]{1,0:T(8,128)(2...) custom-call(s32[24]{0:T(128)S(1)} %stack.220.table, ...), custom_call_target="tpu_custom_call" | custom-call | flops 1024 | bytes 1024 | tf_op jit(solution)/shard_map/pallas_call | solution.py:714
  152.4 3.3 collective-permute-start.25
  168.0 18.3 %shard_map.217 = (bf16[80,1536]{1,0:T(8,128)(2,1)S(1)}, bf16[80,1536]{1,0:T(8,128)(2,1)S(1)}, bf16[80,1536]{1,0:T(8,128)(2,1)S(1)}, bf16[80,1536]{1,0:T(8,128)(2...) custom-call(s32[24]{0:T(128)S(1)} %copy-done.73, ...), custom_call_target="tpu_custom_call" | custom-call | flops 1024 | bytes 1024 | tf_op jit(solution)/shard_map/pallas_call | solution.py:714
  188.5 3.4 add_convert_fusion.3
  192.0 3.1 add_convert_fusion.13
  197.0 3.2 add_convert_fusion.15
  202.0 2.9 collective-permute-done.20.refs_2_
  204.9 5.6 %collective-permute-done.21.refs_3_ = bf16[80,1536]{1,0:T(8,128)(2,1)S(1)} collective-permute-done((bf16[80,1536]{1,0:T(8,128)(2,1)S(1)}, bf16[80,1536]{1,0:T(8,128)(2,1)S(1)}, u32[]{:S(2)}, u32[]{:S(2)}) %collective-permute-start.21) | collective-permute-done | bytes 245792 | tf_op jit(solution)/shard_map/ppermute | solution.py:573
  210.5 4.8 shard_map.218
  240.1 3.9 collective-permute-done.28.refs_9_
  244.1 2.9 collective-permute-start.29
  250.0 9.0 %collective-permute-done.29.refs_10_ = bf16[128,384]{1,0:T(8,128)(2,1)S(1)} collective-permute-done((bf16[128,384]{1,0:T(8,128)(2,1)S(1)}, bf16[128,384]{1,0:T(8,128)(2,1)S(1)}, u32[]{:S(2)}, u32[]{:S(2)}) %collective-permute-start.29) | collective-permute-done | bytes 98336 | tf_op jit(solution)/shard_map/ppermute | solution.py:573
  263.8 19.6 %shard_map.219 = (bf16[128,384]{1,0:T(8,128)(2,1)}, bf16[128,384]{1,0:T(8,128)(2,1)}, bf16[128,384]{1,0:T(8,128)(2,1)}, bf16[128,384]{1,0:T(8,128)(2,1)}, bf16[2...) custom-call(s32[7]{0:T(128)} %copy-done.71, ...), custom_call_target="tpu_custom_call" | custom-call | flops 1024 | bytes 1024 | tf_op jit(solution)/shard_map/pallas_call | solution.py:417
  283.5 4.6 collective-permute-start.34
  294.4 3.6 add_convert_fusion.1
  312.8 10.2 %collective-permute-done.37 = bf16[192,2048]{1,0:T(8,128)(2,1)S(1)} collective-permute-done((bf16[192,2048]{1,0:T(8,128)(2,1)S(1)}, bf16[192,2048]{1,0:T(8,128)(2,1)S(1)}, u32[]{:S(2)}, u32[]{:S(2)}) %collective-permute-start.37) | collective-permute-done | bytes 786464 | tf_op jit(solution)/shard_map/ppermute | solution.py:737
  324.9 3.5 collective-permute-done.74
  330.2 3.2 collective-permute-done.55
  334.7 20.2 %collective-permute-done.58 = bf16[96,2048]{1,0:T(8,128)(2,1)S(1)} collective-permute-done((bf16[96,2048]{1,0:T(8,128)(2,1)S(1)}, bf16[96,2048]{1,0:T(8,128)(2,1)S(1)}, u32[]{:S(2)}, u32[]{:S(2)}) %collective-permute-start.58) | collective-permute-done | bytes 393248 | tf_op jit(solution)/shard_map/ppermute | solution.py:737
  361.6 2.8 collective-permute-start.42
  366.4 2.8 collective-permute-start.56
  370.5 5.3 %shard_map.220 = (bf16[256,2304]{1,0:T(8,128)(2,1)S(1)}, f32[256,768]{1,0:T(8,128)}, f32[1,768]{1,0:T(1,128)S(1)}) custom-call(s32[1]{0:T(128)} %bitcast.here, bf16[768,2304]{1,0:T(8,128)(2,1)} %w_ref.7, f32[256,128]{1,0:T(8,128)S(1)} %copy-done.13, f32[256,128]{1,0:T(8,128)S(1)} %copy-done.11, bf16[256,768]{1,0:T(8,128)(2,1)S(1)} %bitcast.166, ...), custom_call_target="tpu_custom_call" | custom-call | flops 1024 | bytes 1024 | tf_op jit(solution)/shard_map/pallas_call | solution.py:477
  379.5 2.9 copy.91
  392.9 24.8 %collective-permute-done.68 = bf16[1,384,1024]{2,1,0:T(8,128)(2,1)S(1)} collective-permute-done((bf16[1,384,1024]{2,1,0:T(8,128)(2,1)}, bf16[1,384,1024]{2,1,0:T(8,128)(2,1)S(1)}, u32[]{:S(2)}, u32[]{:S(2)}) %collective-permute-start.68) | collective-permute-done | bytes 786464 | tf_op jit(solution)/shard_map/ppermute | solution.py:737
  418.8 3.2 add_convert_fusion.8
  428.6 7.0 %collective-permute-done.69 = bf16[1,192,1024]{2,1,0:T(8,128)(2,1)S(1)} collective-permute-done((bf16[1,192,1024]{2,1,0:T(8,128)(2,1)}, bf16[1,192,1024]{2,1,0:T(8,128)(2,1)S(1)}, u32[]{:S(2)}, u32[]{:S(2)}) %collective-permute-start.69) | collective-permute-done | bytes 393248 | tf_op jit(solution)/shard_map/ppermute | solution.py:737
  440.6 2.9 collective-permute-start.60
  443.5 11.2 %collective-permute-done.70 = bf16[1,96,1024]{2,1,0:T(8,128)(2,1)S(1)} collective-permute-done((bf16[1,96,1024]{2,1,0:T(8,128)(2,1)S(1)}, bf16[1,96,1024]{2,1,0:T(8,128)(2,1)S(1)}, u32[]{:S(2)}, u32[]{:S(2)}) %collective-permute-start.70) | collective-permute-done | bytes 196640 | tf_op jit(solution)/shard_map/ppermute | solution.py:737
  456.6 9.0 %collective-permute-done.60 = bf16[96,2048]{1,0:T(8,128)(2,1)S(1)} collective-permute-done((bf16[96,2048]{1,0:T(8,128)(2,1)S(1)}, bf16[96,2048]{1,0:T(8,128)(2,1)S(1)}, u32[]{:S(2)}, u32[]{:S(2)}) %collective-permute-start.60) | collective-permute-done | bytes 393248 | tf_op jit(solution)/shard_map/ppermute | solution.py:737
  471.6 4.3 collective-permute-done.49
  476.8 18.7 %collective-permute-done.50 = bf16[1,192,640]{1,2,0:T(8,128)(2,1)S(1)} collective-permute-done((bf16[1,192,640]{1,2,0:T(8,128)(2,1)S(1)}, bf16[1,192,640]{1,2,0:T(8,128)(2,1)S(1)}, u32[]{:S(2)}, u32[]{:S(2)}) %collective-permute-start.50) | collective-permute-done | bytes 245792 | tf_op jit(solution)/shard_map/ppermute | solution.py:737
  496.0 4.1 copy.100
  500.9 2.9 collective-permute-start.67
  503.8 9.2 %collective-permute-done.51 = bf16[1,96,640]{1,2,0:T(8,128)(2,1)S(1)} collective-permute-done((bf16[1,96,640]{1,2,0:T(8,128)(2,1)S(1)}, bf16[1,96,640]{1,2,0:T(8,128)(2,1)S(1)}, u32[]{:S(2)}, u32[]{:S(2)}) %collective-permute-start.51) | collective-permute-done | bytes 122912 | tf_op jit(solution)/shard_map/ppermute | solution.py:737
  514.6 3.3 collective-permute-done.67
  (514 shorter events, 173.3 us)
Async XLA Ops:
  9.4 33.1 %collective-permute-start.3 = (bf16[256,384]{1,0:T(8,128)(2,1)S(1)}, bf16[256,384]{1,0:T(8,128)(2,1)S(1)}, u32[]{:S(2)}, u32[]{:S(2)}) collective-permute-start(bf16[256,384]{1,0:T(8,128)(2,1)S(1)} %get-tuple-element.106), channel_id=1, source_target_pairs={{0,8},{8,0},{16,24},{24,16},{1,9},{9,1},{17,25},{25,17},{2,10},{10... | collective-permute-start | bytes 589832 | tf_op jit(solution)/shard_map/ppermute | solution.py:573
  12.5 30.7 %collective-permute-start.4 = (bf16[256,384]{1,0:T(8,128)(2,1)S(1)}, bf16[256,384]{1,0:T(8,128)(2,1)S(1)}, u32[]{:S(2)}, u32[]{:S(2)}) collective-permute-start(bf16[256,384]{1,0:T(8,128)(2,1)S(1)} %get-tuple-element.107), channel_id=1, source_target_pairs={{0,16},{8,24},{16,0},{24,8},{1,17},{9,25},{17,1},{25,9},{2,18},{10... | collective-permute-start | bytes 589832 | tf_op jit(solution)/shard_map/ppermute | solution.py:573
  15.0 29.6 %collective-permute-start.5 = (bf16[256,384]{1,0:T(8,128)(2,1)S(1)}, bf16[256,384]{1,0:T(8,128)(2,1)S(1)}, u32[]{:S(2)}, u32[]{:S(2)}) collective-permute-start(bf16[256,384]{1,0:T(8,128)(2,1)S(1)} %get-tuple-element.108), channel_id=1, source_target_pairs={{0,24},{8,16},{16,8},{24,0},{1,25},{9,17},{17,9},{25,1},{2,26},{10... | collective-permute-start | bytes 589832 | tf_op jit(solution)/shard_map/ppermute | solution.py:573
  15.0 37.8 %collective-permute-start.6 = (bf16[256,384]{1,0:T(8,128)(2,1)S(1)}, bf16[256,384]{1,0:T(8,128)(2,1)S(1)}, u32[]{:S(2)}, u32[]{:S(2)}) collective-permute-start(bf16[256,384]{1,0:T(8,128)(2,1)S(1)} %get-tuple-element.105.refs_4_.refs_12_), channel_id=1, source_target_pairs={{0,4},{4,0},{1,5},{5,1},{2,6},{6,2},{3,7},{7,3},{8,12},{12,8},{9,1... | collective-permute-start | bytes 589832 | tf_op jit(solution)/shard_map/ppermute | solution.py:737
  16.8 22.3 %collective-permute-start = (bf16[128,384]{1,0:T(8,128)(2,1)S(1)}, bf16[128,384]{1,0:T(8,128)(2,1)S(1)}, u32[]{:S(2)}, u32[]{:S(2)}) collective-permute-start(bf16[128,384]{1,0:T(8,128)(2,1)S(1)} %get-tuple-element.102), channel_id=1, source_target_pairs={{0,8},{8,0},{16,24},{24,16},{1,9},{9,1},{17,25},{25,17},{2,10},{10... | collective-permute-start | bytes 294920 | tf_op jit(solution)/shard_map/ppermute | solution.py:573
  87.6 23.7 %collective-permute-start.13 = (bf16[2,80,768]{2,1,0:T(8,128)(2,1)}, bf16[2,80,768]{2,1,0:T(8,128)(2,1)S(1)}, u32[]{:S(2)}, u32[]{:S(2)}) collective-permute-start(bf16[2,80,768]{2,1,0:T(8,128)(2,1)} %get-tuple-element.120), channel_id=1, source_target_pairs={{0,1},{1,0},{2,3},{3,2},{4,5},{5,4},{6,7},{7,6},{8,9},{9,8},{10,11... | collective-permute-start | bytes 737288 | tf_op jit(solution)/shard_map/ppermute | solution.py:573
  87.6 25.2 %collective-permute-start.14 = (bf16[2,80,768]{2,1,0:T(8,128)(2,1)}, bf16[2,80,768]{2,1,0:T(8,128)(2,1)S(1)}, u32[]{:S(2)}, u32[]{:S(2)}) collective-permute-start(bf16[2,80,768]{2,1,0:T(8,128)(2,1)} %get-tuple-element.121), channel_id=1, source_target_pairs={{0,2},{1,3},{2,0},{3,1},{4,6},{5,7},{6,4},{7,5},{8,10},{9,11},{10,... | collective-permute-start | bytes 737288 | tf_op jit(solution)/shard_map/ppermute | solution.py:573
  110.5 76.5 %collective-permute-start.71 = (bf16[384,2048]{1,0:T(8,128)(2,1)}, bf16[384,2048]{1,0:T(8,128)(2,1)}, u32[]{:S(2)}, u32[]{:S(2)}) collective-permute-start(bf16[384,2048]{1,0:T(8,128)(2,1)} %get-tuple-element.187), channel_id=1, source_target_pairs={{0,1},{1,0},{2,3},{3,2},{4,5},{5,4},{6,7},{7,6},{8,9},{9,8},{10,11... | collective-permute-start | bytes 4718600 | tf_op jit(solution)/shard_map/ppermute | solution.py:737
  112.8 16.4 %collective-permute-start.18 = (bf16[2,80,768]{2,1,0:T(8,128)(2,1)S(1)}, bf16[2,80,768]{2,1,0:T(8,128)(2,1)S(1)}, u32[]{:S(2)}, u32[]{:S(2)}) collective-permute-start(bf16[2,80,768]{2,1,0:T(8,128)(2,1)S(1)} %copy-done.77), channel_id=1, source_target_pairs={{0,3},{1,2},{2,1},{3,0},{4,7},{5,6},{6,5},{7,4},{8,11},{9,10},{10,... | collective-permute-start | bytes 737288 | tf_op jit(solution)/shard_map/ppermute | solution.py:573
  151.4 40.5 %collective-permute-start.26 = (bf16[1024,768]{1,0:T(8,128)(2,1)}, bf16[1024,768]{1,0:T(8,128)(2,1)}, u32[]{:S(2)}, u32[]{:S(2)}) collective-permute-start(bf16[1024,768]{1,0:T(8,128)(2,1)} %get-tuple-element.139), channel_id=1, source_target_pairs={{0,8},{8,0},{16,24},{24,16},{1,9},{9,1},{17,25},{25,17},{2,10},{10... | collective-permute-start | bytes 4718600 | tf_op jit(solution)/shard_map/ppermute | solution.py:737
  152.4 43.1 %collective-permute-start.25 = (bf16[384,2048]{1,0:T(8,128)(2,1)}, bf16[384,2048]{1,0:T(8,128)(2,1)}, u32[]{:S(2)}, u32[]{:S(2)}) collective-permute-start(bf16[384,2048]{1,0:T(8,128)(2,1)} %get-tuple-element.137), channel_id=1, source_target_pairs={{0,4},{4,0},{1,5},{5,1},{2,6},{6,2},{3,7},{7,3},{8,12},{12,8},{9,1... | collective-permute-start | bytes 4718600 | tf_op jit(solution)/shard_map/ppermute | solution.py:737
  186.4 13.8 %collective-permute-start.22 = (bf16[80,1536]{1,0:T(8,128)(2,1)S(1)}, bf16[80,1536]{1,0:T(8,128)(2,1)S(1)}, u32[]{:S(2)}, u32[]{:S(2)}) collective-permute-start(bf16[80,1536]{1,0:T(8,128)(2,1)S(1)} %get-tuple-element.133), channel_id=1, source_target_pairs={{0,1},{1,0},{2,3},{3,2},{4,5},{5,4},{6,7},{7,6},{8,9},{9,8},{10,11... | collective-permute-start | bytes 737288 | tf_op jit(solution)/shard_map/ppermute | solution.py:573
  195.6 14.9 %collective-permute-start.21 = (bf16[80,1536]{1,0:T(8,128)(2,1)S(1)}, bf16[80,1536]{1,0:T(8,128)(2,1)S(1)}, u32[]{:S(2)}, u32[]{:S(2)}) collective-permute-start(bf16[80,1536]{1,0:T(8,128)(2,1)S(1)} %copy-done.79), channel_id=1, source_target_pairs={{0,3},{1,2},{2,1},{3,0},{4,7},{5,6},{6,5},{7,4},{8,11},{9,10},{10,... | collective-permute-start | bytes 737288 | tf_op jit(solution)/shard_map/ppermute | solution.py:573
  200.2 93.4 %collective-permute-start.39 = (bf16[2,768,1024]{2,1,0:T(8,128)(2,1)}, bf16[2,768,1024]{2,1,0:T(8,128)(2,1)}, u32[]{:S(2)}, u32[]{:S(2)}) collective-permute-start(bf16[2,768,1024]{2,1,0:T(8,128)(2,1)} %get-tuple-element.163), channel_id=1, source_target_pairs={{0,1},{1,0},{2,3},{3,2},{4,5},{5,4},{6,7},{7,6},{8,9},{9,8},{10,11... | collective-permute-start | bytes 9437192 | tf_op jit(solution)/shard_map/ppermute | solution.py:737
  200.6 31.3 %collective-permute-start.72 = (bf16[192,2048]{1,0:T(8,128)(2,1)}, bf16[192,2048]{1,0:T(8,128)(2,1)}, u32[]{:S(2)}, u32[]{:S(2)}) collective-permute-start(bf16[192,2048]{1,0:T(8,128)(2,1)} %get-tuple-element.188), channel_id=1, source_target_pairs={{0,2},{2,0},{1,3},{3,1},{4,6},{6,4},{5,7},{7,5},{8,10},{10,8},{9,1... | collective-permute-start | bytes 2359304 | tf_op jit(solution)/shard_map/ppermute | solution.py:737
  201.0 27.9 %collective-permute-start.27 = (bf16[192,2048]{1,0:T(8,128)(2,1)}, bf16[192,2048]{1,0:T(8,128)(2,1)}, u32[]{:S(2)}, u32[]{:S(2)}) collective-permute-start(bf16[192,2048]{1,0:T(8,128)(2,1)} %get-tuple-element.261), channel_id=1, source_target_pairs={{0,8},{8,0},{16,24},{24,16},{1,9},{9,1},{17,25},{25,17},{2,10},{10... | collective-permute-start | bytes 2359304 | tf_op jit(solution)/shard_map/ppermute | solution.py:737
  226.6 20.7 %collective-permute-start.36 = (bf16[512,768]{1,0:T(8,128)(2,1)}, bf16[512,768]{1,0:T(8,128)(2,1)}, u32[]{:S(2)}, u32[]{:S(2)}) collective-permute-start(bf16[512,768]{1,0:T(8,128)(2,1)} %get-tuple-element.259), channel_id=1, source_target_pairs={{0,4},{4,0},{1,5},{5,1},{2,6},{6,2},{3,7},{7,3},{8,12},{12,8},{9,1... | collective-permute-start | bytes 2359304 | tf_op jit(solution)/shard_map/ppermute | solution.py:737
  228.9 69.1 %collective-permute-start.35 = (bf16[384,2048]{1,0:T(8,128)(2,1)}, bf16[384,2048]{1,0:T(8,128)(2,1)S(1)}, u32[]{:S(2)}, u32[]{:S(2)}) collective-permute-start(bf16[384,2048]{1,0:T(8,128)(2,1)} %get-tuple-element.157), channel_id=1, source_target_pairs={{0,4},{4,0},{1,5},{5,1},{2,6},{6,2},{3,7},{7,3},{8,12},{12,8},{9,1... | collective-permute-start | bytes 4718600 | tf_op jit(solution)/shard_map/ppermute | solution.py:737
  231.9 29.6 %collective-permute-start.57 = (bf16[96,2048]{1,0:T(8,128)(2,1)S(1)}, bf16[96,2048]{1,0:T(8,128)(2,1)S(1)}, u32[]{:S(2)}, u32[]{:S(2)}) collective-permute-start(bf16[96,2048]{1,0:T(8,128)(2,1)S(1)} %add_convert_fusion.32), channel_id=1, source_target_pairs={{0,16},{8,24},{16,0},{24,8},{1,17},{9,25},{17,1},{25,9},{2,18},{10... | collective-permute-start | bytes 1179656 | tf_op jit(solution)/shard_map/ppermute | solution.py:737
  244.1 15.0 %collective-permute-start.29 = (bf16[128,384]{1,0:T(8,128)(2,1)S(1)}, bf16[128,384]{1,0:T(8,128)(2,1)S(1)}, u32[]{:S(2)}, u32[]{:S(2)}) collective-permute-start(bf16[128,384]{1,0:T(8,128)(2,1)S(1)} %copy-done.87), channel_id=1, source_target_pairs={{0,16},{8,24},{16,0},{24,8},{1,17},{9,25},{17,1},{25,9},{2,18},{10... | collective-permute-start | bytes 294920 | tf_op jit(solution)/shard_map/ppermute | solution.py:573
  259.1 30.2 %collective-permute-start.73 = (bf16[192,1024]{1,0:T(8,128)(2,1)}, bf16[192,1024]{1,0:T(8,128)(2,1)S(1)}, u32[]{:S(2)}, u32[]{:S(2)}) collective-permute-start(bf16[192,1024]{1,0:T(8,128)(2,1)} %get-tuple-element.266), channel_id=1, source_target_pairs={{0,4},{4,0},{1,5},{5,1},{2,6},{6,2},{3,7},{7,3},{8,12},{12,8},{9,1... | collective-permute-start | bytes 1179656 | tf_op jit(solution)/shard_map/ppermute | solution.py:737
  259.4 30.7 %collective-permute-start.64 = (bf16[256,768]{1,0:T(8,128)(2,1)S(1)}, bf16[256,768]{1,0:T(8,128)(2,1)S(1)}, u32[]{:S(2)}, u32[]{:S(2)}) collective-permute-start(bf16[256,768]{1,0:T(8,128)(2,1)S(1)} %add_convert_fusion.26), channel_id=1, source_target_pairs={{0,16},{8,24},{16,0},{24,8},{1,17},{9,25},{17,1},{25,9},{2,18},{10... | collective-permute-start | bytes 1179656 | tf_op jit(solution)/shard_map/ppermute | solution.py:737
  261.5 22.0 %collective-permute-start.53 = (bf16[1,768,256]{1,2,0:T(8,128)(2,1)}, bf16[1,768,256]{1,2,0:T(8,128)(2,1)S(1)}, u32[]{:S(2)}, u32[]{:S(2)}) collective-permute-start(bf16[1,768,256]{1,2,0:T(8,128)(2,1)} %get-tuple-element.270), channel_id=1, source_target_pairs={{0,2},{2,0},{1,3},{3,1},{4,6},{6,4},{5,7},{7,5},{8,10},{10,8},{9,1... | collective-permute-start | bytes 1179656 | tf_op jit(solution)/shard_map/ppermute | solution.py:737
  283.5 26.7 %collective-permute-start.34 = (bf16[256,384]{1,0:T(8,128)(2,1)}, bf16[256,384]{1,0:T(8,128)(2,1)S(1)}, u32[]{:S(2)}, u32[]{:S(2)}) collective-permute-start(bf16[256,384]{1,0:T(8,128)(2,1)} %get-tuple-element.154), channel_id=1, source_target_pairs={{0,4},{4,0},{1,5},{5,1},{2,6},{6,2},{3,7},{7,3},{8,12},{12,8},{9,1... | collective-permute-start | bytes 589832 | tf_op jit(solution)/shard_map/ppermute | solution.py:737
  289.2 19.0 %collective-permute-start.54 = (bf16[1,384,256]{1,2,0:T(8,128)(2,1)S(1)}, bf16[1,384,256]{1,2,0:T(8,128)(2,1)S(1)}, u32[]{:S(2)}, u32[]{:S(2)}) collective-permute-start(bf16[1,384,256]{1,2,0:T(8,128)(2,1)S(1)} %get-tuple-element.278), channel_id=1, source_target_pairs={{0,4},{4,0},{1,5},{5,1},{2,6},{6,2},{3,7},{7,3},{8,12},{12,8},{9,1... | collective-permute-start | bytes 589832 | tf_op jit(solution)/shard_map/ppermute | solution.py:737
  302.5 20.5 %collective-permute-start.37 = (bf16[192,2048]{1,0:T(8,128)(2,1)S(1)}, bf16[192,2048]{1,0:T(8,128)(2,1)S(1)}, u32[]{:S(2)}, u32[]{:S(2)}) collective-permute-start(bf16[192,2048]{1,0:T(8,128)(2,1)S(1)} %get-tuple-element.257), channel_id=1, source_target_pairs={{0,8},{8,0},{16,24},{24,16},{1,9},{9,1},{17,25},{25,17},{2,10},{10... | collective-permute-start | bytes 2359304 | tf_op jit(solution)/shard_map/ppermute | solution.py:737
  306.7 51.5 %collective-permute-start.40 = (bf16[1,768,1024]{2,1,0:T(8,128)(2,1)S(1)}, bf16[1,768,1024]{2,1,0:T(8,128)(2,1)S(1)}, u32[]{:S(2)}, u32[]{:S(2)}) collective-permute-start(bf16[1,768,1024]{2,1,0:T(8,128)(2,1)S(1)} %get-tuple-element.164), channel_id=1, source_target_pairs={{0,2},{2,0},{1,3},{3,1},{4,6},{6,4},{5,7},{7,5},{8,10},{10,8},{9,1... | collective-permute-start | bytes 4718600 | tf_op jit(solution)/shard_map/ppermute | solution.py:737
  308.2 20.3 %collective-permute-start.74 = (bf16[192,512]{1,0:T(8,128)(2,1)S(1)}, bf16[192,512]{1,0:T(8,128)(2,1)S(1)}, u32[]{:S(2)}, u32[]{:S(2)}) collective-permute-start(bf16[192,512]{1,0:T(8,128)(2,1)S(1)} %get-tuple-element.276), channel_id=1, source_target_pairs={{0,8},{8,0},{16,24},{24,16},{1,9},{9,1},{17,25},{25,17},{2,10},{10... | collective-permute-start | bytes 589832 | tf_op jit(solution)/shard_map/ppermute | solution.py:737
  310.2 51.4 %collective-permute-start.31 = (bf16[128,384]{1,0:T(8,128)(2,1)S(1)}, bf16[128,384]{1,0:T(8,128)(2,1)S(1)}, u32[]{:S(2)}, u32[]{:S(2)}) collective-permute-start(bf16[128,384]{1,0:T(8,128)(2,1)S(1)} %copy-done.129), channel_id=1, source_target_pairs={{0,8},{8,0},{16,24},{24,16},{1,9},{9,1},{17,25},{25,17},{2,10},{10... | collective-permute-start | bytes 294920 | tf_op jit(solution)/shard_map/ppermute | solution.py:573
  310.7 51.0 %collective-permute-start.38 = (bf16[384,2048]{1,0:T(8,128)(2,1)S(1)}, bf16[384,2048]{1,0:T(8,128)(2,1)S(1)}, u32[]{:S(2)}, u32[]{:S(2)}) collective-permute-start(bf16[384,2048]{1,0:T(8,128)(2,1)S(1)} %copy-done.75), channel_id=1, source_target_pairs={{0,4},{4,0},{1,5},{5,1},{2,6},{6,2},{3,7},{7,3},{8,12},{12,8},{9,1... | collective-permute-start | bytes 4718600 | tf_op jit(solution)/shard_map/ppermute | solution.py:737
  328.5 26.4 %collective-permute-start.58 = (bf16[96,2048]{1,0:T(8,128)(2,1)S(1)}, bf16[96,2048]{1,0:T(8,128)(2,1)S(1)}, u32[]{:S(2)}, u32[]{:S(2)}) collective-permute-start(bf16[96,2048]{1,0:T(8,128)(2,1)S(1)} %add_convert_fusion.31), channel_id=1, source_target_pairs={{0,16},{8,24},{16,0},{24,8},{1,17},{9,25},{17,1},{25,9},{2,18},{10... | collective-permute-start | bytes 1179656 | tf_op jit(solution)/shard_map/ppermute | solution.py:737
  333.4 32.9 %collective-permute-start.32 = (bf16[128,384]{1,0:T(8,128)(2,1)S(1)}, bf16[128,384]{1,0:T(8,128)(2,1)S(1)}, u32[]{:S(2)}, u32[]{:S(2)}) collective-permute-start(bf16[128,384]{1,0:T(8,128)(2,1)S(1)} %copy-done.128), channel_id=1, source_target_pairs={{0,16},{8,24},{16,0},{24,8},{1,17},{9,25},{17,1},{25,9},{2,18},{10... | collective-permute-start | bytes 294920 | tf_op jit(solution)/shard_map/ppermute | solution.py:573
  366.3 17.7 %collective-permute-start.75 = (bf16[192,256]{1,0:T(8,128)(2,1)}, bf16[192,256]{1,0:T(8,128)(2,1)}, u32[]{:S(2)}, u32[]{:S(2)}) collective-permute-start(bf16[192,256]{1,0:T(8,128)(2,1)} %add_convert_fusion.52), channel_id=1, source_target_pairs={{0,16},{8,24},{16,0},{24,8},{1,17},{9,25},{17,1},{25,9},{2,18},{10... | collective-permute-start | bytes 294920 | tf_op jit(solution)/shard_map/ppermute | solution.py:737
  366.4 21.2 %collective-permute-start.56 = (bf16[1,96,256]{1,2,0:T(8,128)(2,1)S(1)}, bf16[1,96,256]{1,2,0:T(8,128)(2,1)}, u32[]{:S(2)}, u32[]{:S(2)}) collective-permute-start(bf16[1,96,256]{1,2,0:T(8,128)(2,1)S(1)} %add_convert_fusion.54), channel_id=1, source_target_pairs={{0,16},{8,24},{16,0},{24,8},{1,17},{9,25},{17,1},{25,9},{2,18},{10... | collective-permute-start | bytes 147464 | tf_op jit(solution)/shard_map/ppermute | solution.py:737
  376.0 42.8 %collective-permute-start.61 = (bf16[384,2048]{1,0:T(8,128)(2,1)}, bf16[384,2048]{1,0:T(8,128)(2,1)}, u32[]{:S(2)}, u32[]{:S(2)}) collective-permute-start(bf16[384,2048]{1,0:T(8,128)(2,1)} %get-tuple-element.182), channel_id=1, source_target_pairs={{0,4},{4,0},{1,5},{5,1},{2,6},{6,2},{3,7},{7,3},{8,12},{12,8},{9,1... | collective-permute-start | bytes 4718600 | tf_op jit(solution)/shard_map/ppermute | solution.py:737
  384.0 52.4 %collective-permute-start.47 = (bf16[2,768,640]{1,2,0:T(8,128)(2,1)}, bf16[2,768,640]{1,2,0:T(8,128)(2,1)}, u32[]{:S(2)}, u32[]{:S(2)}) collective-permute-start(bf16[2,768,640]{1,2,0:T(8,128)(2,1)} %maximum_bitcast_fusion), channel_id=1, source_target_pairs={{0,1},{1,0},{2,3},{3,2},{4,5},{5,4},{6,7},{7,6},{8,9},{9,8},{10,11... | collective-permute-start | bytes 5898248 | tf_op jit(solution)/shard_map/ppermute | solution.py:737
  385.7 32.1 %collective-permute-start.68 = (bf16[1,384,1024]{2,1,0:T(8,128)(2,1)}, bf16[1,384,1024]{2,1,0:T(8,128)(2,1)S(1)}, u32[]{:S(2)}, u32[]{:S(2)}) collective-permute-start(bf16[1,384,1024]{2,1,0:T(8,128)(2,1)} %get-tuple-element.249), channel_id=1, source_target_pairs={{0,4},{4,0},{1,5},{5,1},{2,6},{6,2},{3,7},{7,3},{8,12},{12,8},{9,1... | collective-permute-start | bytes 2359304 | tf_op jit(solution)/shard_map/ppermute | solution.py:737
  392.9 46.5 %collective-permute-start.59 = (bf16[192,2048]{1,0:T(8,128)(2,1)}, bf16[192,2048]{1,0:T(8,128)(2,1)}, u32[]{:S(2)}, u32[]{:S(2)}) collective-permute-start(bf16[192,2048]{1,0:T(8,128)(2,1)} %get-tuple-element.253), channel_id=1, source_target_pairs={{0,8},{8,0},{16,24},{24,16},{1,9},{9,1},{17,25},{25,17},{2,10},{10... | collective-permute-start | bytes 2359304 | tf_op jit(solution)/shard_map/ppermute | solution.py:737
  418.8 16.8 %collective-permute-start.69 = (bf16[1,192,1024]{2,1,0:T(8,128)(2,1)}, bf16[1,192,1024]{2,1,0:T(8,128)(2,1)S(1)}, u32[]{:S(2)}, u32[]{:S(2)}) collective-permute-start(bf16[1,192,1024]{2,1,0:T(8,128)(2,1)} %get-tuple-element.268), channel_id=1, source_target_pairs={{0,8},{8,0},{16,24},{24,16},{1,9},{9,1},{17,25},{25,17},{2,10},{10... | collective-permute-start | bytes 1179656 | tf_op jit(solution)/shard_map/ppermute | solution.py:737
  422.0 33.4 %collective-permute-start.62 = (bf16[192,2048]{1,0:T(8,128)(2,1)}, bf16[192,2048]{1,0:T(8,128)(2,1)}, u32[]{:S(2)}, u32[]{:S(2)}) collective-permute-start(bf16[192,2048]{1,0:T(8,128)(2,1)} %get-tuple-element.256), channel_id=1, source_target_pairs={{0,8},{8,0},{16,24},{24,16},{1,9},{9,1},{17,25},{25,17},{2,10},{10... | collective-permute-start | bytes 2359304 | tf_op jit(solution)/shard_map/ppermute | solution.py:737
  435.7 19.0 %collective-permute-start.70 = (bf16[1,96,1024]{2,1,0:T(8,128)(2,1)S(1)}, bf16[1,96,1024]{2,1,0:T(8,128)(2,1)S(1)}, u32[]{:S(2)}, u32[]{:S(2)}) collective-permute-start(bf16[1,96,1024]{2,1,0:T(8,128)(2,1)S(1)} %add_convert_fusion.40), channel_id=1, source_target_pairs={{0,16},{8,24},{16,0},{24,8},{1,17},{9,25},{17,1},{25,9},{2,18},{10... | collective-permute-start | bytes 589832 | tf_op jit(solution)/shard_map/ppermute | solution.py:737
  435.7 35.4 %collective-permute-start.65 = (bf16[1024,768]{1,0:T(8,128)(2,1)}, bf16[1024,768]{1,0:T(8,128)(2,1)S(1)}, u32[]{:S(2)}, u32[]{:S(2)}) collective-permute-start(bf16[1024,768]{1,0:T(8,128)(2,1)} %get-tuple-element.185), channel_id=1, source_target_pairs={{0,4},{4,0},{1,5},{5,1},{2,6},{6,2},{3,7},{7,3},{8,12},{12,8},{9,1... | collective-permute-start | bytes 4718600 | tf_op jit(solution)/shard_map/ppermute | solution.py:737
  438.5 28.3 %collective-permute-start.48 = (bf16[1,768,640]{1,2,0:T(8,128)(2,1)S(1)}, bf16[1,768,640]{1,2,0:T(8,128)(2,1)S(1)}, u32[]{:S(2)}, u32[]{:S(2)}) collective-permute-start(bf16[1,768,640]{1,2,0:T(8,128)(2,1)S(1)} %get-tuple-element.246), channel_id=1, source_target_pairs={{0,2},{2,0},{1,3},{3,1},{4,6},{6,4},{5,7},{7,5},{8,10},{10,8},{9,1... | collective-permute-start | bytes 2949128 | tf_op jit(solution)/shard_map/ppermute | solution.py:737
  440.6 25.1 %collective-permute-start.60 = (bf16[96,2048]{1,0:T(8,128)(2,1)S(1)}, bf16[96,2048]{1,0:T(8,128)(2,1)S(1)}, u32[]{:S(2)}, u32[]{:S(2)}) collective-permute-start(bf16[96,2048]{1,0:T(8,128)(2,1)S(1)} %add_convert_fusion.29), channel_id=1, source_target_pairs={{0,16},{8,24},{16,0},{24,8},{1,17},{9,25},{17,1},{25,9},{2,18},{10... | collective-permute-start | bytes 1179656 | tf_op jit(solution)/shard_map/ppermute | solution.py:737
  471.6 28.5 %collective-permute-start.66 = (bf16[512,768]{1,0:T(8,128)(2,1)S(1)}, bf16[512,768]{1,0:T(8,128)(2,1)S(1)}, u32[]{:S(2)}, u32[]{:S(2)}) collective-permute-start(bf16[512,768]{1,0:T(8,128)(2,1)S(1)} %get-tuple-element.252), channel_id=1, source_target_pairs={{0,8},{8,0},{16,24},{24,16},{1,9},{9,1},{17,25},{25,17},{2,10},{10... | collective-permute-start | bytes 2359304 | tf_op jit(solution)/shard_map/ppermute | solution.py:737
  476.6 18.9 %collective-permute-start.50 = (bf16[1,192,640]{1,2,0:T(8,128)(2,1)S(1)}, bf16[1,192,640]{1,2,0:T(8,128)(2,1)S(1)}, u32[]{:S(2)}, u32[]{:S(2)}) collective-permute-start(bf16[1,192,640]{1,2,0:T(8,128)(2,1)S(1)} %get-tuple-element.274), channel_id=1, source_target_pairs={{0,8},{8,0},{16,24},{24,16},{1,9},{9,1},{17,25},{25,17},{2,10},{10... | collective-permute-start | bytes 737288 | tf_op jit(solution)/shard_map/ppermute | solution.py:737
  495.6 17.4 %collective-permute-start.51 = (bf16[1,96,640]{1,2,0:T(8,128)(2,1)S(1)}, bf16[1,96,640]{1,2,0:T(8,128)(2,1)S(1)}, u32[]{:S(2)}, u32[]{:S(2)}) collective-permute-start(bf16[1,96,640]{1,2,0:T(8,128)(2,1)S(1)} %add_convert_fusion.48), channel_id=1, source_target_pairs={{0,16},{8,24},{16,0},{24,8},{1,17},{9,25},{17,1},{25,9},{2,18},{10... | collective-permute-start | bytes 368648 | tf_op jit(solution)/shard_map/ppermute | solution.py:737
  500.9 17.0 %collective-permute-start.67 = (bf16[256,768]{1,0:T(8,128)(2,1)}, bf16[256,768]{1,0:T(8,128)(2,1)S(1)}, u32[]{:S(2)}, u32[]{:S(2)}) collective-permute-start(bf16[256,768]{1,0:T(8,128)(2,1)} %add_convert_fusion.24), channel_id=1, source_target_pairs={{0,16},{8,24},{16,0},{24,8},{1,17},{9,25},{17,1},{25,9},{2,18},{10... | collective-permute-start | bytes 1179656 | tf_op jit(solution)/shard_map/ppermute | solution.py:737
  (160 other events, 1880.5 us)
